TPU v7x, 32 devices: a whole 2x2x4 slice. The times are simulated.
32 devices in a mesh: tm: 4 (over x, core), tile: 8 (over z, y).
Axes of the slice: x: 2, y: 2, z: 4, core: 2. Of those that a mesh axis runs over, the one named last changes fastest.
Arguments:
- recording: bfloat16 [65536, 512], P('tile', 'tm'), may hold values from -300 to 300
- footprints: bfloat16 [65536, 256], P('tile'), may hold values from -0.375 to 0.375
- pattern: int32 [256, 4], P('tile'), may hold values from 0 to 35, as said below
- decay: float32 [16384], P('tile'), may hold values from 0.96 to 1
- frame_gain: float32 [512], P('tm'), may hold values from 0.6 to 1
- spikes: float32 [16384, 512], P('tile', 'tm'), may hold values from 0 to 0.15
Outputs:
- spikes_out: float32 [16384, 512], P('tile', 'tm')
- traces_last: float32 [16384, 512], P('tile', 'tm')
Inputs may be any that keep to these rules, and one draw needn't show every extreme that they name: `pattern`: with p = q % 32, row q holds 4 different values between p and p + 4, always including p, p + 2 and p + 4, in some order; value v names the stripe's own neuron block v - 2, so values under 2 or over 2048 // 64 + 1 name edge blocks of the adjacent stripes.
All inputs are finite; a program needn't handle non-finite values.
Results may differ from a plain program's by a relative error of at most 0.00073.
Values may be sent and summed in bfloat16 or wider, within the bound.
No kernel may reach another device: no remote copies, remote signals or barrier semaphores. Data moves between devices by JAX's collectives and lax.ppermute only.
A program may use at most 128 MiB of HBM per device.

v0:
```python
import jax
import jax.numpy as jnp
from jax import lax
from jax.experimental import pallas as pl
from jax.experimental.pallas import tpu as pltpu
from jax.sharding import PartitionSpec as P

NEU_BLOCK = 64
PIX_BLOCK = 256
PARTS = 4
K = 4
HB = 2
ITERS = 2
LANES = 128
RIM = HB * NEU_BLOCK // LANES
F32 = jnp.float32
BF16 = jnp.bfloat16
VMEM = pl.BlockSpec(memory_space=pltpu.VMEM)
HBM = pl.BlockSpec(memory_space=pltpu.HBM)
SMEM = pl.BlockSpec(memory_space=pltpu.SMEM)


def padded8(rows):
    return -(-rows // 8) * 8


def table(frames, reverse):
    row = lax.broadcasted_iota(jnp.int32, (frames, 2 * frames), 0)
    col = lax.broadcasted_iota(jnp.int32, (frames, 2 * frames), 1)
    col = jnp.where(col >= frames, col - frames, col)
    keep = col >= row if reverse else col <= row
    return jnp.where(keep, 1.0, 0.0).astype(BF16)


def summed(sums_table, values):
    high = values.astype(BF16)
    low = (values - high.astype(F32)).astype(BF16)
    both = jnp.concatenate([high, low], axis=0)
    return jnp.dot(sums_table, both, preferred_element_type=F32)


def powers(log_decay, frames, mid, sign):
    groups = frames // 8
    coarse = (8 * lax.broadcasted_iota(jnp.int32, (groups, LANES), 0) - mid).astype(F32) * sign
    fine = lax.broadcasted_iota(jnp.int32, (8, LANES), 0).astype(F32) * sign
    coarse = jnp.exp(coarse * log_decay)
    fine = jnp.exp(fine * log_decay)
    return (coarse[:, None, :] * fine[None, :, :]).reshape(frames, LANES)


def chunk(field, c):
    own, rim = field
    inner = own.shape[0]
    if c < RIM:
        return rim.at[c]
    if c >= RIM + inner:
        return rim.at[c - inner]
    return own.at[c - RIM]


def chunk_count(field):
    return field[0].shape[0] + field[1].shape[0]


def prep_chunk(c, rate, field, gains, s3, p3, pinv3, z3, rows, pay):
    frames = field.shape[1]
    middle, prefix_col, inverse_col, sums_table = gains
    mid = frames // 2 - 1
    rate = jnp.where(rate > 0.0, rate, 1.0)
    log_rate = jnp.log(rate)
    gain = jnp.sqrt(1.0 - rate * rate)
    p = powers(log_rate, frames, mid, 1.0) * prefix_col
    pinv = powers(log_rate, frames, mid, -1.0) * inverse_col
    field = field.T
    z = summed(sums_table, field * gain * pinv)
    last = p[frames - 1 : frames, :]
    s3[...] = field
    p3[...] = p
    pinv3[...] = pinv
    z3[...] = z
    half = rate
    for _ in range(frames.bit_length() - 2):
        half = half * half
    rows[0, c : c + 1, :] = gain
    rows[1, c : c + 1, :] = half * middle
    rows[2, c : c + 1, :] = half * half
    pay[0, c : c + 1, :] = last * z[frames - 1 : frames, :]
    scale = last * gain
    pay[1, c : c + 1, :] = scale * scale * jnp.sum(pinv * pinv, axis=0, keepdims=True)


def gain_columns(gains):
    frames = gains.shape[1]
    mid = frames // 2 - 1
    lane = lax.broadcasted_iota(jnp.int32, (8, frames), 1)
    prefix = jnp.broadcast_to(gains, (8, frames))
    step = 1
    while step < frames:
        prefix = prefix * jnp.where(lane >= step, pltpu.roll(prefix, step, 1), 1.0)
        step *= 2
    middle = jnp.broadcast_to(prefix[0:1, mid : mid + 1], (1, LANES))
    whole = jnp.broadcast_to(prefix[0:1, frames - 1 : frames], (1, LANES))
    prefix_col = jnp.broadcast_to(prefix[0:1] / middle, (LANES, frames)).T
    inverse_col = jnp.broadcast_to(middle / prefix[0:1], (LANES, frames)).T
    return middle, whole, prefix_col, inverse_col


def rims_kernel(spikes, decay, first, second, rates_here, spikes_here, sems):
    edge = RIM * LANES
    neurons = spikes.shape[0]
    own = decay.shape[0]
    even = lax.axis_index("tile") % 2 == 0
    top = jnp.where(even, neurons - edge, 0)
    bottom = jnp.where(even, 0, neurons - edge)
    copies = [
        pltpu.make_async_copy(decay, rates_here, sems.at[0]),
        pltpu.make_async_copy(
            spikes.at[pl.ds(pl.multiple_of(top, LANES), edge)], first.at[pl.ds(0, edge)], sems.at[1]
        ),
        pltpu.make_async_copy(
            spikes.at[pl.ds(pl.multiple_of(bottom, LANES), edge)],
            second.at[pl.ds(0, edge)],
            sems.at[2],
        ),
        pltpu.make_async_copy(spikes, spikes_here, sems.at[3]),
    ]
    for copy in copies:
        copy.start()
    first[edge:, :] = jnp.zeros_like(first[edge:, :])
    second[edge:, :] = jnp.zeros_like(second[edge:, :])
    copies[0].wait()
    lower, upper = rates_here[0:RIM, :], rates_here[own - RIM : own, :]
    first[edge : edge + RIM, :] = jnp.where(even, upper, lower)
    second[edge : edge + RIM, :] = jnp.where(even, lower, upper)
    for copy in copies[1:]:
        copy.wait()


def prep_own_kernel(
    spikes, decay, gains, feet, s3, p3, pinv3, z3, rows, pay, columns, feet_ends, sems
):
    own = s3.shape[0]
    chunks = own + 2 * RIM
    size = feet_ends.shape[0] // 2
    fetches = [
        pltpu.make_async_copy(
            feet.at[pl.ds(start, size)], feet_ends.at[pl.ds(i * size, size)], sems.at[i]
        )
        for i, start in enumerate((0, feet.shape[0] - size))
    ]
    for fetch in fetches:
        fetch.start()
    middle, whole, prefix_col, inverse_col = gain_columns(gains[...])
    columns[0] = prefix_col
    columns[1] = inverse_col
    rows[...] = jnp.ones_like(rows)
    rows[0, chunks : chunks + 1, :] = middle
    pay[...] = jnp.zeros_like(pay)
    pay[0, chunks : chunks + 1, :] = whole
    shared = middle, prefix_col, inverse_col, table(spikes.shape[1], False)
    for i in range(own):
        field = spikes[i * LANES : (i + 1) * LANES, :]
        at = [ref.at[i] for ref in (s3, p3, pinv3, z3)]
        prep_chunk(i + RIM, decay[i : i + 1, :], field, shared, *at, rows, pay)
    for fetch in fetches:
        fetch.wait()


def sides(even, first, second):
    return jnp.where(even, second, first), jnp.where(even, first, second)


def prep_rim_kernel(first, second, columns, rows_own, pay_own, s3, p3, pinv3, z3, rows, pay):
    rims, frames = s3.shape[0], s3.shape[1]
    own = rows_own.shape[1] - padded8(1)
    chunks = own + 2 * RIM
    middle = rows_own[0, chunks : chunks + 1, :]
    shared = middle, columns[0], columns[1], table(frames, False)
    rows[...] = rows_own[...]
    pay[...] = pay_own[...]
    even = lax.axis_index("tile") % 2 == 0
    below, above = sides(even, first[...], second[...])
    for i in range(rims):
        message = below if i < RIM else above
        j = i % RIM
        c = i if i < RIM else own + i
        at = [ref.at[i] for ref in (s3, p3, pinv3, z3)]
        field = message[j * LANES : (j + 1) * LANES, :]
        rate = message[RIM * LANES + j : RIM * LANES + j + 1, :]
        prep_chunk(c, rate, field, shared, *at, rows, pay)


def block_totals(pays, chunks, rows):
    return [rows[2] * pays[m, 0, chunks : chunks + 1, :] for m in range(pays.shape[0])]


def step_size(stats):
    both = jnp.sum(jnp.sum(stats[...], axis=0), axis=1, keepdims=True)
    return jnp.broadcast_to(both[0:1] / (both[1:2] + 1e-06), (1, LANES))


def update_kernel(s3, g3, stats, p3, pinv3, rows, new3, z3, pay):
    chunks = chunk_count(s3)
    frames = g3.shape[1]
    sums_table = table(frames, False)
    size = step_size(stats)
    pay[...] = jnp.zeros_like(pay)
    for c in range(chunks):
        field = jnp.maximum(chunk(s3, c)[...] - size * g3[c], 0.0)
        z = summed(sums_table, field * rows[0, c : c + 1, :] * chunk(pinv3, c)[...])
        if len(new3) == 2:
            chunk(new3, c)[...] = field
        elif RIM <= c < chunks - RIM:
            new3[0][c - RIM] = field
        chunk(z3, c)[...] = z
        last = chunk(p3, c)[frames - 1 : frames, :]
        pay[c : c + 1, :] = last * z[frames - 1 : frames, :]


def final_kernel(s3, g3, stats, out, here, sems):
    size = step_size(stats)
    own = s3.shape[0]
    rows = out.shape[0] // PARTS
    copies = [
        pltpu.make_async_copy(
            here.at[pl.ds(i * rows, rows)], out.at[pl.ds(i * rows, rows)], sems.at[i]
        )
        for i in range(PARTS)
    ]
    for i in range(own):
        field = jnp.maximum(s3[i] - size * g3[i + RIM], 0.0)
        here[i * LANES : (i + 1) * LANES, :] = field.T
        if (i + 1) % (own // PARTS) == 0:
            copies[i // (own // PARTS)].start()
    for copy in copies:
        copy.wait()


def picked(ext, pattern, q, first=0):
    parts = [
        ext[pl.ds(pl.multiple_of((pattern[k, q] - first) * NEU_BLOCK, NEU_BLOCK), NEU_BLOCK), :]
        for k in range(K)
    ]
    return jnp.concatenate(parts, axis=0)


def block_of(field, q):
    return field[q * PIX_BLOCK : (q + 1) * PIX_BLOCK, :]


def foot_of(feet, q, stripe):
    count = feet.shape[0] // PIX_BLOCK
    return block_of(feet, q if q < count // 2 else q - stripe + count)


def note_places(pattern, place, start, stop):
    for q in range(start, stop):
        for v in range(2 * HB + 1):
            place[q, v] = -1
        for k in range(K):
            place[q, pattern[k, q] - q] = k


def pull_back(pattern, ext, feet, record, contrib, q):
    foot = foot_of(feet, q, pattern.shape[1])
    fitted = jnp.dot(foot, picked(ext, pattern, q), preferred_element_type=F32)
    residual = (fitted - block_of(record, q).astype(F32)).astype(BF16)
    contrib[q * K * NEU_BLOCK : (q + 1) * K * NEU_BLOCK, :] = lax.dot_general(
        foot, residual, (((0,), (0,)), ((), ())), preferred_element_type=F32
    )


def gathered(contrib, place, c, ranges):
    frames = contrib.shape[1]
    per_chunk = LANES // NEU_BLOCK
    halves = []
    for b in range(c * per_chunk, (c + 1) * per_chunk):
        total = jnp.zeros((NEU_BLOCK, frames), F32)
        for v in range(2 * HB + 1):
            q = b - v
            if any(start <= q < stop for start, stop in ranges):
                k = place[q, v]
                at = pl.multiple_of((q * K + jnp.maximum(k, 0)) * NEU_BLOCK, NEU_BLOCK)
                value = contrib[pl.ds(at, NEU_BLOCK), :]
                if v % 2:
                    value = jnp.where(k >= 0, value, 0.0)
                total = total + value
        halves.append(total)
    return jnp.concatenate(halves, axis=0).T


def edge_kernel(
    pattern, z3, p3, rows, pay, pays, feet, record, ext, zones, spill, send_a, send_b, *rest
):
    *traces, contrib, place = rest
    chunks = chunk_count(z3)
    stripe = pattern.shape[1]
    edge = 2 * HB
    me = lax.axis_index("tm")
    totals = block_totals(pay, chunks, rows)
    carry = jnp.zeros_like(totals[0])
    for m in range(pays.shape[0]):
        carry = jnp.where(m < me, pays[m] + totals[m] * carry, carry)
    carry = carry * rows[1]
    ranges = ((0, edge), (stripe - edge, stripe))
    for start, stop in ranges:
        note_places(pattern, place, start, stop)

    def trace(c):
        field = (chunk(p3, c)[...] * (chunk(z3, c)[...] + carry[c : c + 1, :])).T
        ext[c * LANES : (c + 1) * LANES, :] = field.astype(BF16)
        if traces and RIM <= c < chunks - RIM:
            traces[0][(c - RIM) * LANES : (c - RIM + 1) * LANES, :] = field

    near = 4 * RIM
    for c in [*range(near), *range(chunks - near, chunks)]:
        trace(c)
    for start, stop in ranges:
        for q in range(start, stop):
            pull_back(pattern, ext, feet, record, contrib, q)
    for c in range(near, chunks - near):
        trace(c)
    even = lax.axis_index("tile") % 2 == 0
    for i in range(2 * RIM):
        below = gathered(contrib, place, i, ranges)
        above = gathered(contrib, place, chunks - 2 * RIM + i, ranges)
        zones[i] = below
        zones[2 * RIM + i] = above
        send_a[i] = jnp.where(even, above, below).astype(BF16)
        send_b[i] = jnp.where(even, below, above).astype(BF16)
        spill[i] = gathered(contrib, place, 2 * RIM + i, ranges)
        spill[2 * RIM + i] = gathered(contrib, place, chunks - 4 * RIM + i, ranges)

def adjoint_chunk(sums_table, field, p, pinv, rows, c, r3, pay):
    frames = field.shape[0]
    r = summed(sums_table, field * p)
    r3[...] = r
    gain = rows[0, c : c + 1, :]
    pay[0, c : c + 1, :] = rows[1, c : c + 1, :] * r[0:1, :]
    ends = p[frames - 1 : frames, :] * gain * gain
    pay[1, c : c + 1, :] = ends * jnp.sum(pinv * pinv * r, axis=0, keepdims=True)


def inner_kernel(pattern, p3, pinv3, rows, ext, spill, feet, record, traces, r3, pay, *rest):
    if traces:
        out, contrib, place, sem = rest
        copy = pltpu.make_async_copy(traces[0], out, sem)
        copy.start()
    else:
        contrib, place = rest
    chunks = chunk_count(p3)
    frames = spill.shape[1]
    stripe = pattern.shape[1]
    edge = 2 * HB
    note_places(pattern, place, edge, stripe - edge)
    sums_table = table(frames, True)
    pay[...] = jnp.zeros_like(pay)
    inner = chunks - 4 * RIM
    for q in range(edge, stripe - edge):
        pull_back(pattern, ext, feet, record, contrib, q)
    for i in range(inner):
        c = i + 2 * RIM
        field = gathered(contrib, place, c, ((edge, stripe - edge),))
        if i < 2 * RIM:
            field = field + spill[i]
        if i >= inner - 2 * RIM:
            field = field + spill[i - inner + 4 * RIM]
        p, pinv = chunk(p3, c)[...], chunk(pinv3, c)[...]
        adjoint_chunk(sums_table, field, p, pinv, rows, c, r3.at[i], pay)
    if traces:
        copy.wait()


def border_kernel(zones, got_a, got_b, p3, pinv3, rows, pay_inner, r3, pay):
    chunks = chunk_count(p3)
    frames = zones.shape[1]
    sums_table = table(frames, True)
    pay[...] = pay_inner[...]
    even = lax.axis_index("tile") % 2 == 0
    for i in range(2 * RIM):
        both = sides(even, got_a[i].astype(F32), got_b[i].astype(F32))
        for side, c in ((0, i), (1, chunks - 2 * RIM + i)):
            at = side * 2 * RIM + i
            field = zones[at] + both[side]
            p, pinv = chunk(p3, c)[...], chunk(pinv3, c)[...]
            adjoint_chunk(sums_table, field, p, pinv, rows, c, r3.at[at], pay)


def direction_kernel(
    pattern, r_inner, r_border, p3, pinv3, rows, pay, pays, feet, g3, stats, low, high
):
    chunks, frames = g3.shape[0], g3.shape[1]
    own = chunks - 2 * RIM
    stripe = pattern.shape[1]
    me = lax.axis_index("tm")
    totals = block_totals(pay, chunks, rows)
    blocks = pays.shape[0]
    entering = [None] * blocks
    state = jnp.zeros_like(totals[0])
    for m in reversed(range(blocks)):
        entering[m] = state
        state = pays[m, 0] + totals[m] * state
    carry = jnp.zeros_like(totals[0])
    adjoint = jnp.zeros_like(totals[0])
    for m in range(blocks):
        end = pays[m, 1] + pay[m, 1] * entering[m]
        carry = jnp.where(m < me, end + totals[m] * carry, carry)
        adjoint = jnp.where(m == me, entering[m], adjoint)
    carry = carry * rows[1]
    sums_table = table(frames, False)
    grad_sq = jnp.zeros((8, LANES), F32)
    image_sq = jnp.zeros((8, frames), F32)
    per_chunk = LANES // NEU_BLOCK
    low_chunks = low.shape[0] // LANES
    first_high = chunks - high.shape[0] // LANES
    for c in range(chunks):
        p = chunk(p3, c)[...]
        if c < 2 * RIM:
            r = r_border[c]
        elif c >= chunks - 2 * RIM:
            r = r_border[c - chunks + 4 * RIM]
        else:
            r = r_inner[c - 2 * RIM]
        scale = rows[0, c : c + 1, :] * chunk(pinv3, c)[...]
        gradient = scale * (r + p[frames - 1 : frames, :] * adjoint[c : c + 1, :])
        g3[c] = gradient
        if RIM <= c < RIM + own:
            grad_sq += jnp.sum((gradient * gradient).reshape(frames // 8, 8, LANES), axis=0)
        z = summed(sums_table, scale * gradient)
        field = (p * (z + carry[c : c + 1, :])).astype(BF16).T
        if c < low_chunks:
            low[c * LANES : (c + 1) * LANES, :] = field
        if c >= first_high:
            high[(c - first_high) * LANES : (c - first_high + 1) * LANES, :] = field
    for q in range(stripe):
        if q + 2 * HB < low_chunks * per_chunk:
            named = picked(low, pattern, q, 0)
        else:
            named = picked(high, pattern, q, first_high * per_chunk)
        image = jnp.dot(foot_of(feet, q, stripe), named, preferred_element_type=F32)
        image_sq += jnp.sum((image * image).reshape(PIX_BLOCK // 8, 8, frames), axis=0)
    both = jnp.concatenate(
        [
            jnp.sum(grad_sq, axis=0, keepdims=True),
            jnp.sum(image_sq, axis=0, keepdims=True),
        ],
        axis=0,
    )
    stats[...] = jnp.broadcast_to(both[None], stats.shape)


def f32(*shape):
    return jax.ShapeDtypeStruct(shape, F32)


def bf16(*shape):
    return jax.ShapeDtypeStruct(shape, BF16)


def call(
    kernel, name, micros, outs, args, scratch=(), far=(), far_out=(), keep=(), limit=16
):
    def spec(arg):
        if any(arg is other for other in far):
            return HBM
        return SMEM if arg.dtype == jnp.int32 else VMEM

    in_specs = [jax.tree.map(spec, arg) for arg in args]
    in_specs.append(jax.tree.map(lambda _: VMEM, keep))

    def body(*refs):
        kernel(*refs[: len(args)], *refs[len(args) + 1 :])

    return pl.pallas_call(
        body,
        name=name,
        out_shape=outs,
        in_specs=in_specs,
        out_specs=tuple(
            jax.tree.map(lambda _: HBM if place in far_out else VMEM, out)
            for place, out in enumerate(outs)
        ),
        scratch_shapes=scratch,
        compiler_params=pltpu.CompilerParams(vmem_limit_bytes=int(limit * 2**20)),
        cost_estimate=pl.CostEstimate(
            flops=int(micros * 1e8), bytes_accessed=int(micros * 3e6), transcendentals=0
        ),
    )(*args, keep)


def swapped(first, second):
    size = lax.axis_size("tile")

    def pairs(start):
        both = [(i, i + 1) for i in range(start, size - 1, 2)]
        return both + [(j, i) for i, j in both]

    return lax.ppermute(first, "tile", pairs(0)), lax.ppermute(second, "tile", pairs(1))


def per_device(recording, footprints, pattern, decay, frame_gain, spikes):
    neurons, frames = spikes.shape
    stripe = pattern.shape[0]
    pattern = pattern.T
    own = neurons // LANES
    chunks = own + 2 * RIM
    lines = own + padded8(1)
    devices = lax.axis_size("tile") * lax.axis_size("tm")
    split = (f32(own, frames, LANES), f32(2 * RIM, frames, LANES))
    message = f32(RIM * LANES + padded8(RIM), frames)
    gains = frame_gain.reshape(1, frames)
    rates = decay.reshape(own, LANES)
    first, second, rates, spikes = call(
        rims_kernel,
        "rims",
        1.0,
        (message, message, f32(own, LANES), f32(neurons, frames)),
        (spikes, rates),
        [pltpu.SemaphoreType.DMA((4,))],
        far=(spikes, rates),
        limit=52,
    )
    first, second = swapped(first, second)
    ends_size = 4 * HB * PIX_BLOCK
    *owns, rows, pay, columns, feet_ends = call(
        prep_own_kernel,
        "prep_own",
        1.6,
        (split[0],) * 4
        + (f32(3, lines, LANES), f32(2, lines, LANES), f32(2, frames, LANES))
        + (bf16(ends_size, K * NEU_BLOCK),),
        (spikes, rates, gains, footprints),
        [pltpu.SemaphoreType.DMA((2,))],
        far=(footprints,),
        limit=44,
    )
    *rims, rows, pay = call(
        prep_rim_kernel,
        "prep_rim",
        0.3,
        (split[1],) * 4 + (f32(3, lines, LANES), f32(2, lines, LANES)),
        (first, second, columns, rows, pay),
    )
    s3, p3, pinv3, z3 = zip(owns, rims)
    constants = lax.all_gather(pay, "tm")
    pays = constants[:, 0]
    scratch = [
        pltpu.VMEM((stripe * K * NEU_BLOCK, frames), F32),
        pltpu.SMEM((stripe, 2 * HB + 1), jnp.int32),
    ]
    staged = [pltpu.VMEM((neurons, frames), F32), pltpu.SemaphoreType.DMA((PARTS,))]
    middle = stripe * NEU_BLOCK // LANES // 2
    halves = (middle + 2 * RIM, chunks - middle)
    zone = (2 * RIM, frames, LANES)
    border = (4 * RIM, frames, LANES)
    for iteration in range(ITERS):
        ends = iteration == ITERS - 1
        ext, zones, spill, send_a, send_b, *traces = call(
            edge_kernel,
            "edge",
            2.5,
            (
                bf16(chunks * LANES, frames),
                f32(*border),
                f32(*border),
                bf16(*zone),
                bf16(*zone),
            )
            + ((f32(neurons, frames),) if ends else ()),
            (pattern, z3, p3, rows, constants, pays, feet_ends, recording),
            scratch,
            keep=(s3[0],) if ends else (),
        )
        got_a, got_b = swapped(send_a, send_b)
        held = (s3[0],) if ends else ()
        r_inner, pay, *traces = call(
            inner_kernel,
            "inner",
            4.0,
            (f32(chunks - 4 * RIM, frames, LANES), f32(2, lines, LANES))
            + ((f32(neurons, frames),) if ends else ()),
            (pattern, p3, pinv3, rows, ext, spill, footprints, recording, traces),
            scratch + ([pltpu.SemaphoreType.DMA] if ends else []),
            far_out=(2,),
            keep=held,
        )
        r_border, pay = call(
            border_kernel,
            "border",
            0.3,
            (f32(*border), f32(2, lines, LANES)),
            (zones, got_a, got_b, p3, pinv3, rows, pay),
            keep=held,
        )
        pays = lax.all_gather(pay, "tm")
        g3, stats = call(
            direction_kernel,
            "direction",
            4.0,
            (f32(chunks, frames, LANES), f32(devices, 2, LANES)),
            (pattern, r_inner, r_border, p3, pinv3, rows, constants, pays, footprints),
            [
                pltpu.VMEM((halves[0] * LANES, frames), BF16),
                pltpu.VMEM((halves[1] * LANES, frames), BF16),
            ],
            keep=held,
        )
        stats = lax.all_to_all(stats, ("tile", "tm") if ends else ("tm", "tile"), 0, 0)
        if ends:
            (out,) = call(
                final_kernel,
                "final",
                1.4,
                (f32(neurons, frames),),
                (s3[0], g3, stats),
                staged,
                far_out=(0,),
            )
            return out, traces[0]
        s3, z3, pay = call(
            update_kernel,
            "update",
            0.6,
            (split if iteration < ITERS - 2 else split[:1], split, f32(lines, LANES)),
            (s3, g3, stats, p3, pinv3, rows),
        )
        pays = lax.all_gather(pay, "tm")


def solution(mesh):
    return jax.shard_map(
        per_device,
        mesh=mesh,
        in_specs=(
            P("tile", "tm"),
            P("tile", None),
            P("tile", None),
            P("tile"),
            P("tm"),
            P("tile", "tm"),
        ),
        out_specs=(P("tile", "tm"), P("tile", "tm")),
        check_vma=False,
    )
```

profile of v0, /device:TPU:0, one launch (start us, length us, event | category | flops | bytes accessed | tf_op | source)
XLA Modules:
  0.0 82.6 jit_solution(8681940128043317306)
XLA Ops:
  0.6 0.0 copy-start.3
  0.6 0.7 copy-done.3
  1.3 1.4 %rims.1 = (f32[136,128]{1,0:T(8,128)S(1)}, f32[136,128]{1,0:T(8,128)S(1)}, f32[16,128]{1,0:T(8,128)S(1)}, f32[2048,128]{1,0:T(8,128)S(1)}) custom-call(f32[2048,128]{1,0:T(8,128)} %refs_0_.1, f32[16,128]{1,0:T(8,128)S(1)} %bitcast.23), custom_call_target="tpu_custom_call" | custom-call | flops 100000000 | bytes 3000000 | tf_op jit(solution)/shard_map/rims/pallas_call | solution.py:474
  2.7 3.0 %collective-permute-start = (f32[136,128]{1,0:T(8,128)S(1)}, f32[136,128]{1,0:T(8,128)S(1)}, u32[]{:S(2)}, u32[]{:S(2)}) collective-permute-start(f32[136,128]{1,0:T(8,128)S(1)} %get-tuple-element.51), channel_id=1, source_target_pairs={{0,1},{2,3},{4,5},{6,7},{1,0},{3,2},{5,4},{7,6},{8,9},{10,11},{12,... | collective-permute-start | bytes 208904 | tf_op jit(solution)/shard_map/ppermute | solution.py:498
  5.7 0.7 collective-permute-start.1
  6.4 0.0 copy-start.4
  6.4 0.6 copy-done.4
  7.0 0.0 copy-start.1
  7.0 0.0 copy-start.2
  7.0 2.5 %prep_own.1 = (f32[16,128,128]{2,1,0:T(8,128)S(1)}, f32[16,128,128]{2,1,0:T(8,128)S(1)}, f32[16,128,128]{2,1,0:T(8,128)S(1)}, f32[16,128,128]{2,1,0:T(8,128)S(1)...) custom-call(f32[2048,128]{1,0:T(8,128)S(1)} %get-tuple-element.48.re, ...), custom_call_target="tpu_custom_call" | custom-call | flops 160000000 | bytes 4800000 | tf_op jit(solution)/shard_map/prep_own/pallas_call | solution.py:474
  9.5 0.0 collective-permute-done.refs_0_
  9.5 0.0 collective-permute-done.1.refs_1_
  9.5 0.3 prep_rim.1
  9.8 5.3 %all-gather = f32[8,24,128]{2,1,0:T(8,128)S(1)} all-gather(f32[2,24,128]{2,1,0:T(8,128)S(1)} %get-tuple-element.64), channel_id=2, replica_groups=mesh['tm'=4,'tile'=8] {'tm'}, dimensions={0}, use_global_device_ids=true | all-gather | bytes 122880 | tf_op jit(solution)/shard_map/all_gather | solution.py:545
  15.2 0.0 copy-done.1
  15.2 0.0 copy-done.2
  15.2 0.0 copy-start
  15.2 1.9 %edge.2 = (bf16[2304,128]{1,0:T(8,128)(2,1)S(1)}, f32[4,128,128]{2,1,0:T(8,128)S(1)}, f32[4,128,128]{2,1,0:T(8,128)S(1)}, bf16[2,128,128]{2,1,0:T(8,128)(2,1)S(1)}, bf16[2,128,128]{2,1,0:T(8,128)(2,1)S(1)}) custom-call(s32[4,32]{1,0:T(4,128)S(1)} %bitcast.17, f32[16,128,128]{2,1,0:T(8,128)S(1)} %get-tuple-element.62.refs_1__0_, ...), custom_call_target="tpu_custom_call" | custom-call | flops 250000000 | bytes 7500000 | tf_op jit(solution)/shard_map/edge/pallas_call | solution.py:474
  17.0 4.3 %collective-permute-start.2 = (bf16[2,128,128]{2,1,0:T(8,128)(2,1)S(1)}, bf16[2,128,128]{2,1,0:T(8,128)(2,1)S(1)}, u32[]{:S(2)}, u32[]{:S(2)}) collective-permute-start(bf16[2,128,128]{2,1,0:T(8,128)(2,1)S(1)} %get-tuple-element.70), channel_id=1, source_target_pairs={{0,1},{2,3},{4,5},{6,7},{1,0},{3,2},{5,4},{7,6},{8,9},{10,11},{12,... | collective-permute-start | bytes 196616 | tf_op jit(solution)/shard_map/ppermute | solution.py:498
  21.4 0.7 collective-permute-start.3
  22.1 0.0 copy-done
  22.1 3.3 %inner.2 = (f32[14,128,128]{2,1,0:T(8,128)S(1)}, f32[2,24,128]{2,1,0:T(8,128)S(1)}) custom-call(s32[4,32]{1,0:T(4,128)S(1)} %bitcast.18, f32[16,128,128]{2,1,0:T(8,128)S(1)} %get-tuple-element.57.refs_2__0_.refs_1__0_.refs_3__0_, f32[2,128,128]{2,1,0:T(8,128)S(1)} %get-tuple-element.58.refs_2__1_.refs_1__1_.refs_3__1_, ...), custom_call_target="tpu_custom_call" | custom-call | flops 400000000 | bytes 12000000 | tf_op jit(solution)/shard_map/inner/pallas_call | solution.py:474
  25.4 0.0 collective-permute-done.2.refs_1_
  25.4 0.0 collective-permute-done.3.refs_2_
  25.4 0.3 border.2
  25.7 5.3 %all-gather.1 = f32[8,24,128]{2,1,0:T(8,128)S(1)} all-gather(f32[2,24,128]{2,1,0:T(8,128)S(1)} %get-tuple-element.74), channel_id=3, replica_groups=mesh['tm'=4,'tile'=8] {'tm'}, dimensions={0}, use_global_device_ids=true | all-gather | bytes 122880 | tf_op jit(solution)/shard_map/all_gather | solution.py:595
  31.0 2.5 %direction.2 = (f32[18,128,128]{2,1,0:T(8,128)S(1)}, f32[32,2,128]{2,1,0:T(2,128)S(1)}) custom-call(s32[4,32]{1,0:T(4,128)S(1)} %bitcast.19, f32[14,128,128]{2,1,0:T(8,128)S(1)} %get-tuple-element.68.refs_1_, f32[4,128,128]{2,1,0:T(8,128)S(1)} %get-tuple-element.73.refs_2_, f32[16,128,128]{2,1,0:T(8,128)S(1)} %get-tuple-element.57.refs_2__0_.refs_1__0_.refs_3__0_, ...), custom_call_target="tpu_custom_call" | custom-call | flops 400000000 | bytes 12000000 | tf_op jit(solution)/shard_map/direction/pallas_call | solution.py:474
  33.5 14.4 %all_to_all.10.refs_2_ = f32[32,2,128]{2,1,0:T(2,128)S(1)} all-to-all(f32[32,2,128]{2,1,0:T(2,128)S(1)} %get-tuple-element.76), channel_id=1, replica_groups=mesh['tm'=4,'tile'=8] {'tm','tile'}, dimensions={0} | all-to-all | bytes 65536 | tf_op jit(solution)/shard_map/all_to_all | solution.py:608
  47.9 0.7 update.1
  48.6 5.2 %all-gather.2 = f32[96,128]{1,0:T(8,128)S(1)} all-gather(f32[24,128]{1,0:T(8,128)S(1)} %get-tuple-element.80), channel_id=4, replica_groups=mesh['tm'=4,'tile'=8] {'tm'}, dimensions={0}, use_global_device_ids=true | all-gather | bytes 61440 | tf_op jit(solution)/shard_map/all_gather | solution.py:627
  53.8 1.9 %edge.3 = (bf16[2304,128]{1,0:T(8,128)(2,1)S(1)}, f32[4,128,128]{2,1,0:T(8,128)S(1)}, f32[4,128,128]{2,1,0:T(8,128)S(1)}, bf16[2,128,128]{2,1,0:T(8,128)(2,1)S(1...) custom-call(s32[4,32]{1,0:T(4,128)S(1)} %bitcast.20, f32[16,128,128]{2,1,0:T(8,128)S(1)} %get-tuple-element.78.refs_1__0_, ...), custom_call_target="tpu_custom_call" | custom-call | flops 250000000 | bytes 7500000 | tf_op jit(solution)/shard_map/edge/pallas_call | solution.py:474
  55.7 0.7 collective-permute-start.4
  56.5 0.8 %collective-permute-start.5 = (bf16[2,128,128]{2,1,0:T(8,128)(2,1)S(1)}, bf16[2,128,128]{2,1,0:T(8,128)(2,1)S(1)}, u32[]{:S(2)}, u32[]{:S(2)}) collective-permute-start(bf16[2,128,128]{2,1,0:T(8,128)(2,1)S(1)} %get-tuple-element.87), channel_id=1, source_target_pairs={{1,2},{3,4},{5,6},{2,1},{4,3},{6,5},{9,10},{11,12},{13,14},{10,9},... | collective-permute-start | bytes 196616 | tf_op jit(solution)/shard_map/ppermute | solution.py:498
  57.3 4.0 %inner.3 = (f32[14,128,128]{2,1,0:T(8,128)S(1)}, f32[2,24,128]{2,1,0:T(8,128)S(1)}, f32[2048,128]{1,0:T(8,128)}) custom-call(s32[4,32]{1,0:T(4,128)S(1)} %bitcast.21, f32[16,128,128]{2,1,0:T(8,128)S(1)} %get-tuple-element.57.refs_2__0_.refs_1__0_.refs_3__0_, f32[2,128,128]{2,1,0:T(8,128)S(1)} %get-tuple-element.58.refs_2__1_.refs_1__1_.refs_3__1_, ...), custom_call_target="tpu_custom_call" | custom-call | flops 400000000 | bytes 12000000 | tf_op jit(solution)/shard_map/inner/pallas_call | solution.py:474
  61.4 0.0 collective-permute-done.4.refs_1_
  61.4 0.0 collective-permute-done.5.refs_2_
  61.4 0.3 border.3
  61.7 5.3 %all-gather.3 = f32[8,24,128]{2,1,0:T(8,128)S(1)} all-gather(f32[2,24,128]{2,1,0:T(8,128)S(1)} %get-tuple-element.90), channel_id=5, replica_groups=mesh['tm'=4,'tile'=8] {'tm'}, dimensions={0}, use_global_device_ids=true | all-gather | bytes 122880 | tf_op jit(solution)/shard_map/all_gather | solution.py:595
  67.0 2.5 %direction.3 = (f32[18,128,128]{2,1,0:T(8,128)S(1)}, f32[32,2,128]{2,1,0:T(2,128)S(1)}) custom-call(s32[4,32]{1,0:T(4,128)S(1)} %bitcast.22, f32[14,128,128]{2,1,0:T(8,128)S(1)} %get-tuple-element.84.refs_1_, f32[4,128,128]{2,1,0:T(8,128)S(1)} %get-tuple-element.89.refs_2_, f32[16,128,128]{2,1,0:T(8,128)S(1)} %get-tuple-element.57.refs_2__0_.refs_1__0_.refs_3__0_, ...), custom_call_target="tpu_custom_call" | custom-call | flops 400000000 | bytes 12000000 | tf_op jit(solution)/shard_map/direction/pallas_call | solution.py:474
  69.5 11.6 %all_to_all.11.refs_2_ = f32[32,2,128]{2,1,0:T(2,128)S(1)} all-to-all(f32[32,2,128]{2,1,0:T(2,128)S(1)} %get-tuple-element.92), channel_id=1, replica_groups=mesh['tm'=4,'tile'=8] {'tile','tm'}, dimensions={0} | all-to-all | bytes 65536 | tf_op jit(solution)/shard_map/all_to_all | solution.py:608
  81.1 1.3 %final.1 = f32[2048,128]{1,0:T(8,128)} custom-call(f32[16,128,128]{2,1,0:T(8,128)S(1)} %get-tuple-element.77.refs_8__0_.refs_9__0_.refs_7__0_.refs_0_, f32[18,128,128]{2,1,0:T(8,128)S(1)} %get-tuple-element.91.refs_1_, f32[32,2,128]{2,1,0:T(2,128)S(1)} %all_to_all.11.refs_2_), custom_call_target="tpu_custom_call" | custom-call | flops 140000000 | bytes 4200000 | tf_op jit(solution)/shard_map/final/pallas_call | solution.py:474
  (1 shorter events, 0.0 us)
Async XLA Ops:
  0.6 0.7 copy-start.3
  2.7 6.8 %collective-permute-start = (f32[136,128]{1,0:T(8,128)S(1)}, f32[136,128]{1,0:T(8,128)S(1)}, u32[]{:S(2)}, u32[]{:S(2)}) collective-permute-start(f32[136,128]{1,0:T(8,128)S(1)} %get-tuple-element.51), channel_id=1, source_target_pairs={{0,1},{2,3},{4,5},{6,7},{1,0},{3,2},{5,4},{7,6},{8,9},{10,11},{12,... | collective-permute-start | bytes 208904 | tf_op jit(solution)/shard_map/ppermute | solution.py:498
  5.7 3.8 %collective-permute-start.1 = (f32[136,128]{1,0:T(8,128)S(1)}, f32[136,128]{1,0:T(8,128)S(1)}, u32[]{:S(2)}, u32[]{:S(2)}) collective-permute-start(f32[136,128]{1,0:T(8,128)S(1)} %get-tuple-element.52), channel_id=1, source_target_pairs={{1,2},{3,4},{5,6},{2,1},{4,3},{6,5},{9,10},{11,12},{13,14},{10,9},... | collective-permute-start | bytes 208904 | tf_op jit(solution)/shard_map/ppermute | solution.py:498
  6.4 0.7 copy-start.4
  7.0 8.1 %copy-start.1 = (bf16[8192,128]{1,0:T(8,128)(2,1)S(1)}, bf16[8192,128]{1,0:T(8,128)(2,1)}, u32[]{:S(2)}) copy-start(bf16[8192,128]{1,0:T(8,128)(2,1)} %refs_7_.7) | copy-start | bytes 6291460
  7.0 8.1 %copy-start.2 = (s32[32,4]{0,1:T(4,128)S(1)}, s32[32,4]{0,1:T(4,128)}, u32[]{:S(2)}) copy-start(s32[32,4]{0,1:T(4,128)} %param.8) | copy-start | bytes 1540
  15.2 6.9 %copy-start = (bf16[8192,256]{1,0:T(8,128)(2,1)S(1)}, bf16[8192,256]{1,0:T(8,128)(2,1)}, u32[]{:S(2)}) copy-start(bf16[8192,256]{1,0:T(8,128)(2,1)} %refs_8_.3) | copy-start | bytes 12582916
  17.0 8.3 %collective-permute-start.2 = (bf16[2,128,128]{2,1,0:T(8,128)(2,1)S(1)}, bf16[2,128,128]{2,1,0:T(8,128)(2,1)S(1)}, u32[]{:S(2)}, u32[]{:S(2)}) collective-permute-start(bf16[2,128,128]{2,1,0:T(8,128)(2,1)S(1)} %get-tuple-element.70), channel_id=1, source_target_pairs={{0,1},{2,3},{4,5},{6,7},{1,0},{3,2},{5,4},{7,6},{8,9},{10,11},{12,... | collective-permute-start | bytes 196616 | tf_op jit(solution)/shard_map/ppermute | solution.py:498
  21.4 4.0 %collective-permute-start.3 = (bf16[2,128,128]{2,1,0:T(8,128)(2,1)S(1)}, bf16[2,128,128]{2,1,0:T(8,128)(2,1)S(1)}, u32[]{:S(2)}, u32[]{:S(2)}) collective-permute-start(bf16[2,128,128]{2,1,0:T(8,128)(2,1)S(1)} %get-tuple-element.71), channel_id=1, source_target_pairs={{1,2},{3,4},{5,6},{2,1},{4,3},{6,5},{9,10},{11,12},{13,14},{10,9},... | collective-permute-start | bytes 196616 | tf_op jit(solution)/shard_map/ppermute | solution.py:498
  55.7 5.6 %collective-permute-start.4 = (bf16[2,128,128]{2,1,0:T(8,128)(2,1)S(1)}, bf16[2,128,128]{2,1,0:T(8,128)(2,1)S(1)}, u32[]{:S(2)}, u32[]{:S(2)}) collective-permute-start(bf16[2,128,128]{2,1,0:T(8,128)(2,1)S(1)} %get-tuple-element.86), channel_id=1, source_target_pairs={{0,1},{2,3},{4,5},{6,7},{1,0},{3,2},{5,4},{7,6},{8,9},{10,11},{12,... | collective-permute-start | bytes 196616 | tf_op jit(solution)/shard_map/ppermute | solution.py:498
  56.5 4.9 %collective-permute-start.5 = (bf16[2,128,128]{2,1,0:T(8,128)(2,1)S(1)}, bf16[2,128,128]{2,1,0:T(8,128)(2,1)S(1)}, u32[]{:S(2)}, u32[]{:S(2)}) collective-permute-start(bf16[2,128,128]{2,1,0:T(8,128)(2,1)S(1)} %get-tuple-element.87), channel_id=1, source_target_pairs={{1,2},{3,4},{5,6},{2,1},{4,3},{6,5},{9,10},{11,12},{13,14},{10,9},... | collective-permute-start | bytes 196616 | tf_op jit(solution)/shard_map/ppermute | solution.py:498
where the time goes:
time: 82.9 us; the launch traced here: 82.6 us
  blocking collectives  47.2 us (57%)
  Pallas kernels  22.8 us (28%)
  starting transfers between devices  10.3 us (12%)
  local copies, waits for them, and re-layouts  1.36 us (2%)
  between operations  0.99 us (1%)
    all_to_all x2, blocking collectives, per_device(): lax.all_to_all(stats, ('tile', 'tm') if ends else ('tm', 'tile'), 0, 0)  26 us
    pallas_call x13, Pallas kernels, call(): pl.pallas_call(body, name=name, out_shape=outs, in_specs=in_specs, out_sp...  22.8 us
    all_gather x3, blocking collectives, per_device(): pays = lax.all_gather(pay, 'tm')  15.9 us
    ppermute x3, starting transfers between devices, swapped(): lax.ppermute(first, 'tile', pairs(0))  8.12 us
    all_gather x1, blocking collectives, per_device(): constants = lax.all_gather(pay, 'tm')  5.34 us
    ppermute x3, starting transfers between devices, swapped(): lax.ppermute(second, 'tile', pairs(1))  2.14 us
  transfers between devices with their start and end apart: 6, of which 0 were waited for; matrix products, arithmetic and copies ran while one was open for 0% of the time, Pallas kernels for 12%

commit v1 on v0

--- a/solution.py
+++ b/solution.py
@@ -136,6 +136,10 @@
         copy.wait()
 
 
+def after_start(compute):
+    pl.when(lax.axis_index("tm") >= 0)(compute)
+
+
 def prep_own_kernel(
     spikes, decay, gains, feet, s3, p3, pinv3, z3, rows, pay, columns, feet_ends, sems
 ):
@@ -150,18 +154,22 @@
     ]
     for fetch in fetches:
         fetch.start()
-    middle, whole, prefix_col, inverse_col = gain_columns(gains[...])
-    columns[0] = prefix_col
-    columns[1] = inverse_col
-    rows[...] = jnp.ones_like(rows)
-    rows[0, chunks : chunks + 1, :] = middle
-    pay[...] = jnp.zeros_like(pay)
-    pay[0, chunks : chunks + 1, :] = whole
-    shared = middle, prefix_col, inverse_col, table(spikes.shape[1], False)
-    for i in range(own):
-        field = spikes[i * LANES : (i + 1) * LANES, :]
-        at = [ref.at[i] for ref in (s3, p3, pinv3, z3)]
-        prep_chunk(i + RIM, decay[i : i + 1, :], field, shared, *at, rows, pay)
+
+    @after_start
+    def _():
+        middle, whole, prefix_col, inverse_col = gain_columns(gains[...])
+        columns[0] = prefix_col
+        columns[1] = inverse_col
+        rows[...] = jnp.ones_like(rows)
+        rows[0, chunks : chunks + 1, :] = middle
+        pay[...] = jnp.zeros_like(pay)
+        pay[0, chunks : chunks + 1, :] = whole
+        shared = middle, prefix_col, inverse_col, table(spikes.shape[1], False)
+        for i in range(own):
+            field = spikes[i * LANES : (i + 1) * LANES, :]
+            at = [ref.at[i] for ref in (s3, p3, pinv3, z3)]
+            prep_chunk(i + RIM, decay[i : i + 1, :], field, shared, *at, rows, pay)
+
     for fetch in fetches:
         fetch.wait()
 
@@ -219,21 +227,22 @@
 
 def final_kernel(s3, g3, stats, out, here, sems):
     size = step_size(stats)
-    own = s3.shape[0]
-    rows = out.shape[0] // PARTS
-    copies = [
-        pltpu.make_async_copy(
-            here.at[pl.ds(i * rows, rows)], out.at[pl.ds(i * rows, rows)], sems.at[i]
-        )
-        for i in range(PARTS)
-    ]
-    for i in range(own):
-        field = jnp.maximum(s3[i] - size * g3[i + RIM], 0.0)
-        here[i * LANES : (i + 1) * LANES, :] = field.T
-        if (i + 1) % (own // PARTS) == 0:
-            copies[i // (own // PARTS)].start()
-    for copy in copies:
-        copy.wait()
+    part = s3.shape[0] // PARTS
+
+    def copy(i):
+        at = pl.ds(pl.multiple_of(i * part * LANES, LANES), part * LANES)
+        return pltpu.make_async_copy(here.at[at], out.at[at], sems.at[i])
+
+    @pl.loop(0, PARTS)
+    def _(i):
+        for j in range(part):
+            c = i * part + j
+            field = jnp.maximum(s3[c] - size * g3[c + RIM], 0.0)
+            here[pl.ds(pl.multiple_of(c * LANES, LANES), LANES), :] = field.T
+        copy(i).start()
+
+    for i in range(PARTS):
+        copy(i).wait()
 
 
 def picked(ext, pattern, q, first=0):
@@ -307,10 +316,14 @@
         note_places(pattern, place, start, stop)
 
     def trace(c):
-        field = (chunk(p3, c)[...] * (chunk(z3, c)[...] + carry[c : c + 1, :])).T
-        ext[c * LANES : (c + 1) * LANES, :] = field.astype(BF16)
+        field = chunk(p3, c)[...] * (chunk(z3, c)[...] + carry[c : c + 1, :])
+        at = slice(c * LANES, (c + 1) * LANES)
         if traces and RIM <= c < chunks - RIM:
+            field = field.T
             traces[0][(c - RIM) * LANES : (c - RIM + 1) * LANES, :] = field
+            ext[at, :] = field.astype(BF16)
+        else:
+            ext[at, :] = field.astype(BF16).T
 
     near = 4 * RIM
     for c in [*range(near), *range(chunks - near, chunks)]:
@@ -348,27 +361,33 @@
         copy.start()
     else:
         contrib, place = rest
-    chunks = chunk_count(p3)
-    frames = spill.shape[1]
-    stripe = pattern.shape[1]
-    edge = 2 * HB
-    note_places(pattern, place, edge, stripe - edge)
-    sums_table = table(frames, True)
-    pay[...] = jnp.zeros_like(pay)
-    inner = chunks - 4 * RIM
-    for q in range(edge, stripe - edge):
-        pull_back(pattern, ext, feet, record, contrib, q)
-    for i in range(inner):
-        c = i + 2 * RIM
-        field = gathered(contrib, place, c, ((edge, stripe - edge),))
-        if i < 2 * RIM:
-            field = field + spill[i]
-        if i >= inner - 2 * RIM:
-            field = field + spill[i - inner + 4 * RIM]
-        p, pinv = chunk(p3, c)[...], chunk(pinv3, c)[...]
-        adjoint_chunk(sums_table, field, p, pinv, rows, c, r3.at[i], pay)
+
+    def compute():
+        chunks = chunk_count(p3)
+        frames = spill.shape[1]
+        stripe = pattern.shape[1]
+        edge = 2 * HB
+        note_places(pattern, place, edge, stripe - edge)
+        sums_table = table(frames, True)
+        pay[...] = jnp.zeros_like(pay)
+        inner = chunks - 4 * RIM
+        for q in range(edge, stripe - edge):
+            pull_back(pattern, ext, feet, record, contrib, q)
+        for i in range(inner):
+            c = i + 2 * RIM
+            field = gathered(contrib, place, c, ((edge, stripe - edge),))
+            if i < 2 * RIM:
+                field = field + spill[i]
+            if i >= inner - 2 * RIM:
+                field = field + spill[i - inner + 4 * RIM]
+            p, pinv = chunk(p3, c)[...], chunk(pinv3, c)[...]
+            adjoint_chunk(sums_table, field, p, pinv, rows, c, r3.at[i], pay)
+
     if traces:
+        after_start(compute)
         copy.wait()
+    else:
+        compute()
 
 
 def border_kernel(zones, got_a, got_b, p3, pinv3, rows, pay_inner, r3, pay):
@@ -605,7 +624,7 @@
             ],
             keep=held,
         )
-        stats = lax.all_to_all(stats, ("tile", "tm") if ends else ("tm", "tile"), 0, 0)
+        stats = lax.all_to_all(stats, ("tile", "tm"), 0, 0)
         if ends:
             (out,) = call(
                 final_kernel,

time: 82.9 us -> 82.6 us (level)
  Pallas kernels: 22.8 us -> 21.5 us
  blocking collectives: 47.2 us -> 48.3 us
    pallas_call x13, Pallas kernels: 22.8 us -> 21.5 us  [call(): pl.pallas_call(body, name=name, out_shape=outs, in_specs=in_specs, out_sp...]
    all_to_all x2, blocking collectives: 26 us -> 27.1 us  [per_device(): stats = lax.all_to_all(stats, ('tile', 'tm'), 0, 0)]
  transfers between devices with their start and end apart: 6 -> 6, of which waited for: 0 -> 0; matrix products, arithmetic and copies ran while one was open for 0% -> 0% of each run, Pallas kernels for 12% -> 10%
where the time goes in v1:
time: 82.6 us; the launch traced here: 82.3 us
  blocking collectives  48.3 us (58%)
  Pallas kernels  21.5 us (26%)
  starting transfers between devices  10.1 us (12%)
  local copies, waits for them, and re-layouts  1.36 us (2%)
  between operations  0.99 us (1%)
    all_to_all x2, blocking collectives, per_device(): stats = lax.all_to_all(stats, ('tile', 'tm'), 0, 0)  27.1 us
    pallas_call x13, Pallas kernels, call(): pl.pallas_call(body, name=name, out_shape=outs, in_specs=in_specs, out_sp...  21.5 us
    all_gather x3, blocking collectives, per_device(): pays = lax.all_gather(pay, 'tm')  15.9 us
    ppermute x3, starting transfers between devices, swapped(): lax.ppermute(first, 'tile', pairs(0))  8.14 us
    all_gather x1, blocking collectives, per_device(): constants = lax.all_gather(pay, 'tm')  5.34 us
    ppermute x3, starting transfers between devices, swapped(): lax.ppermute(second, 'tile', pairs(1))  1.96 us
  transfers between devices with their start and end apart: 6, of which 0 were waited for; matrix products, arithmetic and copies ran while one was open for 0% of the time, Pallas kernels for 10%

profile of v1, /device:TPU:0, one launch (start us, length us, event | category | flops | bytes accessed | tf_op | source)
XLA Modules:
  0.0 82.3 jit_solution(5724330822930810722)
XLA Ops:
  0.6 0.0 copy-start.3
  0.6 0.7 copy-done.3
  1.3 1.4 %rims.1 = (f32[136,128]{1,0:T(8,128)S(1)}, f32[136,128]{1,0:T(8,128)S(1)}, f32[16,128]{1,0:T(8,128)S(1)}, f32[2048,128]{1,0:T(8,128)S(1)}) custom-call(f32[2048,128]{1,0:T(8,128)} %refs_0_.1, f32[16,128]{1,0:T(8,128)S(1)} %bitcast.23), custom_call_target="tpu_custom_call" | custom-call | flops 100000000 | bytes 3000000 | tf_op jit(solution)/shard_map/rims/pallas_call | solution.py:493
  2.7 3.0 %collective-permute-start = (f32[136,128]{1,0:T(8,128)S(1)}, f32[136,128]{1,0:T(8,128)S(1)}, u32[]{:S(2)}, u32[]{:S(2)}) collective-permute-start(f32[136,128]{1,0:T(8,128)S(1)} %get-tuple-element.51), channel_id=1, source_target_pairs={{0,1},{2,3},{4,5},{6,7},{1,0},{3,2},{5,4},{7,6},{8,9},{10,11},{12,... | collective-permute-start | bytes 208904 | tf_op jit(solution)/shard_map/ppermute | solution.py:517
  5.7 0.7 collective-permute-start.1
  6.4 0.0 copy-start.4
  6.4 0.6 copy-done.4
  7.0 0.0 copy-start.1
  7.0 0.0 copy-start.2
  7.0 1.4 %prep_own.1 = (f32[16,128,128]{2,1,0:T(8,128)S(1)}, f32[16,128,128]{2,1,0:T(8,128)S(1)}, f32[16,128,128]{2,1,0:T(8,128)S(1)}, f32[16,128,128]{2,1,0:T(8,128)S(1)...) custom-call(f32[2048,128]{1,0:T(8,128)S(1)} %get-tuple-element.48.re, ...), custom_call_target="tpu_custom_call" | custom-call | flops 160000000 | bytes 4800000 | tf_op jit(solution)/shard_map/prep_own/pallas_call | solution.py:493
  8.5 0.0 collective-permute-done.refs_0_
  8.5 0.0 collective-permute-done.1.refs_1_
  8.5 0.3 prep_rim.1
  8.8 5.3 %all-gather = f32[8,24,128]{2,1,0:T(8,128)S(1)} all-gather(f32[2,24,128]{2,1,0:T(8,128)S(1)} %get-tuple-element.64), channel_id=2, replica_groups=mesh['tm'=4,'tile'=8] {'tm'}, dimensions={0}, use_global_device_ids=true | all-gather | bytes 122880 | tf_op jit(solution)/shard_map/all_gather | solution.py:564
  14.1 0.0 copy-done.1
  14.1 0.0 copy-done.2
  14.1 0.0 copy-start
  14.2 1.8 %edge.2 = (bf16[2304,128]{1,0:T(8,128)(2,1)S(1)}, f32[4,128,128]{2,1,0:T(8,128)S(1)}, f32[4,128,128]{2,1,0:T(8,128)S(1)}, bf16[2,128,128]{2,1,0:T(8,128)(2,1)S(1)}, bf16[2,128,128]{2,1,0:T(8,128)(2,1)S(1)}) custom-call(s32[4,32]{1,0:T(4,128)S(1)} %bitcast.17, f32[16,128,128]{2,1,0:T(8,128)S(1)} %get-tuple-element.62.refs_1__0_, ...), custom_call_target="tpu_custom_call" | custom-call | flops 250000000 | bytes 7500000 | tf_op jit(solution)/shard_map/edge/pallas_call | solution.py:493
  16.0 4.5 %collective-permute-start.2 = (bf16[2,128,128]{2,1,0:T(8,128)(2,1)S(1)}, bf16[2,128,128]{2,1,0:T(8,128)(2,1)S(1)}, u32[]{:S(2)}, u32[]{:S(2)}) collective-permute-start(bf16[2,128,128]{2,1,0:T(8,128)(2,1)S(1)} %get-tuple-element.70), channel_id=1, source_target_pairs={{0,1},{2,3},{4,5},{6,7},{1,0},{3,2},{5,4},{7,6},{8,9},{10,11},{12,... | collective-permute-start | bytes 196616 | tf_op jit(solution)/shard_map/ppermute | solution.py:517
  20.5 0.7 collective-permute-start.3
  21.1 0.0 copy-done
  21.1 3.3 %inner.2 = (f32[14,128,128]{2,1,0:T(8,128)S(1)}, f32[2,24,128]{2,1,0:T(8,128)S(1)}) custom-call(s32[4,32]{1,0:T(4,128)S(1)} %bitcast.18, f32[16,128,128]{2,1,0:T(8,128)S(1)} %get-tuple-element.57.refs_2__0_.refs_1__0_.refs_3__0_, f32[2,128,128]{2,1,0:T(8,128)S(1)} %get-tuple-element.58.refs_2__1_.refs_1__1_.refs_3__1_, ...), custom_call_target="tpu_custom_call" | custom-call | flops 400000000 | bytes 12000000 | tf_op jit(solution)/shard_map/inner/pallas_call | solution.py:493
  24.4 0.0 collective-permute-done.2.refs_1_
  24.4 0.0 collective-permute-done.3.refs_2_
  24.5 0.3 border.2
  24.7 5.3 %all-gather.1 = f32[8,24,128]{2,1,0:T(8,128)S(1)} all-gather(f32[2,24,128]{2,1,0:T(8,128)S(1)} %get-tuple-element.74), channel_id=3, replica_groups=mesh['tm'=4,'tile'=8] {'tm'}, dimensions={0}, use_global_device_ids=true | all-gather | bytes 122880 | tf_op jit(solution)/shard_map/all_gather | solution.py:614
  30.1 2.5 %direction.2 = (f32[18,128,128]{2,1,0:T(8,128)S(1)}, f32[32,2,128]{2,1,0:T(2,128)S(1)}) custom-call(s32[4,32]{1,0:T(4,128)S(1)} %bitcast.19, f32[14,128,128]{2,1,0:T(8,128)S(1)} %get-tuple-element.68.refs_1_, f32[4,128,128]{2,1,0:T(8,128)S(1)} %get-tuple-element.73.refs_2_, f32[16,128,128]{2,1,0:T(8,128)S(1)} %get-tuple-element.57.refs_2__0_.refs_1__0_.refs_3__0_, ...), custom_call_target="tpu_custom_call" | custom-call | flops 400000000 | bytes 12000000 | tf_op jit(solution)/shard_map/direction/pallas_call | solution.py:493
  32.6 15.3 %all_to_all.10.refs_2_ = f32[32,2,128]{2,1,0:T(2,128)S(1)} all-to-all(f32[32,2,128]{2,1,0:T(2,128)S(1)} %get-tuple-element.76), channel_id=1, replica_groups=mesh['tm'=4,'tile'=8] {'tile','tm'}, dimensions={0} | all-to-all | bytes 65536 | tf_op jit(solution)/shard_map/all_to_all | solution.py:627
  47.9 0.7 update.1
  48.6 5.2 %all-gather.2 = f32[96,128]{1,0:T(8,128)S(1)} all-gather(f32[24,128]{1,0:T(8,128)S(1)} %get-tuple-element.80), channel_id=4, replica_groups=mesh['tm'=4,'tile'=8] {'tm'}, dimensions={0}, use_global_device_ids=true | all-gather | bytes 61440 | tf_op jit(solution)/shard_map/all_gather | solution.py:646
  53.9 1.9 %edge.3 = (bf16[2304,128]{1,0:T(8,128)(2,1)S(1)}, f32[4,128,128]{2,1,0:T(8,128)S(1)}, f32[4,128,128]{2,1,0:T(8,128)S(1)}, bf16[2,128,128]{2,1,0:T(8,128)(2,1)S(1...) custom-call(s32[4,32]{1,0:T(4,128)S(1)} %bitcast.20, f32[16,128,128]{2,1,0:T(8,128)S(1)} %get-tuple-element.78.refs_1__0_, ...), custom_call_target="tpu_custom_call" | custom-call | flops 250000000 | bytes 7500000 | tf_op jit(solution)/shard_map/edge/pallas_call | solution.py:493
  55.8 0.6 collective-permute-start.4
  56.4 0.7 collective-permute-start.5
  57.1 3.5 %inner.3 = (f32[14,128,128]{2,1,0:T(8,128)S(1)}, f32[2,24,128]{2,1,0:T(8,128)S(1)}, f32[2048,128]{1,0:T(8,128)}) custom-call(s32[4,32]{1,0:T(4,128)S(1)} %bitcast.21, f32[16,128,128]{2,1,0:T(8,128)S(1)} %get-tuple-element.57.refs_2__0_.refs_1__0_.refs_3__0_, f32[2,128,128]{2,1,0:T(8,128)S(1)} %get-tuple-element.58.refs_2__1_.refs_1__1_.refs_3__1_, ...), custom_call_target="tpu_custom_call" | custom-call | flops 400000000 | bytes 12000000 | tf_op jit(solution)/shard_map/inner/pallas_call | solution.py:493
  60.6 0.0 collective-permute-done.4.refs_1_
  60.6 0.0 collective-permute-done.5.refs_2_
  60.6 0.3 border.3
  60.9 5.3 %all-gather.3 = f32[8,24,128]{2,1,0:T(8,128)S(1)} all-gather(f32[2,24,128]{2,1,0:T(8,128)S(1)} %get-tuple-element.90), channel_id=5, replica_groups=mesh['tm'=4,'tile'=8] {'tm'}, dimensions={0}, use_global_device_ids=true | all-gather | bytes 122880 | tf_op jit(solution)/shard_map/all_gather | solution.py:614
  66.2 2.5 %direction.3 = (f32[18,128,128]{2,1,0:T(8,128)S(1)}, f32[32,2,128]{2,1,0:T(2,128)S(1)}) custom-call(s32[4,32]{1,0:T(4,128)S(1)} %bitcast.22, f32[14,128,128]{2,1,0:T(8,128)S(1)} %get-tuple-element.84.refs_1_, f32[4,128,128]{2,1,0:T(8,128)S(1)} %get-tuple-element.89.refs_2_, f32[16,128,128]{2,1,0:T(8,128)S(1)} %get-tuple-element.57.refs_2__0_.refs_1__0_.refs_3__0_, ...), custom_call_target="tpu_custom_call" | custom-call | flops 400000000 | bytes 12000000 | tf_op jit(solution)/shard_map/direction/pallas_call | solution.py:493
  68.8 11.8 %all_to_all.11.refs_2_ = f32[32,2,128]{2,1,0:T(2,128)S(1)} all-to-all(f32[32,2,128]{2,1,0:T(2,128)S(1)} %get-tuple-element.92), channel_id=1, replica_groups=mesh['tm'=4,'tile'=8] {'tile','tm'}, dimensions={0} | all-to-all | bytes 65536 | tf_op jit(solution)/shard_map/all_to_all | solution.py:627
  80.5 1.6 %final.1 = f32[2048,128]{1,0:T(8,128)} custom-call(f32[16,128,128]{2,1,0:T(8,128)S(1)} %get-tuple-element.77.refs_8__0_.refs_9__0_.refs_7__0_.refs_0_, f32[18,128,128]{2,1,0:T(8,128)S(1)} %get-tuple-element.91.refs_1_, f32[32,2,128]{2,1,0:T(2,128)S(1)} %all_to_all.11.refs_2_), custom_call_target="tpu_custom_call" | custom-call | flops 140000000 | bytes 4200000 | tf_op jit(solution)/shard_map/final/pallas_call | solution.py:493
  (1 shorter events, 0.0 us)
Async XLA Ops:
  0.6 0.7 copy-start.3
  2.7 5.8 %collective-permute-start = (f32[136,128]{1,0:T(8,128)S(1)}, f32[136,128]{1,0:T(8,128)S(1)}, u32[]{:S(2)}, u32[]{:S(2)}) collective-permute-start(f32[136,128]{1,0:T(8,128)S(1)} %get-tuple-element.51), channel_id=1, source_target_pairs={{0,1},{2,3},{4,5},{6,7},{1,0},{3,2},{5,4},{7,6},{8,9},{10,11},{12,... | collective-permute-start | bytes 208904 | tf_op jit(solution)/shard_map/ppermute | solution.py:517
  5.7 2.8 %collective-permute-start.1 = (f32[136,128]{1,0:T(8,128)S(1)}, f32[136,128]{1,0:T(8,128)S(1)}, u32[]{:S(2)}, u32[]{:S(2)}) collective-permute-start(f32[136,128]{1,0:T(8,128)S(1)} %get-tuple-element.52), channel_id=1, source_target_pairs={{1,2},{3,4},{5,6},{2,1},{4,3},{6,5},{9,10},{11,12},{13,14},{10,9},... | collective-permute-start | bytes 208904 | tf_op jit(solution)/shard_map/ppermute | solution.py:517
  6.4 0.7 copy-start.4
  7.0 7.1 %copy-start.1 = (bf16[8192,128]{1,0:T(8,128)(2,1)S(1)}, bf16[8192,128]{1,0:T(8,128)(2,1)}, u32[]{:S(2)}) copy-start(bf16[8192,128]{1,0:T(8,128)(2,1)} %refs_7_.7) | copy-start | bytes 6291460
  7.0 7.1 %copy-start.2 = (s32[32,4]{0,1:T(4,128)S(1)}, s32[32,4]{0,1:T(4,128)}, u32[]{:S(2)}) copy-start(s32[32,4]{0,1:T(4,128)} %param.8) | copy-start | bytes 1540
  14.1 7.0 %copy-start = (bf16[8192,256]{1,0:T(8,128)(2,1)S(1)}, bf16[8192,256]{1,0:T(8,128)(2,1)}, u32[]{:S(2)}) copy-start(bf16[8192,256]{1,0:T(8,128)(2,1)} %refs_8_.3) | copy-start | bytes 12582916
  16.0 8.4 %collective-permute-start.2 = (bf16[2,128,128]{2,1,0:T(8,128)(2,1)S(1)}, bf16[2,128,128]{2,1,0:T(8,128)(2,1)S(1)}, u32[]{:S(2)}, u32[]{:S(2)}) collective-permute-start(bf16[2,128,128]{2,1,0:T(8,128)(2,1)S(1)} %get-tuple-element.70), channel_id=1, source_target_pairs={{0,1},{2,3},{4,5},{6,7},{1,0},{3,2},{5,4},{7,6},{8,9},{10,11},{12,... | collective-permute-start | bytes 196616 | tf_op jit(solution)/shard_map/ppermute | solution.py:517
  20.5 4.0 %collective-permute-start.3 = (bf16[2,128,128]{2,1,0:T(8,128)(2,1)S(1)}, bf16[2,128,128]{2,1,0:T(8,128)(2,1)S(1)}, u32[]{:S(2)}, u32[]{:S(2)}) collective-permute-start(bf16[2,128,128]{2,1,0:T(8,128)(2,1)S(1)} %get-tuple-element.71), channel_id=1, source_target_pairs={{1,2},{3,4},{5,6},{2,1},{4,3},{6,5},{9,10},{11,12},{13,14},{10,9},... | collective-permute-start | bytes 196616 | tf_op jit(solution)/shard_map/ppermute | solution.py:517
  55.8 4.8 %collective-permute-start.4 = (bf16[2,128,128]{2,1,0:T(8,128)(2,1)S(1)}, bf16[2,128,128]{2,1,0:T(8,128)(2,1)S(1)}, u32[]{:S(2)}, u32[]{:S(2)}) collective-permute-start(bf16[2,128,128]{2,1,0:T(8,128)(2,1)S(1)} %get-tuple-element.86), channel_id=1, source_target_pairs={{0,1},{2,3},{4,5},{6,7},{1,0},{3,2},{5,4},{7,6},{8,9},{10,11},{12,... | collective-permute-start | bytes 196616 | tf_op jit(solution)/shard_map/ppermute | solution.py:517
  56.4 4.2 %collective-permute-start.5 = (bf16[2,128,128]{2,1,0:T(8,128)(2,1)S(1)}, bf16[2,128,128]{2,1,0:T(8,128)(2,1)S(1)}, u32[]{:S(2)}, u32[]{:S(2)}) collective-permute-start(bf16[2,128,128]{2,1,0:T(8,128)(2,1)S(1)} %get-tuple-element.87), channel_id=1, source_target_pairs={{1,2},{3,4},{5,6},{2,1},{4,3},{6,5},{9,10},{11,12},{13,14},{10,9},... | collective-permute-start | bytes 196616 | tf_op jit(solution)/shard_map/ppermute | solution.py:517

commit v2 on v1

--- a/solution.py
+++ b/solution.py
@@ -7,7 +7,7 @@
 
 NEU_BLOCK = 64
 PIX_BLOCK = 256
-PARTS = 4
+PARTS = 8
 K = 4
 HB = 2
 ITERS = 2
@@ -105,7 +105,7 @@
     return middle, whole, prefix_col, inverse_col
 
 
-def rims_kernel(spikes, decay, first, second, rates_here, spikes_here, sems):
+def rims_kernel(spikes, decay, first, second, rates_here, sems):
     edge = RIM * LANES
     neurons = spikes.shape[0]
     own = decay.shape[0]
@@ -122,7 +122,6 @@
             second.at[pl.ds(0, edge)],
             sems.at[2],
         ),
-        pltpu.make_async_copy(spikes, spikes_here, sems.at[3]),
     ]
     for copy in copies:
         copy.start()
@@ -228,21 +227,25 @@
 def final_kernel(s3, g3, stats, out, here, sems):
     size = step_size(stats)
     part = s3.shape[0] // PARTS
-
-    def copy(i):
-        at = pl.ds(pl.multiple_of(i * part * LANES, LANES), part * LANES)
-        return pltpu.make_async_copy(here.at[at], out.at[at], sems.at[i])
-
-    @pl.loop(0, PARTS)
-    def _(i):
-        for j in range(part):
-            c = i * part + j
-            field = jnp.maximum(s3[c] - size * g3[c + RIM], 0.0)
-            here[pl.ds(pl.multiple_of(c * LANES, LANES), LANES), :] = field.T
-        copy(i).start()
-
+    copies = [
+        pltpu.make_async_copy(
+            here.at[pl.ds(i * part * LANES, part * LANES)],
+            out.at[pl.ds(i * part * LANES, part * LANES)],
+            sems.at[i],
+        )
+        for i in range(PARTS)
+    ]
     for i in range(PARTS):
-        copy(i).wait()
+
+        @after_start
+        def _():
+            for c in range(i * part, (i + 1) * part):
+                field = jnp.maximum(s3[c] - size * g3[c + RIM], 0.0)
+                here[c * LANES : (c + 1) * LANES, :] = field.T
+            copies[i].start()
+
+    for copy in copies:
+        copy.wait()
 
 
 def picked(ext, pattern, q, first=0):
@@ -529,15 +532,15 @@
     message = f32(RIM * LANES + padded8(RIM), frames)
     gains = frame_gain.reshape(1, frames)
     rates = decay.reshape(own, LANES)
-    first, second, rates, spikes = call(
+    first, second, rates = call(
         rims_kernel,
         "rims",
         1.0,
-        (message, message, f32(own, LANES), f32(neurons, frames)),
+        (message, message, f32(own, LANES)),
         (spikes, rates),
-        [pltpu.SemaphoreType.DMA((4,))],
+        [pltpu.SemaphoreType.DMA((3,))],
         far=(spikes, rates),
-        limit=52,
+        limit=53,
     )
     first, second = swapped(first, second)
     ends_size = 4 * HB * PIX_BLOCK

time: 82.6 us -> 81.9 us (level)
  local copies, waits for them, and re-layouts: 1.36 us -> 2.58 us
  blocking collectives: 48.3 us -> 47.2 us
    unnamed x10 -> x12, local copies, waits for them, and re-layouts: 1.35 us -> 2.58 us
    all_to_all x2, blocking collectives: 27.1 us -> 26 us  [per_device(): stats = lax.all_to_all(stats, ('tile', 'tm'), 0, 0)]
where the time goes in v2:
time: 81.9 us; the launch traced here: 81.5 us
  blocking collectives  47.2 us (58%)
  Pallas kernels  20.7 us (25%)
  starting transfers between devices  9.97 us (12%)
  local copies, waits for them, and re-layouts  2.58 us (3%)
  between operations  0.99 us (1%)
    all_to_all x2, blocking collectives, per_device(): stats = lax.all_to_all(stats, ('tile', 'tm'), 0, 0)  26 us
    pallas_call x13, Pallas kernels, call(): pl.pallas_call(body, name=name, out_shape=outs, in_specs=in_specs, out_sp...  20.7 us
    all_gather x3, blocking collectives, per_device(): pays = lax.all_gather(pay, 'tm')  15.9 us
    ppermute x3, starting transfers between devices, swapped(): lax.ppermute(first, 'tile', pairs(0))  8.01 us
    all_gather x1, blocking collectives, per_device(): constants = lax.all_gather(pay, 'tm')  5.34 us
    unnamed x12, local copies, waits for them, and re-layouts  2.58 us
    ppermute x3, starting transfers between devices, swapped(): lax.ppermute(second, 'tile', pairs(1))  1.96 us
  transfers between devices with their start and end apart: 6, of which 0 were waited for; matrix products, arithmetic and copies ran while one was open for 0% of the time, Pallas kernels for 10%

profile of v2, /device:TPU:0, one launch (start us, length us, event | category | flops | bytes accessed | tf_op | source)
XLA Modules:
  0.0 81.5 jit_solution(14047098292988313925)
XLA Ops:
  0.6 0.0 copy-start.4
  0.6 0.7 copy-done.4
  1.3 0.9 %rims.1 = (f32[136,128]{1,0:T(8,128)S(1)}, f32[136,128]{1,0:T(8,128)S(1)}, f32[16,128]{1,0:T(8,128)S(1)}) custom-call(f32[2048,128]{1,0:T(8,128)} %refs_0_.3, f32[16,128]{1,0:T(8,128)S(1)} %bitcast.23), custom_call_target="tpu_custom_call" | custom-call | flops 100000000 | bytes 3000000 | tf_op jit(solution)/shard_map/rims/pallas_call | solution.py:496
  2.2 3.0 %collective-permute-start = (f32[136,128]{1,0:T(8,128)S(1)}, f32[136,128]{1,0:T(8,128)S(1)}, u32[]{:S(2)}, u32[]{:S(2)}) collective-permute-start(f32[136,128]{1,0:T(8,128)S(1)} %get-tuple-element.49), channel_id=1, source_target_pairs={{0,1},{2,3},{4,5},{6,7},{1,0},{3,2},{5,4},{7,6},{8,9},{10,11},{12,... | collective-permute-start | bytes 208904 | tf_op jit(solution)/shard_map/ppermute | solution.py:520
  5.3 0.7 collective-permute-start.1
  5.9 0.0 copy-start.2
  5.9 1.2 %copy-done.2 = f32[2048,128]{1,0:T(8,128)S(1)} copy-done((f32[2048,128]{1,0:T(8,128)S(1)}, f32[2048,128]{1,0:T(8,128)}, u32[]{:S(2)}) %copy-start.2) | copy-done | bytes 1048600
  7.2 0.0 copy-start.5
  7.2 0.7 copy-done.5
  7.8 0.0 copy-start.1
  7.8 0.0 copy-start.3
  7.8 1.4 %prep_own.1 = (f32[16,128,128]{2,1,0:T(8,128)S(1)}, f32[16,128,128]{2,1,0:T(8,128)S(1)}, f32[16,128,128]{2,1,0:T(8,128)S(1)}, f32[16,128,128]{2,1,0:T(8,128)S(1)...) custom-call(f32[2048,128]{1,0:T(8,128)S(1)} %copy-done.2, ...), custom_call_target="tpu_custom_call" | custom-call | flops 160000000 | bytes 4800000 | tf_op jit(solution)/shard_map/prep_own/pallas_call | solution.py:496
  9.3 0.0 collective-permute-done.refs_0_
  9.3 0.0 collective-permute-done.1.refs_1_
  9.3 0.3 prep_rim.1
  9.6 5.3 %all-gather = f32[8,24,128]{2,1,0:T(8,128)S(1)} all-gather(f32[2,24,128]{2,1,0:T(8,128)S(1)} %get-tuple-element.62), channel_id=2, replica_groups=mesh['tm'=4,'tile'=8] {'tm'}, dimensions={0}, use_global_device_ids=true | all-gather | bytes 122880 | tf_op jit(solution)/shard_map/all_gather | solution.py:567
  14.9 0.0 copy-done.1
  14.9 0.0 copy-done.3
  14.9 0.0 copy-start
  14.9 1.8 %edge.2 = (bf16[2304,128]{1,0:T(8,128)(2,1)S(1)}, f32[4,128,128]{2,1,0:T(8,128)S(1)}, f32[4,128,128]{2,1,0:T(8,128)S(1)}, bf16[2,128,128]{2,1,0:T(8,128)(2,1)S(1)}, bf16[2,128,128]{2,1,0:T(8,128)(2,1)S(1)}) custom-call(s32[4,32]{1,0:T(4,128)S(1)} %bitcast.17, f32[16,128,128]{2,1,0:T(8,128)S(1)} %get-tuple-element.60.refs_1__0_, ...), custom_call_target="tpu_custom_call" | custom-call | flops 250000000 | bytes 7500000 | tf_op jit(solution)/shard_map/edge/pallas_call | solution.py:496
  16.8 4.3 %collective-permute-start.2 = (bf16[2,128,128]{2,1,0:T(8,128)(2,1)S(1)}, bf16[2,128,128]{2,1,0:T(8,128)(2,1)S(1)}, u32[]{:S(2)}, u32[]{:S(2)}) collective-permute-start(bf16[2,128,128]{2,1,0:T(8,128)(2,1)S(1)} %get-tuple-element.68), channel_id=1, source_target_pairs={{0,1},{2,3},{4,5},{6,7},{1,0},{3,2},{5,4},{7,6},{8,9},{10,11},{12,... | collective-permute-start | bytes 196616 | tf_op jit(solution)/shard_map/ppermute | solution.py:520
  21.1 0.7 collective-permute-start.3
  21.8 0.0 copy-done
  21.8 3.3 %inner.2 = (f32[14,128,128]{2,1,0:T(8,128)S(1)}, f32[2,24,128]{2,1,0:T(8,128)S(1)}) custom-call(s32[4,32]{1,0:T(4,128)S(1)} %bitcast.18, f32[16,128,128]{2,1,0:T(8,128)S(1)} %get-tuple-element.55.refs_2__0_.refs_1__0_.refs_3__0_, f32[2,128,128]{2,1,0:T(8,128)S(1)} %get-tuple-element.56.refs_2__1_.refs_1__1_.refs_3__1_, ...), custom_call_target="tpu_custom_call" | custom-call | flops 400000000 | bytes 12000000 | tf_op jit(solution)/shard_map/inner/pallas_call | solution.py:496
  25.1 0.0 collective-permute-done.2.refs_1_
  25.1 0.0 collective-permute-done.3.refs_2_
  25.1 0.3 border.2
  25.4 5.3 %all-gather.1 = f32[8,24,128]{2,1,0:T(8,128)S(1)} all-gather(f32[2,24,128]{2,1,0:T(8,128)S(1)} %get-tuple-element.72), channel_id=3, replica_groups=mesh['tm'=4,'tile'=8] {'tm'}, dimensions={0}, use_global_device_ids=true | all-gather | bytes 122880 | tf_op jit(solution)/shard_map/all_gather | solution.py:617
  30.7 2.5 %direction.2 = (f32[18,128,128]{2,1,0:T(8,128)S(1)}, f32[32,2,128]{2,1,0:T(2,128)S(1)}) custom-call(s32[4,32]{1,0:T(4,128)S(1)} %bitcast.19, f32[14,128,128]{2,1,0:T(8,128)S(1)} %get-tuple-element.66.refs_1_, f32[4,128,128]{2,1,0:T(8,128)S(1)} %get-tuple-element.71.refs_2_, f32[16,128,128]{2,1,0:T(8,128)S(1)} %get-tuple-element.55.refs_2__0_.refs_1__0_.refs_3__0_, ...), custom_call_target="tpu_custom_call" | custom-call | flops 400000000 | bytes 12000000 | tf_op jit(solution)/shard_map/direction/pallas_call | solution.py:496
  33.2 14.2 %all_to_all.10.refs_2_ = f32[32,2,128]{2,1,0:T(2,128)S(1)} all-to-all(f32[32,2,128]{2,1,0:T(2,128)S(1)} %get-tuple-element.74), channel_id=1, replica_groups=mesh['tm'=4,'tile'=8] {'tile','tm'}, dimensions={0} | all-to-all | bytes 65536 | tf_op jit(solution)/shard_map/all_to_all | solution.py:630
  47.5 0.7 update.1
  48.2 5.2 %all-gather.2 = f32[96,128]{1,0:T(8,128)S(1)} all-gather(f32[24,128]{1,0:T(8,128)S(1)} %get-tuple-element.78), channel_id=4, replica_groups=mesh['tm'=4,'tile'=8] {'tm'}, dimensions={0}, use_global_device_ids=true | all-gather | bytes 61440 | tf_op jit(solution)/shard_map/all_gather | solution.py:649
  53.4 1.9 %edge.3 = (bf16[2304,128]{1,0:T(8,128)(2,1)S(1)}, f32[4,128,128]{2,1,0:T(8,128)S(1)}, f32[4,128,128]{2,1,0:T(8,128)S(1)}, bf16[2,128,128]{2,1,0:T(8,128)(2,1)S(1...) custom-call(s32[4,32]{1,0:T(4,128)S(1)} %bitcast.20, f32[16,128,128]{2,1,0:T(8,128)S(1)} %get-tuple-element.76.refs_1__0_, ...), custom_call_target="tpu_custom_call" | custom-call | flops 250000000 | bytes 7500000 | tf_op jit(solution)/shard_map/edge/pallas_call | solution.py:496
  55.3 0.6 collective-permute-start.4
  55.9 0.7 collective-permute-start.5
  56.6 3.5 %inner.3 = (f32[14,128,128]{2,1,0:T(8,128)S(1)}, f32[2,24,128]{2,1,0:T(8,128)S(1)}, f32[2048,128]{1,0:T(8,128)}) custom-call(s32[4,32]{1,0:T(4,128)S(1)} %bitcast.21, f32[16,128,128]{2,1,0:T(8,128)S(1)} %get-tuple-element.55.refs_2__0_.refs_1__0_.refs_3__0_, f32[2,128,128]{2,1,0:T(8,128)S(1)} %get-tuple-element.56.refs_2__1_.refs_1__1_.refs_3__1_, ...), custom_call_target="tpu_custom_call" | custom-call | flops 400000000 | bytes 12000000 | tf_op jit(solution)/shard_map/inner/pallas_call | solution.py:496
  60.1 0.0 collective-permute-done.4.refs_1_
  60.2 0.0 collective-permute-done.5.refs_2_
  60.2 0.3 border.3
  60.4 5.3 %all-gather.3 = f32[8,24,128]{2,1,0:T(8,128)S(1)} all-gather(f32[2,24,128]{2,1,0:T(8,128)S(1)} %get-tuple-element.88), channel_id=5, replica_groups=mesh['tm'=4,'tile'=8] {'tm'}, dimensions={0}, use_global_device_ids=true | all-gather | bytes 122880 | tf_op jit(solution)/shard_map/all_gather | solution.py:617
  65.8 2.5 %direction.3 = (f32[18,128,128]{2,1,0:T(8,128)S(1)}, f32[32,2,128]{2,1,0:T(2,128)S(1)}) custom-call(s32[4,32]{1,0:T(4,128)S(1)} %bitcast.22, f32[14,128,128]{2,1,0:T(8,128)S(1)} %get-tuple-element.82.refs_1_, f32[4,128,128]{2,1,0:T(8,128)S(1)} %get-tuple-element.87.refs_2_, f32[16,128,128]{2,1,0:T(8,128)S(1)} %get-tuple-element.55.refs_2__0_.refs_1__0_.refs_3__0_, ...), custom_call_target="tpu_custom_call" | custom-call | flops 400000000 | bytes 12000000 | tf_op jit(solution)/shard_map/direction/pallas_call | solution.py:496
  68.3 11.8 %all_to_all.11.refs_2_ = f32[32,2,128]{2,1,0:T(2,128)S(1)} all-to-all(f32[32,2,128]{2,1,0:T(2,128)S(1)} %get-tuple-element.90), channel_id=1, replica_groups=mesh['tm'=4,'tile'=8] {'tile','tm'}, dimensions={0} | all-to-all | bytes 65536 | tf_op jit(solution)/shard_map/all_to_all | solution.py:630
  80.1 1.3 %final.1 = f32[2048,128]{1,0:T(8,128)} custom-call(f32[16,128,128]{2,1,0:T(8,128)S(1)} %get-tuple-element.75.refs_8__0_.refs_9__0_.refs_7__0_.refs_0_, f32[18,128,128]{2,1,0:T(8,128)S(1)} %get-tuple-element.89.refs_1_, f32[32,2,128]{2,1,0:T(2,128)S(1)} %all_to_all.11.refs_2_), custom_call_target="tpu_custom_call" | custom-call | flops 140000000 | bytes 4200000 | tf_op jit(solution)/shard_map/final/pallas_call | solution.py:496
  (1 shorter events, 0.0 us)
Async XLA Ops:
  0.6 0.7 copy-start.4
  2.2 7.0 %collective-permute-start = (f32[136,128]{1,0:T(8,128)S(1)}, f32[136,128]{1,0:T(8,128)S(1)}, u32[]{:S(2)}, u32[]{:S(2)}) collective-permute-start(f32[136,128]{1,0:T(8,128)S(1)} %get-tuple-element.49), channel_id=1, source_target_pairs={{0,1},{2,3},{4,5},{6,7},{1,0},{3,2},{5,4},{7,6},{8,9},{10,11},{12,... | collective-permute-start | bytes 208904 | tf_op jit(solution)/shard_map/ppermute | solution.py:520
  5.3 4.0 %collective-permute-start.1 = (f32[136,128]{1,0:T(8,128)S(1)}, f32[136,128]{1,0:T(8,128)S(1)}, u32[]{:S(2)}, u32[]{:S(2)}) collective-permute-start(f32[136,128]{1,0:T(8,128)S(1)} %get-tuple-element.50), channel_id=1, source_target_pairs={{1,2},{3,4},{5,6},{2,1},{4,3},{6,5},{9,10},{11,12},{13,14},{10,9},... | collective-permute-start | bytes 208904 | tf_op jit(solution)/shard_map/ppermute | solution.py:520
  5.9 1.2 %copy-start.2 = (f32[2048,128]{1,0:T(8,128)S(1)}, f32[2048,128]{1,0:T(8,128)}, u32[]{:S(2)}) copy-start(f32[2048,128]{1,0:T(8,128)} %refs_0_.3) | copy-start | bytes 3145732
  7.2 0.7 copy-start.5
  7.8 7.1 %copy-start.1 = (bf16[8192,128]{1,0:T(8,128)(2,1)S(1)}, bf16[8192,128]{1,0:T(8,128)(2,1)}, u32[]{:S(2)}) copy-start(bf16[8192,128]{1,0:T(8,128)(2,1)} %refs_7_.7) | copy-start | bytes 6291460
  7.8 7.1 %copy-start.3 = (s32[32,4]{0,1:T(4,128)S(1)}, s32[32,4]{0,1:T(4,128)}, u32[]{:S(2)}) copy-start(s32[32,4]{0,1:T(4,128)} %param.8) | copy-start | bytes 1540
  14.9 6.9 %copy-start = (bf16[8192,256]{1,0:T(8,128)(2,1)S(1)}, bf16[8192,256]{1,0:T(8,128)(2,1)}, u32[]{:S(2)}) copy-start(bf16[8192,256]{1,0:T(8,128)(2,1)} %refs_8_.3) | copy-start | bytes 12582916
  16.8 8.3 %collective-permute-start.2 = (bf16[2,128,128]{2,1,0:T(8,128)(2,1)S(1)}, bf16[2,128,128]{2,1,0:T(8,128)(2,1)S(1)}, u32[]{:S(2)}, u32[]{:S(2)}) collective-permute-start(bf16[2,128,128]{2,1,0:T(8,128)(2,1)S(1)} %get-tuple-element.68), channel_id=1, source_target_pairs={{0,1},{2,3},{4,5},{6,7},{1,0},{3,2},{5,4},{7,6},{8,9},{10,11},{12,... | collective-permute-start | bytes 196616 | tf_op jit(solution)/shard_map/ppermute | solution.py:520
  21.1 4.0 %collective-permute-start.3 = (bf16[2,128,128]{2,1,0:T(8,128)(2,1)S(1)}, bf16[2,128,128]{2,1,0:T(8,128)(2,1)S(1)}, u32[]{:S(2)}, u32[]{:S(2)}) collective-permute-start(bf16[2,128,128]{2,1,0:T(8,128)(2,1)S(1)} %get-tuple-element.69), channel_id=1, source_target_pairs={{1,2},{3,4},{5,6},{2,1},{4,3},{6,5},{9,10},{11,12},{13,14},{10,9},... | collective-permute-start | bytes 196616 | tf_op jit(solution)/shard_map/ppermute | solution.py:520
  55.3 4.8 %collective-permute-start.4 = (bf16[2,128,128]{2,1,0:T(8,128)(2,1)S(1)}, bf16[2,128,128]{2,1,0:T(8,128)(2,1)S(1)}, u32[]{:S(2)}, u32[]{:S(2)}) collective-permute-start(bf16[2,128,128]{2,1,0:T(8,128)(2,1)S(1)} %get-tuple-element.84), channel_id=1, source_target_pairs={{0,1},{2,3},{4,5},{6,7},{1,0},{3,2},{5,4},{7,6},{8,9},{10,11},{12,... | collective-permute-start | bytes 196616 | tf_op jit(solution)/shard_map/ppermute | solution.py:520
  55.9 4.2 %collective-permute-start.5 = (bf16[2,128,128]{2,1,0:T(8,128)(2,1)S(1)}, bf16[2,128,128]{2,1,0:T(8,128)(2,1)S(1)}, u32[]{:S(2)}, u32[]{:S(2)}) collective-permute-start(bf16[2,128,128]{2,1,0:T(8,128)(2,1)S(1)} %get-tuple-element.85), channel_id=1, source_target_pairs={{1,2},{3,4},{5,6},{2,1},{4,3},{6,5},{9,10},{11,12},{13,14},{10,9},... | collective-permute-start | bytes 196616 | tf_op jit(solution)/shard_map/ppermute | solution.py:520

commit v3 on v2

--- a/solution.py
+++ b/solution.py
@@ -197,8 +197,19 @@
         prep_chunk(c, rate, field, shared, *at, rows, pay)
 
 
-def block_totals(pays, chunks, rows):
-    return [rows[2] * pays[m, 0, chunks : chunks + 1, :] for m in range(pays.shape[0])]
+def by_block(parts, me, index):
+    values = [part[index] for part in parts]
+    ordered = []
+    for m in range(len(values)):
+        value = values[0]
+        for j in range(1, len(values)):
+            value = jnp.where(me == m ^ j, values[j], value)
+        ordered.append(value)
+    return ordered
+
+
+def block_totals(pay, me, chunks, rows):
+    return [rows[2] * whole for whole in by_block(pay, me, (0, slice(chunks, chunks + 1)))]
 
 
 def step_size(stats):
@@ -221,7 +232,7 @@
             new3[0][c - RIM] = field
         chunk(z3, c)[...] = z
         last = chunk(p3, c)[frames - 1 : frames, :]
-        pay[c : c + 1, :] = last * z[frames - 1 : frames, :]
+        pay[0, c : c + 1, :] = last * z[frames - 1 : frames, :]
 
 
 def final_kernel(s3, g3, stats, out, here, sems):
@@ -309,10 +320,11 @@
     stripe = pattern.shape[1]
     edge = 2 * HB
     me = lax.axis_index("tm")
-    totals = block_totals(pay, chunks, rows)
+    totals = block_totals(pay, me, chunks, rows)
+    ends = by_block(pays, me, 0)
     carry = jnp.zeros_like(totals[0])
-    for m in range(pays.shape[0]):
-        carry = jnp.where(m < me, pays[m] + totals[m] * carry, carry)
+    for m, end in enumerate(ends):
+        carry = jnp.where(m < me, end + totals[m] * carry, carry)
     carry = carry * rows[1]
     ranges = ((0, edge), (stripe - edge, stripe))
     for start, stop in ranges:
@@ -415,17 +427,20 @@
     own = chunks - 2 * RIM
     stripe = pattern.shape[1]
     me = lax.axis_index("tm")
-    totals = block_totals(pay, chunks, rows)
-    blocks = pays.shape[0]
+    totals = block_totals(pay, me, chunks, rows)
+    gains = by_block(pay, me, 1)
+    starts = by_block(pays, me, 0)
+    ends = by_block(pays, me, 1)
+    blocks = len(pays)
     entering = [None] * blocks
     state = jnp.zeros_like(totals[0])
     for m in reversed(range(blocks)):
         entering[m] = state
-        state = pays[m, 0] + totals[m] * state
+        state = starts[m] + totals[m] * state
     carry = jnp.zeros_like(totals[0])
     adjoint = jnp.zeros_like(totals[0])
     for m in range(blocks):
-        end = pays[m, 1] + pay[m, 1] * entering[m]
+        end = ends[m] + gains[m] * entering[m]
         carry = jnp.where(m < me, end + totals[m] * carry, carry)
         adjoint = jnp.where(m == me, entering[m], adjoint)
     carry = carry * rows[1]
@@ -518,6 +533,16 @@
         return both + [(j, i) for i, j in both]
 
     return lax.ppermute(first, "tile", pairs(0)), lax.ppermute(second, "tile", pairs(1))
+
+
+def shared_blocks(value):
+    size = lax.axis_size("tm")
+    known = [value]
+    bit = 1
+    while bit < size:
+        known += [lax.ppermute(x, "tm", [(i, i ^ bit) for i in range(size)]) for x in known]
+        bit *= 2
+    return tuple(known)
 
 
 def per_device(recording, footprints, pattern, decay, frame_gain, spikes):
@@ -564,8 +589,7 @@
         (first, second, columns, rows, pay),
     )
     s3, p3, pinv3, z3 = zip(owns, rims)
-    constants = lax.all_gather(pay, "tm")
-    pays = constants[:, 0]
+    constants = pays = shared_blocks(pay)
     scratch = [
         pltpu.VMEM((stripe * K * NEU_BLOCK, frames), F32),
         pltpu.SMEM((stripe, 2 * HB + 1), jnp.int32),
@@ -614,7 +638,7 @@
             (zones, got_a, got_b, p3, pinv3, rows, pay),
             keep=held,
         )
-        pays = lax.all_gather(pay, "tm")
+        pays = shared_blocks(pay)
         g3, stats = call(
             direction_kernel,
             "direction",
@@ -643,10 +667,10 @@
             update_kernel,
             "update",
             0.6,
-            (split if iteration < ITERS - 2 else split[:1], split, f32(lines, LANES)),
+            (split if iteration < ITERS - 2 else split[:1], split, f32(1, lines, LANES)),
             (s3, g3, stats, p3, pinv3, rows),
         )
-        pays = lax.all_gather(pay, "tm")
+        pays = shared_blocks(pay)
 
 
 def solution(mesh):

time: 81.9 us -> 81.2 us (level)
  blocking collectives: 47.2 us -> 26 us
  waiting for transfers between devices: 0.02 us -> 11.7 us
  starting transfers between devices: 9.97 us -> 18.8 us
    all_gather x4 -> x0, blocking collectives: 21.2 us -> none  [the longest x3 15.9 us: per_device(): pays = lax.all_gather(pay, 'tm')]
    ppermute x0 -> x12, waiting for transfers between devices: none -> 11.7 us  [shared_blocks(): lax.ppermute(x, 'tm', [(i, i ^ bit) for i in range(size)])]
    ppermute x0 -> x12, starting transfers between devices: none -> 8.84 us  [shared_blocks(): lax.ppermute(x, 'tm', [(i, i ^ bit) for i in range(size)])]
  transfers between devices with their start and end apart: 6 -> 18, of which waited for: 0 -> 10; matrix products, arithmetic and copies ran while one was open for 0% -> 0% of each run, Pallas kernels for 10% -> 10%
where the time goes in v3:
time: 81.2 us; the launch traced here: 80.9 us
  blocking collectives  26 us (32%)
  Pallas kernels  20.8 us (26%)
  starting transfers between devices  18.8 us (23%)
  waiting for transfers between devices  11.7 us (14%)
  local copies, waits for them, and re-layouts  2.58 us (3%)
  between operations  1.01 us (1%)
    all_to_all x2, blocking collectives, per_device(): stats = lax.all_to_all(stats, ('tile', 'tm'), 0, 0)  26 us
    pallas_call x13, Pallas kernels, call(): pl.pallas_call(body, name=name, out_shape=outs, in_specs=in_specs, out_sp...  20.8 us
    ppermute x12, waiting for transfers between devices, shared_blocks(): lax.ppermute(x, 'tm', [(i, i ^ bit) for i in range(size)])  11.7 us
    ppermute x12, starting transfers between devices, shared_blocks(): lax.ppermute(x, 'tm', [(i, i ^ bit) for i in range(size)])  8.84 us
    ppermute x3, starting transfers between devices, swapped(): lax.ppermute(first, 'tile', pairs(0))  8.01 us
    unnamed x12, local copies, waits for them, and re-layouts  2.58 us
    ppermute x3, starting transfers between devices, swapped(): lax.ppermute(second, 'tile', pairs(1))  1.96 us
  transfers between devices with their start and end apart: 18, of which 10 were waited for; matrix products, arithmetic and copies ran while one was open for 0% of the time, Pallas kernels for 10%

profile of v3, /device:TPU:0, one launch (start us, length us, event | category | flops | bytes accessed | tf_op | source)
XLA Modules:
  0.0 80.9 jit_solution(6998255052905950869)
XLA Ops:
  0.6 0.0 copy-start.4
  0.6 0.7 copy-done.4
  1.3 0.9 %rims.1 = (f32[136,128]{1,0:T(8,128)S(1)}, f32[136,128]{1,0:T(8,128)S(1)}, f32[16,128]{1,0:T(8,128)S(1)}) custom-call(f32[2048,128]{1,0:T(8,128)} %refs_0_.3, f32[16,128]{1,0:T(8,128)S(1)} %bitcast.9), custom_call_target="tpu_custom_call" | custom-call | flops 100000000 | bytes 3000000 | tf_op jit(solution)/shard_map/rims/pallas_call | solution.py:511
  2.2 3.0 %collective-permute-start = (f32[136,128]{1,0:T(8,128)S(1)}, f32[136,128]{1,0:T(8,128)S(1)}, u32[]{:S(2)}, u32[]{:S(2)}) collective-permute-start(f32[136,128]{1,0:T(8,128)S(1)} %get-tuple-element.49), channel_id=1, source_target_pairs={{0,1},{2,3},{4,5},{6,7},{1,0},{3,2},{5,4},{7,6},{8,9},{10,11},{12,... | collective-permute-start | bytes 208904 | tf_op jit(solution)/shard_map/ppermute | solution.py:535
  5.3 0.7 collective-permute-start.1
  5.9 0.0 copy-start.2
  5.9 1.2 %copy-done.2 = f32[2048,128]{1,0:T(8,128)S(1)} copy-done((f32[2048,128]{1,0:T(8,128)S(1)}, f32[2048,128]{1,0:T(8,128)}, u32[]{:S(2)}) %copy-start.2) | copy-done | bytes 1048600
  7.2 0.0 copy-start.5
  7.2 0.7 copy-done.5
  7.8 0.0 copy-start.1
  7.8 0.0 copy-start.3
  7.8 1.4 %prep_own.1 = (f32[16,128,128]{2,1,0:T(8,128)S(1)}, f32[16,128,128]{2,1,0:T(8,128)S(1)}, f32[16,128,128]{2,1,0:T(8,128)S(1)}, f32[16,128,128]{2,1,0:T(8,128)S(1)...) custom-call(f32[2048,128]{1,0:T(8,128)S(1)} %copy-done.2, ...), custom_call_target="tpu_custom_call" | custom-call | flops 160000000 | bytes 4800000 | tf_op jit(solution)/shard_map/prep_own/pallas_call | solution.py:511
  9.3 0.0 collective-permute-done.refs_0_
  9.3 0.0 collective-permute-done.1.refs_1_
  9.3 0.3 prep_rim.1
  9.6 0.1 collective-permute-start.2
  9.6 1.6 %collective-permute-start.3 = (f32[2,24,128]{2,1,0:T(8,128)S(1)}, f32[2,24,128]{2,1,0:T(8,128)S(1)}, u32[]{:S(2)}, u32[]{:S(2)}) collective-permute-start(f32[2,24,128]{2,1,0:T(8,128)S(1)} %get-tuple-element.62.refs_4__0_.refs_5__0_.refs_6__0_), channel_id=1, source_target_pairs={{0,16},{8,24},{16,0},{24,8},{1,17},{9,25},{17,1},{25,9},{2,18},{10... | collective-permute-start | bytes 73736 | tf_op jit(solution)/shard_map/ppermute | solution.py:543
  11.2 0.0 collective-permute-done.2.refs_4__1_.refs_5__1_.refs_6__1_
  11.2 1.1 %collective-permute-start.4 = (f32[2,24,128]{2,1,0:T(8,128)S(1)}, f32[2,24,128]{2,1,0:T(8,128)S(1)}, u32[]{:S(2)}, u32[]{:S(2)}) collective-permute-start(f32[2,24,128]{2,1,0:T(8,128)S(1)} %collective-permute-done.2.refs_4__1_.refs_5__1_.refs_6__1_), channel_id=1, source_target_pairs={{0,16},{8,24},{16,0},{24,8},{1,17},{9,25},{17,1},{25,9},{2,18},{10... | collective-permute-start | bytes 73736 | tf_op jit(solution)/shard_map/ppermute | solution.py:543
  12.3 1.2 %collective-permute-done.3.refs_4__2_.refs_5__2_.refs_6__2_ = f32[2,24,128]{2,1,0:T(8,128)S(1)} collective-permute-done((f32[2,24,128]{2,1,0:T(8,128)S(1)}, f32[2,24,128]{2,1,0:T(8,128)S(1)}, u32[]{:S(2)}, u32[]{:S(2)}) %collective-permute-start.3) | collective-permute-done | bytes 24608 | tf_op jit(solution)/shard_map/ppermute | solution.py:543
  13.5 1.5 %collective-permute-done.4.refs_4__3_.refs_5__3_.refs_6__3_ = f32[2,24,128]{2,1,0:T(8,128)S(1)} collective-permute-done((f32[2,24,128]{2,1,0:T(8,128)S(1)}, f32[2,24,128]{2,1,0:T(8,128)S(1)}, u32[]{:S(2)}, u32[]{:S(2)}) %collective-permute-start.4) | collective-permute-done | bytes 24608 | tf_op jit(solution)/shard_map/ppermute | solution.py:543
  15.0 0.0 copy-done.1
  15.0 0.0 copy-done.3
  15.0 0.0 copy-start
  15.0 1.8 %edge.2 = (bf16[2304,128]{1,0:T(8,128)(2,1)S(1)}, f32[4,128,128]{2,1,0:T(8,128)S(1)}, f32[4,128,128]{2,1,0:T(8,128)S(1)}, bf16[2,128,128]{2,1,0:T(8,128)(2,1)S(1)}, bf16[2,128,128]{2,1,0:T(8,128)(2,1)S(1)}) custom-call(s32[4,32]{1,0:T(4,128)S(1)} %bitcast.3, f32[16,128,128]{2,1,0:T(8,128)S(1)} %get-tuple-element.60.refs_1__0_, ...), custom_call_target="tpu_custom_call" | custom-call | flops 250000000 | bytes 7500000 | tf_op jit(solution)/shard_map/edge/pallas_call | solution.py:511
  16.9 4.3 %collective-permute-start.5 = (bf16[2,128,128]{2,1,0:T(8,128)(2,1)S(1)}, bf16[2,128,128]{2,1,0:T(8,128)(2,1)S(1)}, u32[]{:S(2)}, u32[]{:S(2)}) collective-permute-start(bf16[2,128,128]{2,1,0:T(8,128)(2,1)S(1)} %get-tuple-element.68), channel_id=1, source_target_pairs={{0,1},{2,3},{4,5},{6,7},{1,0},{3,2},{5,4},{7,6},{8,9},{10,11},{12,... | collective-permute-start | bytes 196616 | tf_op jit(solution)/shard_map/ppermute | solution.py:535
  21.2 0.7 collective-permute-start.6
  21.9 0.0 copy-done
  21.9 3.3 %inner.2 = (f32[14,128,128]{2,1,0:T(8,128)S(1)}, f32[2,24,128]{2,1,0:T(8,128)S(1)}) custom-call(s32[4,32]{1,0:T(4,128)S(1)} %bitcast.4, f32[16,128,128]{2,1,0:T(8,128)S(1)} %get-tuple-element.55.refs_2__0_.refs_1__0_.refs_3__0_, f32[2,128,128]{2,1,0:T(8,128)S(1)} %get-tuple-element.56.refs_2__1_.refs_1__1_.refs_3__1_, ...), custom_call_target="tpu_custom_call" | custom-call | flops 400000000 | bytes 12000000 | tf_op jit(solution)/shard_map/inner/pallas_call | solution.py:511
  25.2 0.0 collective-permute-done.5.refs_1_
  25.2 0.0 collective-permute-done.6.refs_2_
  25.2 0.3 border.2
  25.5 0.1 collective-permute-start.7
  25.6 1.2 %collective-permute-start.8 = (f32[2,24,128]{2,1,0:T(8,128)S(1)}, f32[2,24,128]{2,1,0:T(8,128)S(1)}, u32[]{:S(2)}, u32[]{:S(2)}) collective-permute-start(f32[2,24,128]{2,1,0:T(8,128)S(1)} %get-tuple-element.72.refs_7__0_), channel_id=1, source_target_pairs={{0,16},{8,24},{16,0},{24,8},{1,17},{9,25},{17,1},{25,9},{2,18},{10... | collective-permute-start | bytes 73736 | tf_op jit(solution)/shard_map/ppermute | solution.py:543
  26.7 0.0 collective-permute-done.7.refs_7__1_
  26.8 1.1 %collective-permute-start.9 = (f32[2,24,128]{2,1,0:T(8,128)S(1)}, f32[2,24,128]{2,1,0:T(8,128)S(1)}, u32[]{:S(2)}, u32[]{:S(2)}) collective-permute-start(f32[2,24,128]{2,1,0:T(8,128)S(1)} %collective-permute-done.7.refs_7__1_), channel_id=1, source_target_pairs={{0,16},{8,24},{16,0},{24,8},{1,17},{9,25},{17,1},{25,9},{2,18},{10... | collective-permute-start | bytes 73736 | tf_op jit(solution)/shard_map/ppermute | solution.py:543
  27.9 1.6 %collective-permute-done.8.refs_7__2_ = f32[2,24,128]{2,1,0:T(8,128)S(1)} collective-permute-done((f32[2,24,128]{2,1,0:T(8,128)S(1)}, f32[2,24,128]{2,1,0:T(8,128)S(1)}, u32[]{:S(2)}, u32[]{:S(2)}) %collective-permute-start.8) | collective-permute-done | bytes 24608 | tf_op jit(solution)/shard_map/ppermute | solution.py:543
  29.5 1.1 %collective-permute-done.9.refs_7__3_ = f32[2,24,128]{2,1,0:T(8,128)S(1)} collective-permute-done((f32[2,24,128]{2,1,0:T(8,128)S(1)}, f32[2,24,128]{2,1,0:T(8,128)S(1)}, u32[]{:S(2)}, u32[]{:S(2)}) %collective-permute-start.9) | collective-permute-done | bytes 24608 | tf_op jit(solution)/shard_map/ppermute | solution.py:543
  30.6 2.5 %direction.2 = (f32[18,128,128]{2,1,0:T(8,128)S(1)}, f32[32,2,128]{2,1,0:T(2,128)S(1)}) custom-call(s32[4,32]{1,0:T(4,128)S(1)} %bitcast.5, f32[14,128,128]{2,1,0:T(8,128)S(1)} %get-tuple-element.66.refs_1_, f32[4,128,128]{2,1,0:T(8,128)S(1)} %get-tuple-element.71.refs_2_, f32[16,128,128]{2,1,0:T(8,128)S(1)} %get-tuple-element.55.refs_2__0_.refs_1__0_.refs_3__0_, ...), custom_call_target="tpu_custom_call" | custom-call | flops 400000000 | bytes 12000000 | tf_op jit(solution)/shard_map/direction/pallas_call | solution.py:511
  33.1 13.9 %all_to_all.10.refs_2_ = f32[32,2,128]{2,1,0:T(2,128)S(1)} all-to-all(f32[32,2,128]{2,1,0:T(2,128)S(1)} %get-tuple-element.74), channel_id=1, replica_groups=mesh['tm'=4,'tile'=8] {'tile','tm'}, dimensions={0} | all-to-all | bytes 65536 | tf_op jit(solution)/shard_map/all_to_all | solution.py:654
  47.0 0.7 update.1
  47.7 0.2 collective-permute-start.10
  47.9 0.5 collective-permute-start.11
  48.4 0.5 collective-permute-done.10.refs_5__1_
  49.0 1.0 %collective-permute-start.12 = (f32[1,24,128]{2,1,0:T(8,128)S(1)}, f32[1,24,128]{2,1,0:T(8,128)S(1)}, u32[]{:S(2)}, u32[]{:S(2)}) collective-permute-start(f32[1,24,128]{2,1,0:T(8,128)S(1)} %collective-permute-done.10.refs_5__1_), channel_id=1, source_target_pairs={{0,16},{8,24},{16,0},{24,8},{1,17},{9,25},{17,1},{25,9},{2,18},{10... | collective-permute-start | bytes 36872 | tf_op jit(solution)/shard_map/ppermute | solution.py:543
  50.0 1.7 %collective-permute-done.11.refs_5__2_ = f32[1,24,128]{2,1,0:T(8,128)S(1)} collective-permute-done((f32[1,24,128]{2,1,0:T(8,128)S(1)}, f32[1,24,128]{2,1,0:T(8,128)S(1)}, u32[]{:S(2)}, u32[]{:S(2)}) %collective-permute-start.11) | collective-permute-done | bytes 12320 | tf_op jit(solution)/shard_map/ppermute | solution.py:543
  51.6 1.0 %collective-permute-done.12.refs_5__3_ = f32[1,24,128]{2,1,0:T(8,128)S(1)} collective-permute-done((f32[1,24,128]{2,1,0:T(8,128)S(1)}, f32[1,24,128]{2,1,0:T(8,128)S(1)}, u32[]{:S(2)}, u32[]{:S(2)}) %collective-permute-start.12) | collective-permute-done | bytes 12320 | tf_op jit(solution)/shard_map/ppermute | solution.py:543
  52.6 1.9 %edge.3 = (bf16[2304,128]{1,0:T(8,128)(2,1)S(1)}, f32[4,128,128]{2,1,0:T(8,128)S(1)}, f32[4,128,128]{2,1,0:T(8,128)S(1)}, bf16[2,128,128]{2,1,0:T(8,128)(2,1)S(1...) custom-call(s32[4,32]{1,0:T(4,128)S(1)} %bitcast.6, f32[16,128,128]{2,1,0:T(8,128)S(1)} %get-tuple-element.76.refs_1__0_, ...), custom_call_target="tpu_custom_call" | custom-call | flops 250000000 | bytes 7500000 | tf_op jit(solution)/shard_map/edge/pallas_call | solution.py:511
  54.6 0.6 collective-permute-start.13
  55.2 0.7 collective-permute-start.14
  55.8 3.5 %inner.3 = (f32[14,128,128]{2,1,0:T(8,128)S(1)}, f32[2,24,128]{2,1,0:T(8,128)S(1)}, f32[2048,128]{1,0:T(8,128)}) custom-call(s32[4,32]{1,0:T(4,128)S(1)} %bitcast.7, f32[16,128,128]{2,1,0:T(8,128)S(1)} %get-tuple-element.55.refs_2__0_.refs_1__0_.refs_3__0_, f32[2,128,128]{2,1,0:T(8,128)S(1)} %get-tuple-element.56.refs_2__1_.refs_1__1_.refs_3__1_, ...), custom_call_target="tpu_custom_call" | custom-call | flops 400000000 | bytes 12000000 | tf_op jit(solution)/shard_map/inner/pallas_call | solution.py:511
  59.4 0.0 collective-permute-done.13.refs_1_
  59.4 0.0 collective-permute-done.14.refs_2_
  59.4 0.3 border.3
  59.7 0.1 collective-permute-start.15
  59.8 1.0 %collective-permute-start.16 = (f32[2,24,128]{2,1,0:T(8,128)S(1)}, f32[2,24,128]{2,1,0:T(8,128)S(1)}, u32[]{:S(2)}, u32[]{:S(2)}) collective-permute-start(f32[2,24,128]{2,1,0:T(8,128)S(1)} %get-tuple-element.88.refs_7__0_), channel_id=1, source_target_pairs={{0,16},{8,24},{16,0},{24,8},{1,17},{9,25},{17,1},{25,9},{2,18},{10... | collective-permute-start | bytes 73736 | tf_op jit(solution)/shard_map/ppermute | solution.py:543
  60.8 0.2 collective-permute-done.15.refs_7__1_
  60.9 0.9 %collective-permute-start.17 = (f32[2,24,128]{2,1,0:T(8,128)S(1)}, f32[2,24,128]{2,1,0:T(8,128)S(1)}, u32[]{:S(2)}, u32[]{:S(2)}) collective-permute-start(f32[2,24,128]{2,1,0:T(8,128)S(1)} %collective-permute-done.15.refs_7__1_), channel_id=1, source_target_pairs={{0,16},{8,24},{16,0},{24,8},{1,17},{9,25},{17,1},{25,9},{2,18},{10... | collective-permute-start | bytes 73736 | tf_op jit(solution)/shard_map/ppermute | solution.py:543
  61.9 1.8 %collective-permute-done.16.refs_7__2_ = f32[2,24,128]{2,1,0:T(8,128)S(1)} collective-permute-done((f32[2,24,128]{2,1,0:T(8,128)S(1)}, f32[2,24,128]{2,1,0:T(8,128)S(1)}, u32[]{:S(2)}, u32[]{:S(2)}) %collective-permute-start.16) | collective-permute-done | bytes 24608 | tf_op jit(solution)/shard_map/ppermute | solution.py:543
  63.7 1.1 %collective-permute-done.17.refs_7__3_ = f32[2,24,128]{2,1,0:T(8,128)S(1)} collective-permute-done((f32[2,24,128]{2,1,0:T(8,128)S(1)}, f32[2,24,128]{2,1,0:T(8,128)S(1)}, u32[]{:S(2)}, u32[]{:S(2)}) %collective-permute-start.17) | collective-permute-done | bytes 24608 | tf_op jit(solution)/shard_map/ppermute | solution.py:543
  64.8 2.5 %direction.3 = (f32[18,128,128]{2,1,0:T(8,128)S(1)}, f32[32,2,128]{2,1,0:T(2,128)S(1)}) custom-call(s32[4,32]{1,0:T(4,128)S(1)} %bitcast.8, f32[14,128,128]{2,1,0:T(8,128)S(1)} %get-tuple-element.82.refs_1_, f32[4,128,128]{2,1,0:T(8,128)S(1)} %get-tuple-element.87.refs_2_, f32[16,128,128]{2,1,0:T(8,128)S(1)} %get-tuple-element.55.refs_2__0_.refs_1__0_.refs_3__0_, ...), custom_call_target="tpu_custom_call" | custom-call | flops 400000000 | bytes 12000000 | tf_op jit(solution)/shard_map/direction/pallas_call | solution.py:511
  67.3 12.1 %all_to_all.11.refs_2_ = f32[32,2,128]{2,1,0:T(2,128)S(1)} all-to-all(f32[32,2,128]{2,1,0:T(2,128)S(1)} %get-tuple-element.90), channel_id=1, replica_groups=mesh['tm'=4,'tile'=8] {'tile','tm'}, dimensions={0} | all-to-all | bytes 65536 | tf_op jit(solution)/shard_map/all_to_all | solution.py:654
  79.5 1.3 %final.1 = f32[2048,128]{1,0:T(8,128)} custom-call(f32[16,128,128]{2,1,0:T(8,128)S(1)} %get-tuple-element.75.refs_8__0_.refs_9__0_.refs_7__0_.refs_0_, f32[18,128,128]{2,1,0:T(8,128)S(1)} %get-tuple-element.89.refs_1_, f32[32,2,128]{2,1,0:T(2,128)S(1)} %all_to_all.11.refs_2_), custom_call_target="tpu_custom_call" | custom-call | flops 140000000 | bytes 4200000 | tf_op jit(solution)/shard_map/final/pallas_call | solution.py:511
Async XLA Ops:
  0.6 0.7 copy-start.4
  2.2 7.0 %collective-permute-start = (f32[136,128]{1,0:T(8,128)S(1)}, f32[136,128]{1,0:T(8,128)S(1)}, u32[]{:S(2)}, u32[]{:S(2)}) collective-permute-start(f32[136,128]{1,0:T(8,128)S(1)} %get-tuple-element.49), channel_id=1, source_target_pairs={{0,1},{2,3},{4,5},{6,7},{1,0},{3,2},{5,4},{7,6},{8,9},{10,11},{12,... | collective-permute-start | bytes 208904 | tf_op jit(solution)/shard_map/ppermute | solution.py:535
  5.3 4.0 %collective-permute-start.1 = (f32[136,128]{1,0:T(8,128)S(1)}, f32[136,128]{1,0:T(8,128)S(1)}, u32[]{:S(2)}, u32[]{:S(2)}) collective-permute-start(f32[136,128]{1,0:T(8,128)S(1)} %get-tuple-element.50), channel_id=1, source_target_pairs={{1,2},{3,4},{5,6},{2,1},{4,3},{6,5},{9,10},{11,12},{13,14},{10,9},... | collective-permute-start | bytes 208904 | tf_op jit(solution)/shard_map/ppermute | solution.py:535
  5.9 1.2 %copy-start.2 = (f32[2048,128]{1,0:T(8,128)S(1)}, f32[2048,128]{1,0:T(8,128)}, u32[]{:S(2)}) copy-start(f32[2048,128]{1,0:T(8,128)} %refs_0_.3) | copy-start | bytes 3145732
  7.2 0.7 copy-start.5
  7.8 7.2 %copy-start.1 = (bf16[8192,128]{1,0:T(8,128)(2,1)S(1)}, bf16[8192,128]{1,0:T(8,128)(2,1)}, u32[]{:S(2)}) copy-start(bf16[8192,128]{1,0:T(8,128)(2,1)} %refs_7_.7) | copy-start | bytes 6291460
  7.8 7.2 %copy-start.3 = (s32[32,4]{0,1:T(4,128)S(1)}, s32[32,4]{0,1:T(4,128)}, u32[]{:S(2)}) copy-start(s32[32,4]{0,1:T(4,128)} %param.8) | copy-start | bytes 1540
  9.6 1.6 %collective-permute-start.2 = (f32[2,24,128]{2,1,0:T(8,128)S(1)}, f32[2,24,128]{2,1,0:T(8,128)S(1)}, u32[]{:S(2)}, u32[]{:S(2)}) collective-permute-start(f32[2,24,128]{2,1,0:T(8,128)S(1)} %get-tuple-element.62.refs_4__0_.refs_5__0_.refs_6__0_), channel_id=1, source_target_pairs={{0,8},{8,0},{16,24},{24,16},{1,9},{9,1},{17,25},{25,17},{2,10},{10... | collective-permute-start | bytes 73736 | tf_op jit(solution)/shard_map/ppermute | solution.py:543
  9.6 3.9 %collective-permute-start.3 = (f32[2,24,128]{2,1,0:T(8,128)S(1)}, f32[2,24,128]{2,1,0:T(8,128)S(1)}, u32[]{:S(2)}, u32[]{:S(2)}) collective-permute-start(f32[2,24,128]{2,1,0:T(8,128)S(1)} %get-tuple-element.62.refs_4__0_.refs_5__0_.refs_6__0_), channel_id=1, source_target_pairs={{0,16},{8,24},{16,0},{24,8},{1,17},{9,25},{17,1},{25,9},{2,18},{10... | collective-permute-start | bytes 73736 | tf_op jit(solution)/shard_map/ppermute | solution.py:543
  11.2 3.8 %collective-permute-start.4 = (f32[2,24,128]{2,1,0:T(8,128)S(1)}, f32[2,24,128]{2,1,0:T(8,128)S(1)}, u32[]{:S(2)}, u32[]{:S(2)}) collective-permute-start(f32[2,24,128]{2,1,0:T(8,128)S(1)} %collective-permute-done.2.refs_4__1_.refs_5__1_.refs_6__1_), channel_id=1, source_target_pairs={{0,16},{8,24},{16,0},{24,8},{1,17},{9,25},{17,1},{25,9},{2,18},{10... | collective-permute-start | bytes 73736 | tf_op jit(solution)/shard_map/ppermute | solution.py:543
  15.0 6.9 %copy-start = (bf16[8192,256]{1,0:T(8,128)(2,1)S(1)}, bf16[8192,256]{1,0:T(8,128)(2,1)}, u32[]{:S(2)}) copy-start(bf16[8192,256]{1,0:T(8,128)(2,1)} %refs_8_.3) | copy-start | bytes 12582916
  16.9 8.3 %collective-permute-start.5 = (bf16[2,128,128]{2,1,0:T(8,128)(2,1)S(1)}, bf16[2,128,128]{2,1,0:T(8,128)(2,1)S(1)}, u32[]{:S(2)}, u32[]{:S(2)}) collective-permute-start(bf16[2,128,128]{2,1,0:T(8,128)(2,1)S(1)} %get-tuple-element.68), channel_id=1, source_target_pairs={{0,1},{2,3},{4,5},{6,7},{1,0},{3,2},{5,4},{7,6},{8,9},{10,11},{12,... | collective-permute-start | bytes 196616 | tf_op jit(solution)/shard_map/ppermute | solution.py:535
  21.2 4.0 %collective-permute-start.6 = (bf16[2,128,128]{2,1,0:T(8,128)(2,1)S(1)}, bf16[2,128,128]{2,1,0:T(8,128)(2,1)S(1)}, u32[]{:S(2)}, u32[]{:S(2)}) collective-permute-start(bf16[2,128,128]{2,1,0:T(8,128)(2,1)S(1)} %get-tuple-element.69), channel_id=1, source_target_pairs={{1,2},{3,4},{5,6},{2,1},{4,3},{6,5},{9,10},{11,12},{13,14},{10,9},... | collective-permute-start | bytes 196616 | tf_op jit(solution)/shard_map/ppermute | solution.py:535
  25.5 1.3 %collective-permute-start.7 = (f32[2,24,128]{2,1,0:T(8,128)S(1)}, f32[2,24,128]{2,1,0:T(8,128)S(1)}, u32[]{:S(2)}, u32[]{:S(2)}) collective-permute-start(f32[2,24,128]{2,1,0:T(8,128)S(1)} %get-tuple-element.72.refs_7__0_), channel_id=1, source_target_pairs={{0,8},{8,0},{16,24},{24,16},{1,9},{9,1},{17,25},{25,17},{2,10},{10... | collective-permute-start | bytes 73736 | tf_op jit(solution)/shard_map/ppermute | solution.py:543
  25.6 3.9 %collective-permute-start.8 = (f32[2,24,128]{2,1,0:T(8,128)S(1)}, f32[2,24,128]{2,1,0:T(8,128)S(1)}, u32[]{:S(2)}, u32[]{:S(2)}) collective-permute-start(f32[2,24,128]{2,1,0:T(8,128)S(1)} %get-tuple-element.72.refs_7__0_), channel_id=1, source_target_pairs={{0,16},{8,24},{16,0},{24,8},{1,17},{9,25},{17,1},{25,9},{2,18},{10... | collective-permute-start | bytes 73736 | tf_op jit(solution)/shard_map/ppermute | solution.py:543
  26.8 3.8 %collective-permute-start.9 = (f32[2,24,128]{2,1,0:T(8,128)S(1)}, f32[2,24,128]{2,1,0:T(8,128)S(1)}, u32[]{:S(2)}, u32[]{:S(2)}) collective-permute-start(f32[2,24,128]{2,1,0:T(8,128)S(1)} %collective-permute-done.7.refs_7__1_), channel_id=1, source_target_pairs={{0,16},{8,24},{16,0},{24,8},{1,17},{9,25},{17,1},{25,9},{2,18},{10... | collective-permute-start | bytes 73736 | tf_op jit(solution)/shard_map/ppermute | solution.py:543
  47.7 1.2 %collective-permute-start.10 = (f32[1,24,128]{2,1,0:T(8,128)S(1)}, f32[1,24,128]{2,1,0:T(8,128)S(1)}, u32[]{:S(2)}, u32[]{:S(2)}) collective-permute-start(f32[1,24,128]{2,1,0:T(8,128)S(1)} %get-tuple-element.78.refs_5__0_), channel_id=1, source_target_pairs={{0,8},{8,0},{16,24},{24,16},{1,9},{9,1},{17,25},{25,17},{2,10},{10... | collective-permute-start | bytes 36872 | tf_op jit(solution)/shard_map/ppermute | solution.py:543
  47.9 3.7 %collective-permute-start.11 = (f32[1,24,128]{2,1,0:T(8,128)S(1)}, f32[1,24,128]{2,1,0:T(8,128)S(1)}, u32[]{:S(2)}, u32[]{:S(2)}) collective-permute-start(f32[1,24,128]{2,1,0:T(8,128)S(1)} %get-tuple-element.78.refs_5__0_), channel_id=1, source_target_pairs={{0,16},{8,24},{16,0},{24,8},{1,17},{9,25},{17,1},{25,9},{2,18},{10... | collective-permute-start | bytes 36872 | tf_op jit(solution)/shard_map/ppermute | solution.py:543
  49.0 3.7 %collective-permute-start.12 = (f32[1,24,128]{2,1,0:T(8,128)S(1)}, f32[1,24,128]{2,1,0:T(8,128)S(1)}, u32[]{:S(2)}, u32[]{:S(2)}) collective-permute-start(f32[1,24,128]{2,1,0:T(8,128)S(1)} %collective-permute-done.10.refs_5__1_), channel_id=1, source_target_pairs={{0,16},{8,24},{16,0},{24,8},{1,17},{9,25},{17,1},{25,9},{2,18},{10... | collective-permute-start | bytes 36872 | tf_op jit(solution)/shard_map/ppermute | solution.py:543
  54.6 4.8 %collective-permute-start.13 = (bf16[2,128,128]{2,1,0:T(8,128)(2,1)S(1)}, bf16[2,128,128]{2,1,0:T(8,128)(2,1)S(1)}, u32[]{:S(2)}, u32[]{:S(2)}) collective-permute-start(bf16[2,128,128]{2,1,0:T(8,128)(2,1)S(1)} %get-tuple-element.84), channel_id=1, source_target_pairs={{0,1},{2,3},{4,5},{6,7},{1,0},{3,2},{5,4},{7,6},{8,9},{10,11},{12,... | collective-permute-start | bytes 196616 | tf_op jit(solution)/shard_map/ppermute | solution.py:535
  55.2 4.2 %collective-permute-start.14 = (bf16[2,128,128]{2,1,0:T(8,128)(2,1)S(1)}, bf16[2,128,128]{2,1,0:T(8,128)(2,1)S(1)}, u32[]{:S(2)}, u32[]{:S(2)}) collective-permute-start(bf16[2,128,128]{2,1,0:T(8,128)(2,1)S(1)} %get-tuple-element.85), channel_id=1, source_target_pairs={{1,2},{3,4},{5,6},{2,1},{4,3},{6,5},{9,10},{11,12},{13,14},{10,9},... | collective-permute-start | bytes 196616 | tf_op jit(solution)/shard_map/ppermute | solution.py:535
  59.7 1.3 %collective-permute-start.15 = (f32[2,24,128]{2,1,0:T(8,128)S(1)}, f32[2,24,128]{2,1,0:T(8,128)S(1)}, u32[]{:S(2)}, u32[]{:S(2)}) collective-permute-start(f32[2,24,128]{2,1,0:T(8,128)S(1)} %get-tuple-element.88.refs_7__0_), channel_id=1, source_target_pairs={{0,8},{8,0},{16,24},{24,16},{1,9},{9,1},{17,25},{25,17},{2,10},{10... | collective-permute-start | bytes 73736 | tf_op jit(solution)/shard_map/ppermute | solution.py:543
  59.8 3.9 %collective-permute-start.16 = (f32[2,24,128]{2,1,0:T(8,128)S(1)}, f32[2,24,128]{2,1,0:T(8,128)S(1)}, u32[]{:S(2)}, u32[]{:S(2)}) collective-permute-start(f32[2,24,128]{2,1,0:T(8,128)S(1)} %get-tuple-element.88.refs_7__0_), channel_id=1, source_target_pairs={{0,16},{8,24},{16,0},{24,8},{1,17},{9,25},{17,1},{25,9},{2,18},{10... | collective-permute-start | bytes 73736 | tf_op jit(solution)/shard_map/ppermute | solution.py:543
  60.9 3.8 %collective-permute-start.17 = (f32[2,24,128]{2,1,0:T(8,128)S(1)}, f32[2,24,128]{2,1,0:T(8,128)S(1)}, u32[]{:S(2)}, u32[]{:S(2)}) collective-permute-start(f32[2,24,128]{2,1,0:T(8,128)S(1)} %collective-permute-done.15.refs_7__1_), channel_id=1, source_target_pairs={{0,16},{8,24},{16,0},{24,8},{1,17},{9,25},{17,1},{25,9},{2,18},{10... | collective-permute-start | bytes 73736 | tf_op jit(solution)/shard_map/ppermute | solution.py:543

commit v4 on v3

--- a/solution.py
+++ b/solution.py
@@ -17,7 +17,6 @@
 BF16 = jnp.bfloat16
 VMEM = pl.BlockSpec(memory_space=pltpu.VMEM)
 HBM = pl.BlockSpec(memory_space=pltpu.HBM)
-SMEM = pl.BlockSpec(memory_space=pltpu.SMEM)
 
 
 def padded8(rows):
@@ -197,13 +196,22 @@
         prep_chunk(c, rate, field, shared, *at, rows, pay)
 
 
+def distances(size):
+    found = [0]
+    bit = size // 2
+    while bit:
+        found += [other ^ bit for other in found]
+        bit //= 2
+    return found
+
+
 def by_block(parts, me, index):
     values = [part[index] for part in parts]
     ordered = []
     for m in range(len(values)):
         value = values[0]
-        for j in range(1, len(values)):
-            value = jnp.where(me == m ^ j, values[j], value)
+        for distance, other in zip(distances(len(values))[1:], values[1:]):
+            value = jnp.where(me == m ^ distance, other, value)
         ordered.append(value)
     return ordered
 
@@ -313,41 +321,41 @@
 
 
 def edge_kernel(
-    pattern, z3, p3, rows, pay, pays, feet, record, ext, zones, spill, send_a, send_b, *rest
+    pattern_far, z3, p3, rows, pay, pays, feet, record, ext, zones, spill, send_a, send_b, *rest
 ):
-    *traces, contrib, place = rest
+    *traces, contrib, place, pattern, sem = rest
+    fetch = pltpu.make_async_copy(pattern_far, pattern, sem)
+    fetch.start()
     chunks = chunk_count(z3)
     stripe = pattern.shape[1]
     edge = 2 * HB
-    me = lax.axis_index("tm")
-    totals = block_totals(pay, me, chunks, rows)
-    ends = by_block(pays, me, 0)
-    carry = jnp.zeros_like(totals[0])
-    for m, end in enumerate(ends):
-        carry = jnp.where(m < me, end + totals[m] * carry, carry)
-    carry = carry * rows[1]
     ranges = ((0, edge), (stripe - edge, stripe))
+
+    @after_start
+    def _():
+        me = lax.axis_index("tm")
+        totals = block_totals(pay, me, chunks, rows)
+        ends = by_block(pays, me, 0)
+        carry = jnp.zeros_like(totals[0])
+        for m, end in enumerate(ends):
+            carry = jnp.where(m < me, end + totals[m] * carry, carry)
+        carry = carry * rows[1]
+        for c in range(chunks):
+            field = chunk(p3, c)[...] * (chunk(z3, c)[...] + carry[c : c + 1, :])
+            at = slice(c * LANES, (c + 1) * LANES)
+            if traces and RIM <= c < chunks - RIM:
+                field = field.T
+                traces[0][(c - RIM) * LANES : (c - RIM + 1) * LANES, :] = field
+                ext[at, :] = field.astype(BF16)
+            else:
+                ext[at, :] = field.astype(BF16).T
+
+    fetch.wait()
     for start, stop in ranges:
         note_places(pattern, place, start, stop)
-
-    def trace(c):
-        field = chunk(p3, c)[...] * (chunk(z3, c)[...] + carry[c : c + 1, :])
-        at = slice(c * LANES, (c + 1) * LANES)
-        if traces and RIM <= c < chunks - RIM:
-            field = field.T
-            traces[0][(c - RIM) * LANES : (c - RIM + 1) * LANES, :] = field
-            ext[at, :] = field.astype(BF16)
-        else:
-            ext[at, :] = field.astype(BF16).T
-
-    near = 4 * RIM
-    for c in [*range(near), *range(chunks - near, chunks)]:
-        trace(c)
     for start, stop in ranges:
         for q in range(start, stop):
             pull_back(pattern, ext, feet, record, contrib, q)
-    for c in range(near, chunks - near):
-        trace(c)
     even = lax.axis_index("tile") % 2 == 0
     for i in range(2 * RIM):
         below = gathered(contrib, place, i, ranges)
@@ -369,13 +377,14 @@
     pay[1, c : c + 1, :] = ends * jnp.sum(pinv * pinv * r, axis=0, keepdims=True)
 
 
-def inner_kernel(pattern, p3, pinv3, rows, ext, spill, feet, record, traces, r3, pay, *rest):
+def inner_kernel(pattern_far, p3, pinv3, rows, ext, spill, feet, record, traces, r3, pay, *rest):
+    *out, contrib, place, pattern, sem = rest[: 4 + len(traces)]
+    fetch = pltpu.make_async_copy(pattern_far, pattern, sem)
+    fetch.start()
     if traces:
-        out, contrib, place, sem = rest
-        copy = pltpu.make_async_copy(traces[0], out, sem)
+        copy = pltpu.make_async_copy(traces[0], out[0], rest[-1])
         copy.start()
-    else:
-        contrib, place = rest
+    fetch.wait()
 
     def compute():
         chunks = chunk_count(p3)
@@ -421,54 +430,63 @@
 
 
 def direction_kernel(
-    pattern, r_inner, r_border, p3, pinv3, rows, pay, pays, feet, g3, stats, low, high
+    pattern_far, r_inner, r_border, p3, pinv3, rows, pay, pays, feet, g3, stats, low, high, *rest
 ):
+    pattern, sem, grad_sums = rest
+    fetch = pltpu.make_async_copy(pattern_far, pattern, sem)
+    fetch.start()
     chunks, frames = g3.shape[0], g3.shape[1]
     own = chunks - 2 * RIM
     stripe = pattern.shape[1]
-    me = lax.axis_index("tm")
-    totals = block_totals(pay, me, chunks, rows)
-    gains = by_block(pay, me, 1)
-    starts = by_block(pays, me, 0)
-    ends = by_block(pays, me, 1)
-    blocks = len(pays)
-    entering = [None] * blocks
-    state = jnp.zeros_like(totals[0])
-    for m in reversed(range(blocks)):
-        entering[m] = state
-        state = starts[m] + totals[m] * state
-    carry = jnp.zeros_like(totals[0])
-    adjoint = jnp.zeros_like(totals[0])
-    for m in range(blocks):
-        end = ends[m] + gains[m] * entering[m]
-        carry = jnp.where(m < me, end + totals[m] * carry, carry)
-        adjoint = jnp.where(m == me, entering[m], adjoint)
-    carry = carry * rows[1]
-    sums_table = table(frames, False)
-    grad_sq = jnp.zeros((8, LANES), F32)
-    image_sq = jnp.zeros((8, frames), F32)
     per_chunk = LANES // NEU_BLOCK
     low_chunks = low.shape[0] // LANES
     first_high = chunks - high.shape[0] // LANES
-    for c in range(chunks):
-        p = chunk(p3, c)[...]
-        if c < 2 * RIM:
-            r = r_border[c]
-        elif c >= chunks - 2 * RIM:
-            r = r_border[c - chunks + 4 * RIM]
-        else:
-            r = r_inner[c - 2 * RIM]
-        scale = rows[0, c : c + 1, :] * chunk(pinv3, c)[...]
-        gradient = scale * (r + p[frames - 1 : frames, :] * adjoint[c : c + 1, :])
-        g3[c] = gradient
-        if RIM <= c < RIM + own:
-            grad_sq += jnp.sum((gradient * gradient).reshape(frames // 8, 8, LANES), axis=0)
-        z = summed(sums_table, scale * gradient)
-        field = (p * (z + carry[c : c + 1, :])).astype(BF16).T
-        if c < low_chunks:
-            low[c * LANES : (c + 1) * LANES, :] = field
-        if c >= first_high:
-            high[(c - first_high) * LANES : (c - first_high + 1) * LANES, :] = field
+
+    @after_start
+    def _():
+        me = lax.axis_index("tm")
+        totals = block_totals(pay, me, chunks, rows)
+        gains = by_block(pay, me, 1)
+        starts = by_block(pays, me, 0)
+        ends = by_block(pays, me, 1)
+        blocks = len(pays)
+        entering = [None] * blocks
+        state = jnp.zeros_like(totals[0])
+        for m in reversed(range(blocks)):
+            entering[m] = state
+            state = starts[m] + totals[m] * state
+        carry = jnp.zeros_like(totals[0])
+        adjoint = jnp.zeros_like(totals[0])
+        for m in range(blocks):
+            end = ends[m] + gains[m] * entering[m]
+            carry = jnp.where(m < me, end + totals[m] * carry, carry)
+            adjoint = jnp.where(m == me, entering[m], adjoint)
+        carry = carry * rows[1]
+        sums_table = table(frames, False)
+        grad_sq = jnp.zeros((8, LANES), F32)
+        for c in range(chunks):
+            p = chunk(p3, c)[...]
+            if c < 2 * RIM:
+                r = r_border[c]
+            elif c >= chunks - 2 * RIM:
+                r = r_border[c - chunks + 4 * RIM]
+            else:
+                r = r_inner[c - 2 * RIM]
+            scale = rows[0, c : c + 1, :] * chunk(pinv3, c)[...]
+            gradient = scale * (r + p[frames - 1 : frames, :] * adjoint[c : c + 1, :])
+            g3[c] = gradient
+            if RIM <= c < RIM + own:
+                grad_sq += jnp.sum((gradient * gradient).reshape(frames // 8, 8, LANES), axis=0)
+            z = summed(sums_table, scale * gradient)
+            field = (p * (z + carry[c : c + 1, :])).astype(BF16).T
+            if c < low_chunks:
+                low[c * LANES : (c + 1) * LANES, :] = field
+            if c >= first_high:
+                high[(c - first_high) * LANES : (c - first_high + 1) * LANES, :] = field
+        grad_sums[...] = grad_sq
+
+    fetch.wait()
+    image_sq = jnp.zeros((8, frames), F32)
     for q in range(stripe):
         if q + 2 * HB < low_chunks * per_chunk:
             named = picked(low, pattern, q, 0)
@@ -478,7 +496,7 @@
         image_sq += jnp.sum((image * image).reshape(PIX_BLOCK // 8, 8, frames), axis=0)
     both = jnp.concatenate(
         [
-            jnp.sum(grad_sq, axis=0, keepdims=True),
+            jnp.sum(grad_sums[...], axis=0, keepdims=True),
             jnp.sum(image_sq, axis=0, keepdims=True),
         ],
         axis=0,
@@ -500,7 +518,7 @@
     def spec(arg):
         if any(arg is other for other in far):
             return HBM
-        return SMEM if arg.dtype == jnp.int32 else VMEM
+        return pl.BlockSpec(memory_space=pl.ANY) if arg.dtype == jnp.int32 else VMEM
 
     in_specs = [jax.tree.map(spec, arg) for arg in args]
     in_specs.append(jax.tree.map(lambda _: VMEM, keep))
@@ -538,10 +556,10 @@
 def shared_blocks(value):
     size = lax.axis_size("tm")
     known = [value]
-    bit = 1
-    while bit < size:
+    bit = size // 2
+    while bit:
         known += [lax.ppermute(x, "tm", [(i, i ^ bit) for i in range(size)]) for x in known]
-        bit *= 2
+        bit //= 2
     return tuple(known)
 
 
@@ -593,6 +611,8 @@
     scratch = [
         pltpu.VMEM((stripe * K * NEU_BLOCK, frames), F32),
         pltpu.SMEM((stripe, 2 * HB + 1), jnp.int32),
+        pltpu.SMEM(pattern.shape, jnp.int32),
+        pltpu.SemaphoreType.DMA,
     ]
     staged = [pltpu.VMEM((neurons, frames), F32), pltpu.SemaphoreType.DMA((PARTS,))]
     middle = stripe * NEU_BLOCK // LANES // 2
@@ -648,6 +668,8 @@
             [
                 pltpu.VMEM((halves[0] * LANES, frames), BF16),
                 pltpu.VMEM((halves[1] * LANES, frames), BF16),
+                *scratch[2:],
+                pltpu.VMEM((8, LANES), F32),
             ],
             keep=held,
         )

time: 81.2 us -> 79.6 us (0.980)
  starting transfers between devices: 18.8 us -> 14.4 us
  waiting for transfers between devices: 11.7 us -> 15.8 us
  Pallas kernels: 20.8 us -> 19.6 us
    ppermute x12, starting transfers between devices: 8.84 us -> 4.4 us  [shared_blocks(): lax.ppermute(x, 'tm', [(i, i ^ bit) for i in range(size)])]
    ppermute x12, waiting for transfers between devices: 11.7 us -> 15.8 us  [shared_blocks(): lax.ppermute(x, 'tm', [(i, i ^ bit) for i in range(size)])]
    pallas_call x13, Pallas kernels: 20.8 us -> 19.6 us  [call(): pl.pallas_call(body, name=name, out_shape=outs, in_specs=in_specs, out_sp...]
  transfers between devices with their start and end apart: 18 -> 18, of which waited for: 10 -> 8; matrix products, arithmetic and copies ran while one was open for 0% -> 0% of each run, Pallas kernels for 10% -> 10%
where the time goes in v4:
time: 79.6 us; the launch traced here: 79.3 us
  blocking collectives  26 us (33%)
  Pallas kernels  19.6 us (25%)
  waiting for transfers between devices  15.8 us (20%)
  starting transfers between devices  14.4 us (18%)
  local copies, waits for them, and re-layouts  2.58 us (3%)
  between operations  0.99 us (1%)
    all_to_all x2, blocking collectives, per_device(): stats = lax.all_to_all(stats, ('tile', 'tm'), 0, 0)  26 us
    pallas_call x13, Pallas kernels, call(): pl.pallas_call(body, name=name, out_shape=outs, in_specs=in_specs, out_sp...  19.6 us
    ppermute x12, waiting for transfers between devices, shared_blocks(): lax.ppermute(x, 'tm', [(i, i ^ bit) for i in range(size)])  15.8 us
    ppermute x3, starting transfers between devices, swapped(): lax.ppermute(first, 'tile', pairs(0))  8.01 us
    ppermute x12, starting transfers between devices, shared_blocks(): lax.ppermute(x, 'tm', [(i, i ^ bit) for i in range(size)])  4.4 us
    unnamed x12, local copies, waits for them, and re-layouts  2.58 us
    ppermute x3, starting transfers between devices, swapped(): lax.ppermute(second, 'tile', pairs(1))  1.96 us
  transfers between devices with their start and end apart: 18, of which 8 were waited for; matrix products, arithmetic and copies ran while one was open for 0% of the time, Pallas kernels for 10%

profile of v4, /device:TPU:0, one launch (start us, length us, event | category | flops | bytes accessed | tf_op | source)
XLA Modules:
  0.0 79.3 jit_solution(17559327908287319998)
XLA Ops:
  0.6 0.0 copy-start.4
  0.6 0.7 copy-done.4
  1.3 0.9 %rims.1 = (f32[136,128]{1,0:T(8,128)S(1)}, f32[136,128]{1,0:T(8,128)S(1)}, f32[16,128]{1,0:T(8,128)S(1)}) custom-call(f32[2048,128]{1,0:T(8,128)} %refs_0_.3, f32[16,128]{1,0:T(8,128)S(1)} %bitcast.9), custom_call_target="tpu_custom_call" | custom-call | flops 100000000 | bytes 3000000 | tf_op jit(solution)/shard_map/rims/pallas_call | solution.py:529
  2.2 3.0 %collective-permute-start = (f32[136,128]{1,0:T(8,128)S(1)}, f32[136,128]{1,0:T(8,128)S(1)}, u32[]{:S(2)}, u32[]{:S(2)}) collective-permute-start(f32[136,128]{1,0:T(8,128)S(1)} %get-tuple-element.49), channel_id=1, source_target_pairs={{0,1},{2,3},{4,5},{6,7},{1,0},{3,2},{5,4},{7,6},{8,9},{10,11},{12,... | collective-permute-start | bytes 208904 | tf_op jit(solution)/shard_map/ppermute | solution.py:553
  5.3 0.7 collective-permute-start.1
  5.9 0.0 copy-start.2
  5.9 1.2 %copy-done.2 = f32[2048,128]{1,0:T(8,128)S(1)} copy-done((f32[2048,128]{1,0:T(8,128)S(1)}, f32[2048,128]{1,0:T(8,128)}, u32[]{:S(2)}) %copy-start.2) | copy-done | bytes 1048600
  7.2 0.0 copy-start.5
  7.2 0.7 copy-done.5
  7.8 0.0 copy-start.1
  7.8 0.0 copy-start.3
  7.8 1.4 %prep_own.1 = (f32[16,128,128]{2,1,0:T(8,128)S(1)}, f32[16,128,128]{2,1,0:T(8,128)S(1)}, f32[16,128,128]{2,1,0:T(8,128)S(1)}, f32[16,128,128]{2,1,0:T(8,128)S(1)...) custom-call(f32[2048,128]{1,0:T(8,128)S(1)} %copy-done.2, ...), custom_call_target="tpu_custom_call" | custom-call | flops 160000000 | bytes 4800000 | tf_op jit(solution)/shard_map/prep_own/pallas_call | solution.py:529
  9.3 0.0 collective-permute-done.refs_0_
  9.3 0.0 collective-permute-done.1.refs_1_
  9.3 0.3 prep_rim.1
  9.6 1.6 %collective-permute-start.2 = (f32[2,24,128]{2,1,0:T(8,128)S(1)}, f32[2,24,128]{2,1,0:T(8,128)S(1)}, u32[]{:S(2)}, u32[]{:S(2)}) collective-permute-start(f32[2,24,128]{2,1,0:T(8,128)S(1)} %get-tuple-element.62.refs_4__0_.refs_5__0_.refs_6__0_), channel_id=1, source_target_pairs={{0,16},{8,24},{16,0},{24,8},{1,17},{9,25},{17,1},{25,9},{2,18},{10... | collective-permute-start | bytes 73736 | tf_op jit(solution)/shard_map/ppermute | solution.py:561
  11.1 0.0 collective-permute-start.3
  11.1 2.3 %collective-permute-done.2.refs_4__1_.refs_5__1_.refs_6__1_ = f32[2,24,128]{2,1,0:T(8,128)S(1)} collective-permute-done((f32[2,24,128]{2,1,0:T(8,128)S(1)}, f32[2,24,128]{2,1,0:T(8,128)S(1)}, u32[]{:S(2)}, u32[]{:S(2)}) %collective-permute-start.2) | collective-permute-done | bytes 24608 | tf_op jit(solution)/shard_map/ppermute | solution.py:561
  13.5 0.0 collective-permute-start.4
  13.5 0.0 collective-permute-done.3.refs_4__2_.refs_5__2_.refs_6__2_
  13.5 1.2 %collective-permute-done.4.refs_4__3_.refs_5__3_.refs_6__3_ = f32[2,24,128]{2,1,0:T(8,128)S(1)} collective-permute-done((f32[2,24,128]{2,1,0:T(8,128)S(1)}, f32[2,24,128]{2,1,0:T(8,128)S(1)}, u32[]{:S(2)}, u32[]{:S(2)}) %collective-permute-start.4) | collective-permute-done | bytes 24608 | tf_op jit(solution)/shard_map/ppermute | solution.py:561
  14.7 0.0 copy-done.1
  14.7 0.0 copy-done.3
  14.7 0.0 copy-start
  14.7 1.7 %edge.2 = (bf16[2304,128]{1,0:T(8,128)(2,1)S(1)}, f32[4,128,128]{2,1,0:T(8,128)S(1)}, f32[4,128,128]{2,1,0:T(8,128)S(1)}, bf16[2,128,128]{2,1,0:T(8,128)(2,1)S(1)}, bf16[2,128,128]{2,1,0:T(8,128)(2,1)S(1)}) custom-call(s32[4,32]{1,0:T(4,128)S(1)} %bitcast.3, f32[16,128,128]{2,1,0:T(8,128)S(1)} %get-tuple-element.60.refs_1__0_, ...), custom_call_target="tpu_custom_call" | custom-call | flops 250000000 | bytes 7500000 | tf_op jit(solution)/shard_map/edge/pallas_call | solution.py:529
  16.4 4.4 %collective-permute-start.5 = (bf16[2,128,128]{2,1,0:T(8,128)(2,1)S(1)}, bf16[2,128,128]{2,1,0:T(8,128)(2,1)S(1)}, u32[]{:S(2)}, u32[]{:S(2)}) collective-permute-start(bf16[2,128,128]{2,1,0:T(8,128)(2,1)S(1)} %get-tuple-element.68), channel_id=1, source_target_pairs={{0,1},{2,3},{4,5},{6,7},{1,0},{3,2},{5,4},{7,6},{8,9},{10,11},{12,... | collective-permute-start | bytes 196616 | tf_op jit(solution)/shard_map/ppermute | solution.py:553
  20.7 0.7 collective-permute-start.6
  21.4 0.0 copy-done
  21.4 3.3 %inner.2 = (f32[14,128,128]{2,1,0:T(8,128)S(1)}, f32[2,24,128]{2,1,0:T(8,128)S(1)}) custom-call(s32[4,32]{1,0:T(4,128)S(1)} %bitcast.4, f32[16,128,128]{2,1,0:T(8,128)S(1)} %get-tuple-element.55.refs_2__0_.refs_1__0_.refs_3__0_, f32[2,128,128]{2,1,0:T(8,128)S(1)} %get-tuple-element.56.refs_2__1_.refs_1__1_.refs_3__1_, ...), custom_call_target="tpu_custom_call" | custom-call | flops 400000000 | bytes 12000000 | tf_op jit(solution)/shard_map/inner/pallas_call | solution.py:529
  24.7 0.0 collective-permute-done.5.refs_1_
  24.7 0.0 collective-permute-done.6.refs_2_
  24.7 0.3 border.2
  25.0 1.5 %collective-permute-start.7 = (f32[2,24,128]{2,1,0:T(8,128)S(1)}, f32[2,24,128]{2,1,0:T(8,128)S(1)}, u32[]{:S(2)}, u32[]{:S(2)}) collective-permute-start(f32[2,24,128]{2,1,0:T(8,128)S(1)} %get-tuple-element.72.refs_7__0_), channel_id=1, source_target_pairs={{0,16},{8,24},{16,0},{24,8},{1,17},{9,25},{17,1},{25,9},{2,18},{10... | collective-permute-start | bytes 73736 | tf_op jit(solution)/shard_map/ppermute | solution.py:561
  26.5 0.0 collective-permute-start.8
  26.5 2.3 %collective-permute-done.7.refs_7__1_ = f32[2,24,128]{2,1,0:T(8,128)S(1)} collective-permute-done((f32[2,24,128]{2,1,0:T(8,128)S(1)}, f32[2,24,128]{2,1,0:T(8,128)S(1)}, u32[]{:S(2)}, u32[]{:S(2)}) %collective-permute-start.7) | collective-permute-done | bytes 24608 | tf_op jit(solution)/shard_map/ppermute | solution.py:561
  28.9 0.0 collective-permute-start.9
  28.9 0.0 collective-permute-done.8.refs_7__2_
  28.9 1.2 %collective-permute-done.9.refs_7__3_ = f32[2,24,128]{2,1,0:T(8,128)S(1)} collective-permute-done((f32[2,24,128]{2,1,0:T(8,128)S(1)}, f32[2,24,128]{2,1,0:T(8,128)S(1)}, u32[]{:S(2)}, u32[]{:S(2)}) %collective-permute-start.9) | collective-permute-done | bytes 24608 | tf_op jit(solution)/shard_map/ppermute | solution.py:561
  30.1 2.1 %direction.2 = (f32[18,128,128]{2,1,0:T(8,128)S(1)}, f32[32,2,128]{2,1,0:T(2,128)S(1)}) custom-call(s32[4,32]{1,0:T(4,128)S(1)} %bitcast.5, f32[14,128,128]{2,1,0:T(8,128)S(1)} %get-tuple-element.66.refs_1_, f32[4,128,128]{2,1,0:T(8,128)S(1)} %get-tuple-element.71.refs_2_, f32[16,128,128]{2,1,0:T(8,128)S(1)} %get-tuple-element.55.refs_2__0_.refs_1__0_.refs_3__0_, ...), custom_call_target="tpu_custom_call" | custom-call | flops 400000000 | bytes 12000000 | tf_op jit(solution)/shard_map/direction/pallas_call | solution.py:529
  32.2 14.2 %all_to_all.10.refs_2_ = f32[32,2,128]{2,1,0:T(2,128)S(1)} all-to-all(f32[32,2,128]{2,1,0:T(2,128)S(1)} %get-tuple-element.74), channel_id=1, replica_groups=mesh['tm'=4,'tile'=8] {'tile','tm'}, dimensions={0} | all-to-all | bytes 65536 | tf_op jit(solution)/shard_map/all_to_all | solution.py:676
  46.4 0.7 update.1
  47.1 0.6 collective-permute-start.10
  47.7 0.0 collective-permute-start.11
  47.7 3.2 %collective-permute-done.10.refs_5__1_ = f32[1,24,128]{2,1,0:T(8,128)S(1)} collective-permute-done((f32[1,24,128]{2,1,0:T(8,128)S(1)}, f32[1,24,128]{2,1,0:T(8,128)S(1)}, u32[]{:S(2)}, u32[]{:S(2)}) %collective-permute-start.10) | collective-permute-done | bytes 12320 | tf_op jit(solution)/shard_map/ppermute | solution.py:561
  50.9 0.0 collective-permute-start.12
  50.9 0.0 collective-permute-done.11.refs_5__2_
  50.9 1.2 %collective-permute-done.12.refs_5__3_ = f32[1,24,128]{2,1,0:T(8,128)S(1)} collective-permute-done((f32[1,24,128]{2,1,0:T(8,128)S(1)}, f32[1,24,128]{2,1,0:T(8,128)S(1)}, u32[]{:S(2)}, u32[]{:S(2)}) %collective-permute-start.12) | collective-permute-done | bytes 12320 | tf_op jit(solution)/shard_map/ppermute | solution.py:561
  52.1 1.7 %edge.3 = (bf16[2304,128]{1,0:T(8,128)(2,1)S(1)}, f32[4,128,128]{2,1,0:T(8,128)S(1)}, f32[4,128,128]{2,1,0:T(8,128)S(1)}, bf16[2,128,128]{2,1,0:T(8,128)(2,1)S(1...) custom-call(s32[4,32]{1,0:T(4,128)S(1)} %bitcast.6, f32[16,128,128]{2,1,0:T(8,128)S(1)} %get-tuple-element.76.refs_1__0_, ...), custom_call_target="tpu_custom_call" | custom-call | flops 250000000 | bytes 7500000 | tf_op jit(solution)/shard_map/edge/pallas_call | solution.py:529
  53.8 0.6 collective-permute-start.13
  54.4 0.7 collective-permute-start.14
  55.0 3.5 %inner.3 = (f32[14,128,128]{2,1,0:T(8,128)S(1)}, f32[2,24,128]{2,1,0:T(8,128)S(1)}, f32[2048,128]{1,0:T(8,128)}) custom-call(s32[4,32]{1,0:T(4,128)S(1)} %bitcast.7, f32[16,128,128]{2,1,0:T(8,128)S(1)} %get-tuple-element.55.refs_2__0_.refs_1__0_.refs_3__0_, f32[2,128,128]{2,1,0:T(8,128)S(1)} %get-tuple-element.56.refs_2__1_.refs_1__1_.refs_3__1_, ...), custom_call_target="tpu_custom_call" | custom-call | flops 400000000 | bytes 12000000 | tf_op jit(solution)/shard_map/inner/pallas_call | solution.py:529
  58.6 0.0 collective-permute-done.13.refs_1_
  58.6 0.0 collective-permute-done.14.refs_2_
  58.6 0.3 border.3
  58.9 0.7 collective-permute-start.15
  59.6 0.0 collective-permute-start.16
  59.6 3.2 %collective-permute-done.15.refs_7__1_ = f32[2,24,128]{2,1,0:T(8,128)S(1)} collective-permute-done((f32[2,24,128]{2,1,0:T(8,128)S(1)}, f32[2,24,128]{2,1,0:T(8,128)S(1)}, u32[]{:S(2)}, u32[]{:S(2)}) %collective-permute-start.15) | collective-permute-done | bytes 24608 | tf_op jit(solution)/shard_map/ppermute | solution.py:561
  62.8 0.0 collective-permute-start.17
  62.8 0.0 collective-permute-done.16.refs_7__2_
  62.8 1.2 %collective-permute-done.17.refs_7__3_ = f32[2,24,128]{2,1,0:T(8,128)S(1)} collective-permute-done((f32[2,24,128]{2,1,0:T(8,128)S(1)}, f32[2,24,128]{2,1,0:T(8,128)S(1)}, u32[]{:S(2)}, u32[]{:S(2)}) %collective-permute-start.17) | collective-permute-done | bytes 24608 | tf_op jit(solution)/shard_map/ppermute | solution.py:561
  64.0 2.1 %direction.3 = (f32[18,128,128]{2,1,0:T(8,128)S(1)}, f32[32,2,128]{2,1,0:T(2,128)S(1)}) custom-call(s32[4,32]{1,0:T(4,128)S(1)} %bitcast.8, f32[14,128,128]{2,1,0:T(8,128)S(1)} %get-tuple-element.82.refs_1_, f32[4,128,128]{2,1,0:T(8,128)S(1)} %get-tuple-element.87.refs_2_, f32[16,128,128]{2,1,0:T(8,128)S(1)} %get-tuple-element.55.refs_2__0_.refs_1__0_.refs_3__0_, ...), custom_call_target="tpu_custom_call" | custom-call | flops 400000000 | bytes 12000000 | tf_op jit(solution)/shard_map/direction/pallas_call | solution.py:529
  66.1 11.8 %all_to_all.11.refs_2_ = f32[32,2,128]{2,1,0:T(2,128)S(1)} all-to-all(f32[32,2,128]{2,1,0:T(2,128)S(1)} %get-tuple-element.90), channel_id=1, replica_groups=mesh['tm'=4,'tile'=8] {'tile','tm'}, dimensions={0} | all-to-all | bytes 65536 | tf_op jit(solution)/shard_map/all_to_all | solution.py:676
  77.9 1.3 %final.1 = f32[2048,128]{1,0:T(8,128)} custom-call(f32[16,128,128]{2,1,0:T(8,128)S(1)} %get-tuple-element.75.refs_8__0_.refs_9__0_.refs_7__0_.refs_0_, f32[18,128,128]{2,1,0:T(8,128)S(1)} %get-tuple-element.89.refs_1_, f32[32,2,128]{2,1,0:T(2,128)S(1)} %all_to_all.11.refs_2_), custom_call_target="tpu_custom_call" | custom-call | flops 140000000 | bytes 4200000 | tf_op jit(solution)/shard_map/final/pallas_call | solution.py:529
Async XLA Ops:
  0.6 0.7 copy-start.4
  2.2 7.0 %collective-permute-start = (f32[136,128]{1,0:T(8,128)S(1)}, f32[136,128]{1,0:T(8,128)S(1)}, u32[]{:S(2)}, u32[]{:S(2)}) collective-permute-start(f32[136,128]{1,0:T(8,128)S(1)} %get-tuple-element.49), channel_id=1, source_target_pairs={{0,1},{2,3},{4,5},{6,7},{1,0},{3,2},{5,4},{7,6},{8,9},{10,11},{12,... | collective-permute-start | bytes 208904 | tf_op jit(solution)/shard_map/ppermute | solution.py:553
  5.3 4.0 %collective-permute-start.1 = (f32[136,128]{1,0:T(8,128)S(1)}, f32[136,128]{1,0:T(8,128)S(1)}, u32[]{:S(2)}, u32[]{:S(2)}) collective-permute-start(f32[136,128]{1,0:T(8,128)S(1)} %get-tuple-element.50), channel_id=1, source_target_pairs={{1,2},{3,4},{5,6},{2,1},{4,3},{6,5},{9,10},{11,12},{13,14},{10,9},... | collective-permute-start | bytes 208904 | tf_op jit(solution)/shard_map/ppermute | solution.py:553
  5.9 1.2 %copy-start.2 = (f32[2048,128]{1,0:T(8,128)S(1)}, f32[2048,128]{1,0:T(8,128)}, u32[]{:S(2)}) copy-start(f32[2048,128]{1,0:T(8,128)} %refs_0_.3) | copy-start | bytes 3145732
  7.2 0.7 copy-start.5
  7.8 6.8 %copy-start.1 = (bf16[8192,128]{1,0:T(8,128)(2,1)S(1)}, bf16[8192,128]{1,0:T(8,128)(2,1)}, u32[]{:S(2)}) copy-start(bf16[8192,128]{1,0:T(8,128)(2,1)} %refs_7_.7) | copy-start | bytes 6291460
  7.8 6.8 %copy-start.3 = (s32[32,4]{0,1:T(4,128)S(1)}, s32[32,4]{0,1:T(4,128)}, u32[]{:S(2)}) copy-start(s32[32,4]{0,1:T(4,128)} %param.8) | copy-start | bytes 1540
  9.6 3.9 %collective-permute-start.2 = (f32[2,24,128]{2,1,0:T(8,128)S(1)}, f32[2,24,128]{2,1,0:T(8,128)S(1)}, u32[]{:S(2)}, u32[]{:S(2)}) collective-permute-start(f32[2,24,128]{2,1,0:T(8,128)S(1)} %get-tuple-element.62.refs_4__0_.refs_5__0_.refs_6__0_), channel_id=1, source_target_pairs={{0,16},{8,24},{16,0},{24,8},{1,17},{9,25},{17,1},{25,9},{2,18},{10... | collective-permute-start | bytes 73736 | tf_op jit(solution)/shard_map/ppermute | solution.py:561
  11.1 2.3 %collective-permute-start.3 = (f32[2,24,128]{2,1,0:T(8,128)S(1)}, f32[2,24,128]{2,1,0:T(8,128)S(1)}, u32[]{:S(2)}, u32[]{:S(2)}) collective-permute-start(f32[2,24,128]{2,1,0:T(8,128)S(1)} %get-tuple-element.62.refs_4__0_.refs_5__0_.refs_6__0_), channel_id=1, source_target_pairs={{0,8},{8,0},{16,24},{24,16},{1,9},{9,1},{17,25},{25,17},{2,10},{10... | collective-permute-start | bytes 73736 | tf_op jit(solution)/shard_map/ppermute | solution.py:561
  13.5 1.2 %collective-permute-start.4 = (f32[2,24,128]{2,1,0:T(8,128)S(1)}, f32[2,24,128]{2,1,0:T(8,128)S(1)}, u32[]{:S(2)}, u32[]{:S(2)}) collective-permute-start(f32[2,24,128]{2,1,0:T(8,128)S(1)} %collective-permute-done.2.refs_4__1_.refs_5__1_.refs_6__1_), channel_id=1, source_target_pairs={{0,8},{8,0},{16,24},{24,16},{1,9},{9,1},{17,25},{25,17},{2,10},{10... | collective-permute-start | bytes 73736 | tf_op jit(solution)/shard_map/ppermute | solution.py:561
  14.7 6.7 %copy-start = (bf16[8192,256]{1,0:T(8,128)(2,1)S(1)}, bf16[8192,256]{1,0:T(8,128)(2,1)}, u32[]{:S(2)}) copy-start(bf16[8192,256]{1,0:T(8,128)(2,1)} %refs_8_.3) | copy-start | bytes 12582916
  16.4 8.4 %collective-permute-start.5 = (bf16[2,128,128]{2,1,0:T(8,128)(2,1)S(1)}, bf16[2,128,128]{2,1,0:T(8,128)(2,1)S(1)}, u32[]{:S(2)}, u32[]{:S(2)}) collective-permute-start(bf16[2,128,128]{2,1,0:T(8,128)(2,1)S(1)} %get-tuple-element.68), channel_id=1, source_target_pairs={{0,1},{2,3},{4,5},{6,7},{1,0},{3,2},{5,4},{7,6},{8,9},{10,11},{12,... | collective-permute-start | bytes 196616 | tf_op jit(solution)/shard_map/ppermute | solution.py:553
  20.7 4.0 %collective-permute-start.6 = (bf16[2,128,128]{2,1,0:T(8,128)(2,1)S(1)}, bf16[2,128,128]{2,1,0:T(8,128)(2,1)S(1)}, u32[]{:S(2)}, u32[]{:S(2)}) collective-permute-start(bf16[2,128,128]{2,1,0:T(8,128)(2,1)S(1)} %get-tuple-element.69), channel_id=1, source_target_pairs={{1,2},{3,4},{5,6},{2,1},{4,3},{6,5},{9,10},{11,12},{13,14},{10,9},... | collective-permute-start | bytes 196616 | tf_op jit(solution)/shard_map/ppermute | solution.py:553
  25.0 3.9 %collective-permute-start.7 = (f32[2,24,128]{2,1,0:T(8,128)S(1)}, f32[2,24,128]{2,1,0:T(8,128)S(1)}, u32[]{:S(2)}, u32[]{:S(2)}) collective-permute-start(f32[2,24,128]{2,1,0:T(8,128)S(1)} %get-tuple-element.72.refs_7__0_), channel_id=1, source_target_pairs={{0,16},{8,24},{16,0},{24,8},{1,17},{9,25},{17,1},{25,9},{2,18},{10... | collective-permute-start | bytes 73736 | tf_op jit(solution)/shard_map/ppermute | solution.py:561
  26.5 2.4 %collective-permute-start.8 = (f32[2,24,128]{2,1,0:T(8,128)S(1)}, f32[2,24,128]{2,1,0:T(8,128)S(1)}, u32[]{:S(2)}, u32[]{:S(2)}) collective-permute-start(f32[2,24,128]{2,1,0:T(8,128)S(1)} %get-tuple-element.72.refs_7__0_), channel_id=1, source_target_pairs={{0,8},{8,0},{16,24},{24,16},{1,9},{9,1},{17,25},{25,17},{2,10},{10... | collective-permute-start | bytes 73736 | tf_op jit(solution)/shard_map/ppermute | solution.py:561
  28.9 1.2 %collective-permute-start.9 = (f32[2,24,128]{2,1,0:T(8,128)S(1)}, f32[2,24,128]{2,1,0:T(8,128)S(1)}, u32[]{:S(2)}, u32[]{:S(2)}) collective-permute-start(f32[2,24,128]{2,1,0:T(8,128)S(1)} %collective-permute-done.7.refs_7__1_), channel_id=1, source_target_pairs={{0,8},{8,0},{16,24},{24,16},{1,9},{9,1},{17,25},{25,17},{2,10},{10... | collective-permute-start | bytes 73736 | tf_op jit(solution)/shard_map/ppermute | solution.py:561
  47.1 3.8 %collective-permute-start.10 = (f32[1,24,128]{2,1,0:T(8,128)S(1)}, f32[1,24,128]{2,1,0:T(8,128)S(1)}, u32[]{:S(2)}, u32[]{:S(2)}) collective-permute-start(f32[1,24,128]{2,1,0:T(8,128)S(1)} %get-tuple-element.78.refs_5__0_), channel_id=1, source_target_pairs={{0,16},{8,24},{16,0},{24,8},{1,17},{9,25},{17,1},{25,9},{2,18},{10... | collective-permute-start | bytes 36872 | tf_op jit(solution)/shard_map/ppermute | solution.py:561
  47.7 3.2 %collective-permute-start.11 = (f32[1,24,128]{2,1,0:T(8,128)S(1)}, f32[1,24,128]{2,1,0:T(8,128)S(1)}, u32[]{:S(2)}, u32[]{:S(2)}) collective-permute-start(f32[1,24,128]{2,1,0:T(8,128)S(1)} %get-tuple-element.78.refs_5__0_), channel_id=1, source_target_pairs={{0,8},{8,0},{16,24},{24,16},{1,9},{9,1},{17,25},{25,17},{2,10},{10... | collective-permute-start | bytes 36872 | tf_op jit(solution)/shard_map/ppermute | solution.py:561
  50.9 1.2 %collective-permute-start.12 = (f32[1,24,128]{2,1,0:T(8,128)S(1)}, f32[1,24,128]{2,1,0:T(8,128)S(1)}, u32[]{:S(2)}, u32[]{:S(2)}) collective-permute-start(f32[1,24,128]{2,1,0:T(8,128)S(1)} %collective-permute-done.10.refs_5__1_), channel_id=1, source_target_pairs={{0,8},{8,0},{16,24},{24,16},{1,9},{9,1},{17,25},{25,17},{2,10},{10... | collective-permute-start | bytes 36872 | tf_op jit(solution)/shard_map/ppermute | solution.py:561
  53.8 4.8 %collective-permute-start.13 = (bf16[2,128,128]{2,1,0:T(8,128)(2,1)S(1)}, bf16[2,128,128]{2,1,0:T(8,128)(2,1)S(1)}, u32[]{:S(2)}, u32[]{:S(2)}) collective-permute-start(bf16[2,128,128]{2,1,0:T(8,128)(2,1)S(1)} %get-tuple-element.84), channel_id=1, source_target_pairs={{0,1},{2,3},{4,5},{6,7},{1,0},{3,2},{5,4},{7,6},{8,9},{10,11},{12,... | collective-permute-start | bytes 196616 | tf_op jit(solution)/shard_map/ppermute | solution.py:553
  54.4 4.2 %collective-permute-start.14 = (bf16[2,128,128]{2,1,0:T(8,128)(2,1)S(1)}, bf16[2,128,128]{2,1,0:T(8,128)(2,1)S(1)}, u32[]{:S(2)}, u32[]{:S(2)}) collective-permute-start(bf16[2,128,128]{2,1,0:T(8,128)(2,1)S(1)} %get-tuple-element.85), channel_id=1, source_target_pairs={{1,2},{3,4},{5,6},{2,1},{4,3},{6,5},{9,10},{11,12},{13,14},{10,9},... | collective-permute-start | bytes 196616 | tf_op jit(solution)/shard_map/ppermute | solution.py:553
  58.9 3.9 %collective-permute-start.15 = (f32[2,24,128]{2,1,0:T(8,128)S(1)}, f32[2,24,128]{2,1,0:T(8,128)S(1)}, u32[]{:S(2)}, u32[]{:S(2)}) collective-permute-start(f32[2,24,128]{2,1,0:T(8,128)S(1)} %get-tuple-element.88.refs_7__0_), channel_id=1, source_target_pairs={{0,16},{8,24},{16,0},{24,8},{1,17},{9,25},{17,1},{25,9},{2,18},{10... | collective-permute-start | bytes 73736 | tf_op jit(solution)/shard_map/ppermute | solution.py:561
  59.6 3.2 %collective-permute-start.16 = (f32[2,24,128]{2,1,0:T(8,128)S(1)}, f32[2,24,128]{2,1,0:T(8,128)S(1)}, u32[]{:S(2)}, u32[]{:S(2)}) collective-permute-start(f32[2,24,128]{2,1,0:T(8,128)S(1)} %get-tuple-element.88.refs_7__0_), channel_id=1, source_target_pairs={{0,8},{8,0},{16,24},{24,16},{1,9},{9,1},{17,25},{25,17},{2,10},{10... | collective-permute-start | bytes 73736 | tf_op jit(solution)/shard_map/ppermute | solution.py:561
  62.8 1.2 %collective-permute-start.17 = (f32[2,24,128]{2,1,0:T(8,128)S(1)}, f32[2,24,128]{2,1,0:T(8,128)S(1)}, u32[]{:S(2)}, u32[]{:S(2)}) collective-permute-start(f32[2,24,128]{2,1,0:T(8,128)S(1)} %collective-permute-done.15.refs_7__1_), channel_id=1, source_target_pairs={{0,8},{8,0},{16,24},{24,16},{1,9},{9,1},{17,25},{25,17},{2,10},{10... | collective-permute-start | bytes 73736 | tf_op jit(solution)/shard_map/ppermute | solution.py:561

commit v5 on v4

--- a/solution.py
+++ b/solution.py
@@ -292,9 +292,9 @@
             place[q, pattern[k, q] - q] = k
 
 
-def pull_back(pattern, ext, feet, record, contrib, q):
+def pull_back(pattern, ext, feet, record, contrib, q, first=0):
     foot = foot_of(feet, q, pattern.shape[1])
-    fitted = jnp.dot(foot, picked(ext, pattern, q), preferred_element_type=F32)
+    fitted = jnp.dot(foot, picked(ext, pattern, q, first), preferred_element_type=F32)
     residual = (fitted - block_of(record, q).astype(F32)).astype(BF16)
     contrib[q * K * NEU_BLOCK : (q + 1) * K * NEU_BLOCK, :] = lax.dot_general(
         foot, residual, (((0,), (0,)), ((), ())), preferred_element_type=F32
@@ -323,13 +323,26 @@
 def edge_kernel(
     pattern_far, z3, p3, rows, pay, pays, feet, record, ext, zones, spill, send_a, send_b, *rest
 ):
-    *traces, contrib, place, pattern, sem = rest
+    *traces, contrib, place, pattern, sem, near, state = rest
     fetch = pltpu.make_async_copy(pattern_far, pattern, sem)
     fetch.start()
     chunks = chunk_count(z3)
     stripe = pattern.shape[1]
     edge = 2 * HB
     ranges = ((0, edge), (stripe - edge, stripe))
+    near_chunks = near.shape[0] // LANES // 2
+    inner = range(near_chunks, chunks - near_chunks)
+
+    def trace(c):
+        field = chunk(p3, c)[...] * (chunk(z3, c)[...] + state[c : c + 1, :])
+        if traces and RIM <= c < chunks - RIM:
+            field = field.T
+            traces[0][(c - RIM) * LANES : (c - RIM + 1) * LANES, :] = field
+            field = field.astype(BF16)
+        else:
+            field = field.astype(BF16).T
+        ext[c * LANES : (c + 1) * LANES, :] = field
+        return field
 
     @after_start
     def _():
@@ -339,23 +352,21 @@
         carry = jnp.zeros_like(totals[0])
         for m, end in enumerate(ends):
             carry = jnp.where(m < me, end + totals[m] * carry, carry)
-        carry = carry * rows[1]
+        state[...] = carry * rows[1]
         for c in range(chunks):
-            field = chunk(p3, c)[...] * (chunk(z3, c)[...] + carry[c : c + 1, :])
-            at = slice(c * LANES, (c + 1) * LANES)
-            if traces and RIM <= c < chunks - RIM:
-                field = field.T
-                traces[0][(c - RIM) * LANES : (c - RIM + 1) * LANES, :] = field
-                ext[at, :] = field.astype(BF16)
-            else:
-                ext[at, :] = field.astype(BF16).T
+            if c not in inner:
+                at = c if c < near_chunks else c - len(inner)
+                near[at * LANES : (at + 1) * LANES, :] = trace(c)
 
     fetch.wait()
     for start, stop in ranges:
         note_places(pattern, place, start, stop)
     for start, stop in ranges:
+        first = 0 if start == 0 else len(inner) * LANES // NEU_BLOCK
         for q in range(start, stop):
-            pull_back(pattern, ext, feet, record, contrib, q)
+            pull_back(pattern, near, feet, record, contrib, q, first)
+    for c in inner:
+        trace(c)
     even = lax.axis_index("tile") % 2 == 0
     for i in range(2 * RIM):
         below = gathered(contrib, place, i, ranges)
@@ -432,7 +443,7 @@
 def direction_kernel(
     pattern_far, r_inner, r_border, p3, pinv3, rows, pay, pays, feet, g3, stats, low, high, *rest
 ):
-    pattern, sem, grad_sums = rest
+    pattern, sem, grad_sums, image_sums, states = rest
     fetch = pltpu.make_async_copy(pattern_far, pattern, sem)
     fetch.start()
     chunks, frames = g3.shape[0], g3.shape[1]
@@ -441,6 +452,37 @@
     per_chunk = LANES // NEU_BLOCK
     low_chunks = low.shape[0] // LANES
     first_high = chunks - high.shape[0] // LANES
+
+    sums_table = table(frames, False)
+
+    def work(c):
+        p = chunk(p3, c)[...]
+        if c < 2 * RIM:
+            r = r_border[c]
+        elif c >= chunks - 2 * RIM:
+            r = r_border[c - chunks + 4 * RIM]
+        else:
+            r = r_inner[c - 2 * RIM]
+        scale = rows[0, c : c + 1, :] * chunk(pinv3, c)[...]
+        gradient = scale * (r + p[frames - 1 : frames, :] * states[1, c : c + 1, :])
+        g3[c] = gradient
+        z = summed(sums_table, scale * gradient)
+        field = (p * (z + states[0, c : c + 1, :])).astype(BF16).T
+        if c < low_chunks:
+            low[c * LANES : (c + 1) * LANES, :] = field
+        if c >= first_high:
+            high[(c - first_high) * LANES : (c - first_high + 1) * LANES, :] = field
+        if RIM <= c < RIM + own:
+            return jnp.sum((gradient * gradient).reshape(frames // 8, 8, LANES), axis=0)
+        return jnp.zeros((8, LANES), F32)
+
+    def image(q):
+        if q + 2 * HB < low_chunks * per_chunk:
+            named = picked(low, pattern, q, 0)
+        else:
+            named = picked(high, pattern, q, first_high * per_chunk)
+        value = jnp.dot(foot_of(feet, q, stripe), named, preferred_element_type=F32)
+        return jnp.sum((value * value).reshape(PIX_BLOCK // 8, 8, frames), axis=0)
 
     @after_start
     def _():
@@ -461,39 +503,30 @@
             end = ends[m] + gains[m] * entering[m]
             carry = jnp.where(m < me, end + totals[m] * carry, carry)
             adjoint = jnp.where(m == me, entering[m], adjoint)
-        carry = carry * rows[1]
-        sums_table = table(frames, False)
-        grad_sq = jnp.zeros((8, LANES), F32)
-        for c in range(chunks):
-            p = chunk(p3, c)[...]
-            if c < 2 * RIM:
-                r = r_border[c]
-            elif c >= chunks - 2 * RIM:
-                r = r_border[c - chunks + 4 * RIM]
-            else:
-                r = r_inner[c - 2 * RIM]
-            scale = rows[0, c : c + 1, :] * chunk(pinv3, c)[...]
-            gradient = scale * (r + p[frames - 1 : frames, :] * adjoint[c : c + 1, :])
-            g3[c] = gradient
-            if RIM <= c < RIM + own:
-                grad_sq += jnp.sum((gradient * gradient).reshape(frames // 8, 8, LANES), axis=0)
-            z = summed(sums_table, scale * gradient)
-            field = (p * (z + carry[c : c + 1, :])).astype(BF16).T
-            if c < low_chunks:
-                low[c * LANES : (c + 1) * LANES, :] = field
-            if c >= first_high:
-                high[(c - first_high) * LANES : (c - first_high + 1) * LANES, :] = field
+        states[0] = carry * rows[1]
+        states[1] = adjoint
+        grad_sums[...] = sum(work(c) for c in range(low_chunks))
+
+    fetch.wait()
+
+    @after_start
+    def _():
+        grad_sq = grad_sums[...]
+        image_sq = jnp.zeros((8, frames), F32)
+        q = 0
+        rest_chunks = chunks - low_chunks
+        low_blocks = (low_chunks * per_chunk) - 2 * HB
+        for i in range(rest_chunks):
+            grad_sq += work(low_chunks + i)
+            while q < low_blocks * (i + 1) // rest_chunks:
+                image_sq += image(q)
+                q += 1
         grad_sums[...] = grad_sq
-
-    fetch.wait()
-    image_sq = jnp.zeros((8, frames), F32)
-    for q in range(stripe):
-        if q + 2 * HB < low_chunks * per_chunk:
-            named = picked(low, pattern, q, 0)
-        else:
-            named = picked(high, pattern, q, first_high * per_chunk)
-        image = jnp.dot(foot_of(feet, q, stripe), named, preferred_element_type=F32)
-        image_sq += jnp.sum((image * image).reshape(PIX_BLOCK // 8, 8, frames), axis=0)
+        image_sums[...] = image_sq
+
+    image_sq = image_sums[...]
+    for q in range(low_chunks * per_chunk - 2 * HB, stripe):
+        image_sq += image(q)
     both = jnp.concatenate(
         [
             jnp.sum(grad_sums[...], axis=0, keepdims=True),
@@ -634,7 +667,11 @@
             )
             + ((f32(neurons, frames),) if ends else ()),
             (pattern, z3, p3, rows, constants, pays, feet_ends, recording),
-            scratch,
+            [
+                *scratch,
+                pltpu.VMEM((8 * RIM * LANES, frames), BF16),
+                pltpu.VMEM((lines, LANES), F32),
+            ],
             keep=(s3[0],) if ends else (),
         )
         got_a, got_b = swapped(send_a, send_b)
@@ -670,6 +707,8 @@
                 pltpu.VMEM((halves[1] * LANES, frames), BF16),
                 *scratch[2:],
                 pltpu.VMEM((8, LANES), F32),
+                pltpu.VMEM((8, frames), F32),
+                pltpu.VMEM((2, lines, LANES), F32),
             ],
             keep=held,
         )

time: 79.6 us -> 79.7 us (level)
  no operation moved by 1% of the time
where the time goes in v5:
time: 79.7 us; the launch traced here: 79.4 us
  blocking collectives  26 us (33%)
  Pallas kernels  19.7 us (25%)
  waiting for transfers between devices  15.8 us (20%)
  starting transfers between devices  14.4 us (18%)
  local copies, waits for them, and re-layouts  2.58 us (3%)
  between operations  0.99 us (1%)
    all_to_all x2, blocking collectives, per_device(): stats = lax.all_to_all(stats, ('tile', 'tm'), 0, 0)  26 us
    pallas_call x13, Pallas kernels, call(): pl.pallas_call(body, name=name, out_shape=outs, in_specs=in_specs, out_sp...  19.7 us
    ppermute x12, waiting for transfers between devices, shared_blocks(): lax.ppermute(x, 'tm', [(i, i ^ bit) for i in range(size)])  15.8 us
    ppermute x3, starting transfers between devices, swapped(): lax.ppermute(first, 'tile', pairs(0))  8.01 us
    ppermute x12, starting transfers between devices, shared_blocks(): lax.ppermute(x, 'tm', [(i, i ^ bit) for i in range(size)])  4.41 us
    unnamed x12, local copies, waits for them, and re-layouts  2.58 us
    ppermute x3, starting transfers between devices, swapped(): lax.ppermute(second, 'tile', pairs(1))  1.96 us
  transfers between devices with their start and end apart: 18, of which 8 were waited for; matrix products, arithmetic and copies ran while one was open for 0% of the time, Pallas kernels for 10%

profile of v5, /device:TPU:0, one launch (start us, length us, event | category | flops | bytes accessed | tf_op | source)
XLA Modules:
  0.0 79.4 jit_solution(2980519898837780622)
XLA Ops:
  0.6 0.0 copy-start.4
  0.6 0.7 copy-done.4
  1.3 0.9 %rims.1 = (f32[136,128]{1,0:T(8,128)S(1)}, f32[136,128]{1,0:T(8,128)S(1)}, f32[16,128]{1,0:T(8,128)S(1)}) custom-call(f32[2048,128]{1,0:T(8,128)} %refs_0_.3, f32[16,128]{1,0:T(8,128)S(1)} %bitcast.9), custom_call_target="tpu_custom_call" | custom-call | flops 100000000 | bytes 3000000 | tf_op jit(solution)/shard_map/rims/pallas_call | solution.py:562
  2.2 3.0 %collective-permute-start = (f32[136,128]{1,0:T(8,128)S(1)}, f32[136,128]{1,0:T(8,128)S(1)}, u32[]{:S(2)}, u32[]{:S(2)}) collective-permute-start(f32[136,128]{1,0:T(8,128)S(1)} %get-tuple-element.49), channel_id=1, source_target_pairs={{0,1},{2,3},{4,5},{6,7},{1,0},{3,2},{5,4},{7,6},{8,9},{10,11},{12,... | collective-permute-start | bytes 208904 | tf_op jit(solution)/shard_map/ppermute | solution.py:586
  5.3 0.7 collective-permute-start.1
  5.9 0.0 copy-start.2
  5.9 1.2 %copy-done.2 = f32[2048,128]{1,0:T(8,128)S(1)} copy-done((f32[2048,128]{1,0:T(8,128)S(1)}, f32[2048,128]{1,0:T(8,128)}, u32[]{:S(2)}) %copy-start.2) | copy-done | bytes 1048600
  7.2 0.0 copy-start.5
  7.2 0.7 copy-done.5
  7.8 0.0 copy-start.1
  7.8 0.0 copy-start.3
  7.8 1.4 %prep_own.1 = (f32[16,128,128]{2,1,0:T(8,128)S(1)}, f32[16,128,128]{2,1,0:T(8,128)S(1)}, f32[16,128,128]{2,1,0:T(8,128)S(1)}, f32[16,128,128]{2,1,0:T(8,128)S(1)...) custom-call(f32[2048,128]{1,0:T(8,128)S(1)} %copy-done.2, ...), custom_call_target="tpu_custom_call" | custom-call | flops 160000000 | bytes 4800000 | tf_op jit(solution)/shard_map/prep_own/pallas_call | solution.py:562
  9.3 0.0 collective-permute-done.refs_0_
  9.3 0.0 collective-permute-done.1.refs_1_
  9.3 0.3 prep_rim.1
  9.6 1.6 %collective-permute-start.2 = (f32[2,24,128]{2,1,0:T(8,128)S(1)}, f32[2,24,128]{2,1,0:T(8,128)S(1)}, u32[]{:S(2)}, u32[]{:S(2)}) collective-permute-start(f32[2,24,128]{2,1,0:T(8,128)S(1)} %get-tuple-element.62.refs_4__0_.refs_5__0_.refs_6__0_), channel_id=1, source_target_pairs={{0,16},{8,24},{16,0},{24,8},{1,17},{9,25},{17,1},{25,9},{2,18},{10... | collective-permute-start | bytes 73736 | tf_op jit(solution)/shard_map/ppermute | solution.py:594
  11.1 0.0 collective-permute-start.3
  11.1 2.3 %collective-permute-done.2.refs_4__1_.refs_5__1_.refs_6__1_ = f32[2,24,128]{2,1,0:T(8,128)S(1)} collective-permute-done((f32[2,24,128]{2,1,0:T(8,128)S(1)}, f32[2,24,128]{2,1,0:T(8,128)S(1)}, u32[]{:S(2)}, u32[]{:S(2)}) %collective-permute-start.2) | collective-permute-done | bytes 24608 | tf_op jit(solution)/shard_map/ppermute | solution.py:594
  13.5 0.0 collective-permute-start.4
  13.5 0.0 collective-permute-done.3.refs_4__2_.refs_5__2_.refs_6__2_
  13.5 1.2 %collective-permute-done.4.refs_4__3_.refs_5__3_.refs_6__3_ = f32[2,24,128]{2,1,0:T(8,128)S(1)} collective-permute-done((f32[2,24,128]{2,1,0:T(8,128)S(1)}, f32[2,24,128]{2,1,0:T(8,128)S(1)}, u32[]{:S(2)}, u32[]{:S(2)}) %collective-permute-start.4) | collective-permute-done | bytes 24608 | tf_op jit(solution)/shard_map/ppermute | solution.py:594
  14.7 0.0 copy-done.1
  14.7 0.0 copy-done.3
  14.7 0.0 copy-start
  14.7 1.7 %edge.2 = (bf16[2304,128]{1,0:T(8,128)(2,1)S(1)}, f32[4,128,128]{2,1,0:T(8,128)S(1)}, f32[4,128,128]{2,1,0:T(8,128)S(1)}, bf16[2,128,128]{2,1,0:T(8,128)(2,1)S(1)}, bf16[2,128,128]{2,1,0:T(8,128)(2,1)S(1)}) custom-call(s32[4,32]{1,0:T(4,128)S(1)} %bitcast.3, f32[16,128,128]{2,1,0:T(8,128)S(1)} %get-tuple-element.60.refs_1__0_, ...), custom_call_target="tpu_custom_call" | custom-call | flops 250000000 | bytes 7500000 | tf_op jit(solution)/shard_map/edge/pallas_call | solution.py:562
  16.3 4.3 %collective-permute-start.5 = (bf16[2,128,128]{2,1,0:T(8,128)(2,1)S(1)}, bf16[2,128,128]{2,1,0:T(8,128)(2,1)S(1)}, u32[]{:S(2)}, u32[]{:S(2)}) collective-permute-start(bf16[2,128,128]{2,1,0:T(8,128)(2,1)S(1)} %get-tuple-element.68), channel_id=1, source_target_pairs={{0,1},{2,3},{4,5},{6,7},{1,0},{3,2},{5,4},{7,6},{8,9},{10,11},{12,... | collective-permute-start | bytes 196616 | tf_op jit(solution)/shard_map/ppermute | solution.py:586
  20.7 0.7 collective-permute-start.6
  21.4 0.0 copy-done
  21.4 3.3 %inner.2 = (f32[14,128,128]{2,1,0:T(8,128)S(1)}, f32[2,24,128]{2,1,0:T(8,128)S(1)}) custom-call(s32[4,32]{1,0:T(4,128)S(1)} %bitcast.4, f32[16,128,128]{2,1,0:T(8,128)S(1)} %get-tuple-element.55.refs_2__0_.refs_1__0_.refs_3__0_, f32[2,128,128]{2,1,0:T(8,128)S(1)} %get-tuple-element.56.refs_2__1_.refs_1__1_.refs_3__1_, ...), custom_call_target="tpu_custom_call" | custom-call | flops 400000000 | bytes 12000000 | tf_op jit(solution)/shard_map/inner/pallas_call | solution.py:562
  24.7 0.0 collective-permute-done.5.refs_1_
  24.7 0.0 collective-permute-done.6.refs_2_
  24.7 0.3 border.2
  25.0 1.6 %collective-permute-start.7 = (f32[2,24,128]{2,1,0:T(8,128)S(1)}, f32[2,24,128]{2,1,0:T(8,128)S(1)}, u32[]{:S(2)}, u32[]{:S(2)}) collective-permute-start(f32[2,24,128]{2,1,0:T(8,128)S(1)} %get-tuple-element.72.refs_7__0_), channel_id=1, source_target_pairs={{0,16},{8,24},{16,0},{24,8},{1,17},{9,25},{17,1},{25,9},{2,18},{10... | collective-permute-start | bytes 73736 | tf_op jit(solution)/shard_map/ppermute | solution.py:594
  26.5 0.0 collective-permute-start.8
  26.5 2.3 %collective-permute-done.7.refs_7__1_ = f32[2,24,128]{2,1,0:T(8,128)S(1)} collective-permute-done((f32[2,24,128]{2,1,0:T(8,128)S(1)}, f32[2,24,128]{2,1,0:T(8,128)S(1)}, u32[]{:S(2)}, u32[]{:S(2)}) %collective-permute-start.7) | collective-permute-done | bytes 24608 | tf_op jit(solution)/shard_map/ppermute | solution.py:594
  28.9 0.0 collective-permute-start.9
  28.9 0.0 collective-permute-done.8.refs_7__2_
  28.9 1.2 %collective-permute-done.9.refs_7__3_ = f32[2,24,128]{2,1,0:T(8,128)S(1)} collective-permute-done((f32[2,24,128]{2,1,0:T(8,128)S(1)}, f32[2,24,128]{2,1,0:T(8,128)S(1)}, u32[]{:S(2)}, u32[]{:S(2)}) %collective-permute-start.9) | collective-permute-done | bytes 24608 | tf_op jit(solution)/shard_map/ppermute | solution.py:594
  30.1 2.2 %direction.2 = (f32[18,128,128]{2,1,0:T(8,128)S(1)}, f32[32,2,128]{2,1,0:T(2,128)S(1)}) custom-call(s32[4,32]{1,0:T(4,128)S(1)} %bitcast.5, f32[14,128,128]{2,1,0:T(8,128)S(1)} %get-tuple-element.66.refs_1_, f32[4,128,128]{2,1,0:T(8,128)S(1)} %get-tuple-element.71.refs_2_, f32[16,128,128]{2,1,0:T(8,128)S(1)} %get-tuple-element.55.refs_2__0_.refs_1__0_.refs_3__0_, ...), custom_call_target="tpu_custom_call" | custom-call | flops 400000000 | bytes 12000000 | tf_op jit(solution)/shard_map/direction/pallas_call | solution.py:562
  32.2 14.2 %all_to_all.10.refs_2_ = f32[32,2,128]{2,1,0:T(2,128)S(1)} all-to-all(f32[32,2,128]{2,1,0:T(2,128)S(1)} %get-tuple-element.74), channel_id=1, replica_groups=mesh['tm'=4,'tile'=8] {'tile','tm'}, dimensions={0} | all-to-all | bytes 65536 | tf_op jit(solution)/shard_map/all_to_all | solution.py:715
  46.5 0.7 update.1
  47.2 0.6 collective-permute-start.10
  47.7 0.0 collective-permute-start.11
  47.8 3.2 %collective-permute-done.10.refs_5__1_ = f32[1,24,128]{2,1,0:T(8,128)S(1)} collective-permute-done((f32[1,24,128]{2,1,0:T(8,128)S(1)}, f32[1,24,128]{2,1,0:T(8,128)S(1)}, u32[]{:S(2)}, u32[]{:S(2)}) %collective-permute-start.10) | collective-permute-done | bytes 12320 | tf_op jit(solution)/shard_map/ppermute | solution.py:594
  50.9 0.0 collective-permute-start.12
  51.0 0.0 collective-permute-done.11.refs_5__2_
  51.0 1.2 %collective-permute-done.12.refs_5__3_ = f32[1,24,128]{2,1,0:T(8,128)S(1)} collective-permute-done((f32[1,24,128]{2,1,0:T(8,128)S(1)}, f32[1,24,128]{2,1,0:T(8,128)S(1)}, u32[]{:S(2)}, u32[]{:S(2)}) %collective-permute-start.12) | collective-permute-done | bytes 12320 | tf_op jit(solution)/shard_map/ppermute | solution.py:594
  52.1 1.7 %edge.3 = (bf16[2304,128]{1,0:T(8,128)(2,1)S(1)}, f32[4,128,128]{2,1,0:T(8,128)S(1)}, f32[4,128,128]{2,1,0:T(8,128)S(1)}, bf16[2,128,128]{2,1,0:T(8,128)(2,1)S(1...) custom-call(s32[4,32]{1,0:T(4,128)S(1)} %bitcast.6, f32[16,128,128]{2,1,0:T(8,128)S(1)} %get-tuple-element.76.refs_1__0_, ...), custom_call_target="tpu_custom_call" | custom-call | flops 250000000 | bytes 7500000 | tf_op jit(solution)/shard_map/edge/pallas_call | solution.py:562
  53.8 0.6 collective-permute-start.13
  54.4 0.7 collective-permute-start.14
  55.1 3.5 %inner.3 = (f32[14,128,128]{2,1,0:T(8,128)S(1)}, f32[2,24,128]{2,1,0:T(8,128)S(1)}, f32[2048,128]{1,0:T(8,128)}) custom-call(s32[4,32]{1,0:T(4,128)S(1)} %bitcast.7, f32[16,128,128]{2,1,0:T(8,128)S(1)} %get-tuple-element.55.refs_2__0_.refs_1__0_.refs_3__0_, f32[2,128,128]{2,1,0:T(8,128)S(1)} %get-tuple-element.56.refs_2__1_.refs_1__1_.refs_3__1_, ...), custom_call_target="tpu_custom_call" | custom-call | flops 400000000 | bytes 12000000 | tf_op jit(solution)/shard_map/inner/pallas_call | solution.py:562
  58.7 0.0 collective-permute-done.13.refs_1_
  58.7 0.0 collective-permute-done.14.refs_2_
  58.7 0.3 border.3
  58.9 0.7 collective-permute-start.15
  59.7 0.0 collective-permute-start.16
  59.7 3.2 %collective-permute-done.15.refs_7__1_ = f32[2,24,128]{2,1,0:T(8,128)S(1)} collective-permute-done((f32[2,24,128]{2,1,0:T(8,128)S(1)}, f32[2,24,128]{2,1,0:T(8,128)S(1)}, u32[]{:S(2)}, u32[]{:S(2)}) %collective-permute-start.15) | collective-permute-done | bytes 24608 | tf_op jit(solution)/shard_map/ppermute | solution.py:594
  62.8 0.0 collective-permute-start.17
  62.8 0.0 collective-permute-done.16.refs_7__2_
  62.8 1.2 %collective-permute-done.17.refs_7__3_ = f32[2,24,128]{2,1,0:T(8,128)S(1)} collective-permute-done((f32[2,24,128]{2,1,0:T(8,128)S(1)}, f32[2,24,128]{2,1,0:T(8,128)S(1)}, u32[]{:S(2)}, u32[]{:S(2)}) %collective-permute-start.17) | collective-permute-done | bytes 24608 | tf_op jit(solution)/shard_map/ppermute | solution.py:594
  64.0 2.2 %direction.3 = (f32[18,128,128]{2,1,0:T(8,128)S(1)}, f32[32,2,128]{2,1,0:T(2,128)S(1)}) custom-call(s32[4,32]{1,0:T(4,128)S(1)} %bitcast.8, f32[14,128,128]{2,1,0:T(8,128)S(1)} %get-tuple-element.82.refs_1_, f32[4,128,128]{2,1,0:T(8,128)S(1)} %get-tuple-element.87.refs_2_, f32[16,128,128]{2,1,0:T(8,128)S(1)} %get-tuple-element.55.refs_2__0_.refs_1__0_.refs_3__0_, ...), custom_call_target="tpu_custom_call" | custom-call | flops 400000000 | bytes 12000000 | tf_op jit(solution)/shard_map/direction/pallas_call | solution.py:562
  66.2 11.8 %all_to_all.11.refs_2_ = f32[32,2,128]{2,1,0:T(2,128)S(1)} all-to-all(f32[32,2,128]{2,1,0:T(2,128)S(1)} %get-tuple-element.90), channel_id=1, replica_groups=mesh['tm'=4,'tile'=8] {'tile','tm'}, dimensions={0} | all-to-all | bytes 65536 | tf_op jit(solution)/shard_map/all_to_all | solution.py:715
  78.0 1.3 %final.1 = f32[2048,128]{1,0:T(8,128)} custom-call(f32[16,128,128]{2,1,0:T(8,128)S(1)} %get-tuple-element.75.refs_8__0_.refs_9__0_.refs_7__0_.refs_0_, f32[18,128,128]{2,1,0:T(8,128)S(1)} %get-tuple-element.89.refs_1_, f32[32,2,128]{2,1,0:T(2,128)S(1)} %all_to_all.11.refs_2_), custom_call_target="tpu_custom_call" | custom-call | flops 140000000 | bytes 4200000 | tf_op jit(solution)/shard_map/final/pallas_call | solution.py:562
Async XLA Ops:
  0.6 0.7 copy-start.4
  2.2 7.0 %collective-permute-start = (f32[136,128]{1,0:T(8,128)S(1)}, f32[136,128]{1,0:T(8,128)S(1)}, u32[]{:S(2)}, u32[]{:S(2)}) collective-permute-start(f32[136,128]{1,0:T(8,128)S(1)} %get-tuple-element.49), channel_id=1, source_target_pairs={{0,1},{2,3},{4,5},{6,7},{1,0},{3,2},{5,4},{7,6},{8,9},{10,11},{12,... | collective-permute-start | bytes 208904 | tf_op jit(solution)/shard_map/ppermute | solution.py:586
  5.3 4.0 %collective-permute-start.1 = (f32[136,128]{1,0:T(8,128)S(1)}, f32[136,128]{1,0:T(8,128)S(1)}, u32[]{:S(2)}, u32[]{:S(2)}) collective-permute-start(f32[136,128]{1,0:T(8,128)S(1)} %get-tuple-element.50), channel_id=1, source_target_pairs={{1,2},{3,4},{5,6},{2,1},{4,3},{6,5},{9,10},{11,12},{13,14},{10,9},... | collective-permute-start | bytes 208904 | tf_op jit(solution)/shard_map/ppermute | solution.py:586
  5.9 1.2 %copy-start.2 = (f32[2048,128]{1,0:T(8,128)S(1)}, f32[2048,128]{1,0:T(8,128)}, u32[]{:S(2)}) copy-start(f32[2048,128]{1,0:T(8,128)} %refs_0_.3) | copy-start | bytes 3145732
  7.2 0.7 copy-start.5
  7.8 6.8 %copy-start.1 = (bf16[8192,128]{1,0:T(8,128)(2,1)S(1)}, bf16[8192,128]{1,0:T(8,128)(2,1)}, u32[]{:S(2)}) copy-start(bf16[8192,128]{1,0:T(8,128)(2,1)} %refs_7_.7) | copy-start | bytes 6291460
  7.8 6.8 %copy-start.3 = (s32[32,4]{0,1:T(4,128)S(1)}, s32[32,4]{0,1:T(4,128)}, u32[]{:S(2)}) copy-start(s32[32,4]{0,1:T(4,128)} %param.8) | copy-start | bytes 1540
  9.6 3.9 %collective-permute-start.2 = (f32[2,24,128]{2,1,0:T(8,128)S(1)}, f32[2,24,128]{2,1,0:T(8,128)S(1)}, u32[]{:S(2)}, u32[]{:S(2)}) collective-permute-start(f32[2,24,128]{2,1,0:T(8,128)S(1)} %get-tuple-element.62.refs_4__0_.refs_5__0_.refs_6__0_), channel_id=1, source_target_pairs={{0,16},{8,24},{16,0},{24,8},{1,17},{9,25},{17,1},{25,9},{2,18},{10... | collective-permute-start | bytes 73736 | tf_op jit(solution)/shard_map/ppermute | solution.py:594
  11.1 2.3 %collective-permute-start.3 = (f32[2,24,128]{2,1,0:T(8,128)S(1)}, f32[2,24,128]{2,1,0:T(8,128)S(1)}, u32[]{:S(2)}, u32[]{:S(2)}) collective-permute-start(f32[2,24,128]{2,1,0:T(8,128)S(1)} %get-tuple-element.62.refs_4__0_.refs_5__0_.refs_6__0_), channel_id=1, source_target_pairs={{0,8},{8,0},{16,24},{24,16},{1,9},{9,1},{17,25},{25,17},{2,10},{10... | collective-permute-start | bytes 73736 | tf_op jit(solution)/shard_map/ppermute | solution.py:594
  13.5 1.2 %collective-permute-start.4 = (f32[2,24,128]{2,1,0:T(8,128)S(1)}, f32[2,24,128]{2,1,0:T(8,128)S(1)}, u32[]{:S(2)}, u32[]{:S(2)}) collective-permute-start(f32[2,24,128]{2,1,0:T(8,128)S(1)} %collective-permute-done.2.refs_4__1_.refs_5__1_.refs_6__1_), channel_id=1, source_target_pairs={{0,8},{8,0},{16,24},{24,16},{1,9},{9,1},{17,25},{25,17},{2,10},{10... | collective-permute-start | bytes 73736 | tf_op jit(solution)/shard_map/ppermute | solution.py:594
  14.7 6.7 %copy-start = (bf16[8192,256]{1,0:T(8,128)(2,1)S(1)}, bf16[8192,256]{1,0:T(8,128)(2,1)}, u32[]{:S(2)}) copy-start(bf16[8192,256]{1,0:T(8,128)(2,1)} %refs_8_.3) | copy-start | bytes 12582916
  16.3 8.3 %collective-permute-start.5 = (bf16[2,128,128]{2,1,0:T(8,128)(2,1)S(1)}, bf16[2,128,128]{2,1,0:T(8,128)(2,1)S(1)}, u32[]{:S(2)}, u32[]{:S(2)}) collective-permute-start(bf16[2,128,128]{2,1,0:T(8,128)(2,1)S(1)} %get-tuple-element.68), channel_id=1, source_target_pairs={{0,1},{2,3},{4,5},{6,7},{1,0},{3,2},{5,4},{7,6},{8,9},{10,11},{12,... | collective-permute-start | bytes 196616 | tf_op jit(solution)/shard_map/ppermute | solution.py:586
  20.7 4.0 %collective-permute-start.6 = (bf16[2,128,128]{2,1,0:T(8,128)(2,1)S(1)}, bf16[2,128,128]{2,1,0:T(8,128)(2,1)S(1)}, u32[]{:S(2)}, u32[]{:S(2)}) collective-permute-start(bf16[2,128,128]{2,1,0:T(8,128)(2,1)S(1)} %get-tuple-element.69), channel_id=1, source_target_pairs={{1,2},{3,4},{5,6},{2,1},{4,3},{6,5},{9,10},{11,12},{13,14},{10,9},... | collective-permute-start | bytes 196616 | tf_op jit(solution)/shard_map/ppermute | solution.py:586
  25.0 3.9 %collective-permute-start.7 = (f32[2,24,128]{2,1,0:T(8,128)S(1)}, f32[2,24,128]{2,1,0:T(8,128)S(1)}, u32[]{:S(2)}, u32[]{:S(2)}) collective-permute-start(f32[2,24,128]{2,1,0:T(8,128)S(1)} %get-tuple-element.72.refs_7__0_), channel_id=1, source_target_pairs={{0,16},{8,24},{16,0},{24,8},{1,17},{9,25},{17,1},{25,9},{2,18},{10... | collective-permute-start | bytes 73736 | tf_op jit(solution)/shard_map/ppermute | solution.py:594
  26.5 2.3 %collective-permute-start.8 = (f32[2,24,128]{2,1,0:T(8,128)S(1)}, f32[2,24,128]{2,1,0:T(8,128)S(1)}, u32[]{:S(2)}, u32[]{:S(2)}) collective-permute-start(f32[2,24,128]{2,1,0:T(8,128)S(1)} %get-tuple-element.72.refs_7__0_), channel_id=1, source_target_pairs={{0,8},{8,0},{16,24},{24,16},{1,9},{9,1},{17,25},{25,17},{2,10},{10... | collective-permute-start | bytes 73736 | tf_op jit(solution)/shard_map/ppermute | solution.py:594
  28.9 1.2 %collective-permute-start.9 = (f32[2,24,128]{2,1,0:T(8,128)S(1)}, f32[2,24,128]{2,1,0:T(8,128)S(1)}, u32[]{:S(2)}, u32[]{:S(2)}) collective-permute-start(f32[2,24,128]{2,1,0:T(8,128)S(1)} %collective-permute-done.7.refs_7__1_), channel_id=1, source_target_pairs={{0,8},{8,0},{16,24},{24,16},{1,9},{9,1},{17,25},{25,17},{2,10},{10... | collective-permute-start | bytes 73736 | tf_op jit(solution)/shard_map/ppermute | solution.py:594
  47.2 3.8 %collective-permute-start.10 = (f32[1,24,128]{2,1,0:T(8,128)S(1)}, f32[1,24,128]{2,1,0:T(8,128)S(1)}, u32[]{:S(2)}, u32[]{:S(2)}) collective-permute-start(f32[1,24,128]{2,1,0:T(8,128)S(1)} %get-tuple-element.78.refs_5__0_), channel_id=1, source_target_pairs={{0,16},{8,24},{16,0},{24,8},{1,17},{9,25},{17,1},{25,9},{2,18},{10... | collective-permute-start | bytes 36872 | tf_op jit(solution)/shard_map/ppermute | solution.py:594
  47.7 3.2 %collective-permute-start.11 = (f32[1,24,128]{2,1,0:T(8,128)S(1)}, f32[1,24,128]{2,1,0:T(8,128)S(1)}, u32[]{:S(2)}, u32[]{:S(2)}) collective-permute-start(f32[1,24,128]{2,1,0:T(8,128)S(1)} %get-tuple-element.78.refs_5__0_), channel_id=1, source_target_pairs={{0,8},{8,0},{16,24},{24,16},{1,9},{9,1},{17,25},{25,17},{2,10},{10... | collective-permute-start | bytes 36872 | tf_op jit(solution)/shard_map/ppermute | solution.py:594
  50.9 1.2 %collective-permute-start.12 = (f32[1,24,128]{2,1,0:T(8,128)S(1)}, f32[1,24,128]{2,1,0:T(8,128)S(1)}, u32[]{:S(2)}, u32[]{:S(2)}) collective-permute-start(f32[1,24,128]{2,1,0:T(8,128)S(1)} %collective-permute-done.10.refs_5__1_), channel_id=1, source_target_pairs={{0,8},{8,0},{16,24},{24,16},{1,9},{9,1},{17,25},{25,17},{2,10},{10... | collective-permute-start | bytes 36872 | tf_op jit(solution)/shard_map/ppermute | solution.py:594
  53.8 4.8 %collective-permute-start.13 = (bf16[2,128,128]{2,1,0:T(8,128)(2,1)S(1)}, bf16[2,128,128]{2,1,0:T(8,128)(2,1)S(1)}, u32[]{:S(2)}, u32[]{:S(2)}) collective-permute-start(bf16[2,128,128]{2,1,0:T(8,128)(2,1)S(1)} %get-tuple-element.84), channel_id=1, source_target_pairs={{0,1},{2,3},{4,5},{6,7},{1,0},{3,2},{5,4},{7,6},{8,9},{10,11},{12,... | collective-permute-start | bytes 196616 | tf_op jit(solution)/shard_map/ppermute | solution.py:586
  54.4 4.2 %collective-permute-start.14 = (bf16[2,128,128]{2,1,0:T(8,128)(2,1)S(1)}, bf16[2,128,128]{2,1,0:T(8,128)(2,1)S(1)}, u32[]{:S(2)}, u32[]{:S(2)}) collective-permute-start(bf16[2,128,128]{2,1,0:T(8,128)(2,1)S(1)} %get-tuple-element.85), channel_id=1, source_target_pairs={{1,2},{3,4},{5,6},{2,1},{4,3},{6,5},{9,10},{11,12},{13,14},{10,9},... | collective-permute-start | bytes 196616 | tf_op jit(solution)/shard_map/ppermute | solution.py:586
  58.9 3.9 %collective-permute-start.15 = (f32[2,24,128]{2,1,0:T(8,128)S(1)}, f32[2,24,128]{2,1,0:T(8,128)S(1)}, u32[]{:S(2)}, u32[]{:S(2)}) collective-permute-start(f32[2,24,128]{2,1,0:T(8,128)S(1)} %get-tuple-element.88.refs_7__0_), channel_id=1, source_target_pairs={{0,16},{8,24},{16,0},{24,8},{1,17},{9,25},{17,1},{25,9},{2,18},{10... | collective-permute-start | bytes 73736 | tf_op jit(solution)/shard_map/ppermute | solution.py:594
  59.7 3.2 %collective-permute-start.16 = (f32[2,24,128]{2,1,0:T(8,128)S(1)}, f32[2,24,128]{2,1,0:T(8,128)S(1)}, u32[]{:S(2)}, u32[]{:S(2)}) collective-permute-start(f32[2,24,128]{2,1,0:T(8,128)S(1)} %get-tuple-element.88.refs_7__0_), channel_id=1, source_target_pairs={{0,8},{8,0},{16,24},{24,16},{1,9},{9,1},{17,25},{25,17},{2,10},{10... | collective-permute-start | bytes 73736 | tf_op jit(solution)/shard_map/ppermute | solution.py:594
  62.8 1.2 %collective-permute-start.17 = (f32[2,24,128]{2,1,0:T(8,128)S(1)}, f32[2,24,128]{2,1,0:T(8,128)S(1)}, u32[]{:S(2)}, u32[]{:S(2)}) collective-permute-start(f32[2,24,128]{2,1,0:T(8,128)S(1)} %collective-permute-done.15.refs_7__1_), channel_id=1, source_target_pairs={{0,8},{8,0},{16,24},{24,16},{1,9},{9,1},{17,25},{25,17},{2,10},{10... | collective-permute-start | bytes 73736 | tf_op jit(solution)/shard_map/ppermute | solution.py:594

commit v6 on v4

--- a/solution.py
+++ b/solution.py
@@ -196,22 +196,13 @@
         prep_chunk(c, rate, field, shared, *at, rows, pay)
 
 
-def distances(size):
-    found = [0]
-    bit = size // 2
-    while bit:
-        found += [other ^ bit for other in found]
-        bit //= 2
-    return found
-
-
 def by_block(parts, me, index):
     values = [part[index] for part in parts]
     ordered = []
     for m in range(len(values)):
         value = values[0]
-        for distance, other in zip(distances(len(values))[1:], values[1:]):
-            value = jnp.where(me == m ^ distance, other, value)
+        for j in range(1, len(values)):
+            value = jnp.where(me == m ^ j, values[j], value)
         ordered.append(value)
     return ordered
 
@@ -555,12 +546,11 @@
 
 def shared_blocks(value):
     size = lax.axis_size("tm")
-    known = [value]
-    bit = size // 2
-    while bit:
-        known += [lax.ppermute(x, "tm", [(i, i ^ bit) for i in range(size)]) for x in known]
-        bit //= 2
-    return tuple(known)
+    others = [
+        lax.ppermute(value, "tm", [(i, i ^ j) for i in range(size)])
+        for j in reversed(range(1, size))
+    ]
+    return (value, *reversed(others))
 
 
 def per_device(recording, footprints, pattern, decay, frame_gain, spikes):

time: 79.6 us -> 76.3 us (0.959)
  waiting for transfers between devices: 15.8 us -> 9.03 us
  starting transfers between devices: 14.4 us -> 17.2 us
    ppermute x12, waiting for transfers between devices: 15.8 us -> 9.01 us  [shared_blocks(): lax.ppermute(value, 'tm', [(i, i ^ j) for i in range(size)])]
    ppermute x12, starting transfers between devices: 4.4 us -> 7.73 us  [shared_blocks(): lax.ppermute(value, 'tm', [(i, i ^ j) for i in range(size)])]
  transfers between devices with their start and end apart: 18 -> 18, of which waited for: 8 -> 8; matrix products, arithmetic and copies ran while one was open for 0% -> 0% of each run, Pallas kernels for 10% -> 11%
where the time goes in v6:
time: 76.3 us; the launch traced here: 75.9 us
  blocking collectives  26.5 us (35%)
  Pallas kernels  19.6 us (26%)
  starting transfers between devices  17.2 us (23%)
  waiting for transfers between devices  9.03 us (12%)
  local copies, waits for them, and re-layouts  2.58 us (3%)
  between operations  1.01 us (1%)
    all_to_all x2, blocking collectives, per_device(): stats = lax.all_to_all(stats, ('tile', 'tm'), 0, 0)  26.5 us
    pallas_call x13, Pallas kernels, call(): pl.pallas_call(body, name=name, out_shape=outs, in_specs=in_specs, out_sp...  19.6 us
    ppermute x12, waiting for transfers between devices, shared_blocks(): lax.ppermute(value, 'tm', [(i, i ^ j) for i in range(size)])  9.01 us
    ppermute x12, starting transfers between devices, shared_blocks(): lax.ppermute(value, 'tm', [(i, i ^ j) for i in range(size)])  7.73 us
    ppermute x3, starting transfers between devices, swapped(): lax.ppermute(first, 'tile', pairs(0))  7.51 us
    unnamed x12, local copies, waits for them, and re-layouts  2.58 us
    ppermute x3, starting transfers between devices, swapped(): lax.ppermute(second, 'tile', pairs(1))  1.96 us
  transfers between devices with their start and end apart: 18, of which 8 were waited for; matrix products, arithmetic and copies ran while one was open for 0% of the time, Pallas kernels for 11%

profile of v6, /device:TPU:0, one launch (start us, length us, event | category | flops | bytes accessed | tf_op | source)
XLA Modules:
  0.0 75.9 jit_solution(14353287615902828707)
XLA Ops:
  0.6 0.0 copy-start.4
  0.6 0.7 copy-done.4
  1.3 0.9 %rims.1 = (f32[136,128]{1,0:T(8,128)S(1)}, f32[136,128]{1,0:T(8,128)S(1)}, f32[16,128]{1,0:T(8,128)S(1)}) custom-call(f32[2048,128]{1,0:T(8,128)} %refs_0_.3, f32[16,128]{1,0:T(8,128)S(1)} %bitcast.9), custom_call_target="tpu_custom_call" | custom-call | flops 100000000 | bytes 3000000 | tf_op jit(solution)/shard_map/rims/pallas_call | solution.py:520
  2.2 3.0 %collective-permute-start = (f32[136,128]{1,0:T(8,128)S(1)}, f32[136,128]{1,0:T(8,128)S(1)}, u32[]{:S(2)}, u32[]{:S(2)}) collective-permute-start(f32[136,128]{1,0:T(8,128)S(1)} %get-tuple-element.49), channel_id=1, source_target_pairs={{0,1},{2,3},{4,5},{6,7},{1,0},{3,2},{5,4},{7,6},{8,9},{10,11},{12,... | collective-permute-start | bytes 208904 | tf_op jit(solution)/shard_map/ppermute | solution.py:544
  5.3 0.7 collective-permute-start.1
  5.9 0.0 copy-start.2
  5.9 1.2 %copy-done.2 = f32[2048,128]{1,0:T(8,128)S(1)} copy-done((f32[2048,128]{1,0:T(8,128)S(1)}, f32[2048,128]{1,0:T(8,128)}, u32[]{:S(2)}) %copy-start.2) | copy-done | bytes 1048600
  7.2 0.0 copy-start.5
  7.2 0.7 copy-done.5
  7.8 0.0 copy-start.1
  7.8 0.0 copy-start.3
  7.8 1.4 %prep_own.1 = (f32[16,128,128]{2,1,0:T(8,128)S(1)}, f32[16,128,128]{2,1,0:T(8,128)S(1)}, f32[16,128,128]{2,1,0:T(8,128)S(1)}, f32[16,128,128]{2,1,0:T(8,128)S(1)...) custom-call(f32[2048,128]{1,0:T(8,128)S(1)} %copy-done.2, ...), custom_call_target="tpu_custom_call" | custom-call | flops 160000000 | bytes 4800000 | tf_op jit(solution)/shard_map/prep_own/pallas_call | solution.py:520
  9.3 0.0 collective-permute-done.refs_0_
  9.3 0.0 collective-permute-done.1.refs_1_
  9.3 0.3 prep_rim.1
  9.6 0.7 collective-permute-start.4
  10.3 0.9 %collective-permute-start.3 = (f32[2,24,128]{2,1,0:T(8,128)S(1)}, f32[2,24,128]{2,1,0:T(8,128)S(1)}, u32[]{:S(2)}, u32[]{:S(2)}) collective-permute-start(f32[2,24,128]{2,1,0:T(8,128)S(1)} %get-tuple-element.62.refs_4__0_.refs_5__0_.refs_6__0_), channel_id=1, source_target_pairs={{0,16},{8,24},{16,0},{24,8},{1,17},{9,25},{17,1},{25,9},{2,18},{10... | collective-permute-start | bytes 73736 | tf_op jit(solution)/shard_map/ppermute | solution.py:550
  11.2 0.3 collective-permute-start.2
  11.5 1.6 %collective-permute-done.4.refs_4__3_.refs_5__3_.refs_6__3_ = f32[2,24,128]{2,1,0:T(8,128)S(1)} collective-permute-done((f32[2,24,128]{2,1,0:T(8,128)S(1)}, f32[2,24,128]{2,1,0:T(8,128)S(1)}, u32[]{:S(2)}, u32[]{:S(2)}) %collective-permute-start.4) | collective-permute-done | bytes 24608 | tf_op jit(solution)/shard_map/ppermute | solution.py:550
  13.1 1.3 %collective-permute-done.3.refs_4__2_.refs_5__2_.refs_6__2_ = f32[2,24,128]{2,1,0:T(8,128)S(1)} collective-permute-done((f32[2,24,128]{2,1,0:T(8,128)S(1)}, f32[2,24,128]{2,1,0:T(8,128)S(1)}, u32[]{:S(2)}, u32[]{:S(2)}) %collective-permute-start.3) | collective-permute-done | bytes 24608 | tf_op jit(solution)/shard_map/ppermute | solution.py:550
  14.4 0.0 collective-permute-done.2.refs_4__1_.refs_5__1_.refs_6__1_
  14.4 0.0 copy-done.1
  14.4 0.0 copy-done.3
  14.4 0.0 copy-start
  14.4 1.7 %edge.2 = (bf16[2304,128]{1,0:T(8,128)(2,1)S(1)}, f32[4,128,128]{2,1,0:T(8,128)S(1)}, f32[4,128,128]{2,1,0:T(8,128)S(1)}, bf16[2,128,128]{2,1,0:T(8,128)(2,1)S(1)}, bf16[2,128,128]{2,1,0:T(8,128)(2,1)S(1)}) custom-call(s32[4,32]{1,0:T(4,128)S(1)} %bitcast.3, f32[16,128,128]{2,1,0:T(8,128)S(1)} %get-tuple-element.60.refs_1__0_, ...), custom_call_target="tpu_custom_call" | custom-call | flops 250000000 | bytes 7500000 | tf_op jit(solution)/shard_map/edge/pallas_call | solution.py:520
  16.1 3.8 %collective-permute-start.5 = (bf16[2,128,128]{2,1,0:T(8,128)(2,1)S(1)}, bf16[2,128,128]{2,1,0:T(8,128)(2,1)S(1)}, u32[]{:S(2)}, u32[]{:S(2)}) collective-permute-start(bf16[2,128,128]{2,1,0:T(8,128)(2,1)S(1)} %get-tuple-element.68), channel_id=1, source_target_pairs={{0,1},{2,3},{4,5},{6,7},{1,0},{3,2},{5,4},{7,6},{8,9},{10,11},{12,... | collective-permute-start | bytes 196616 | tf_op jit(solution)/shard_map/ppermute | solution.py:544
  19.9 0.7 collective-permute-start.6
  20.6 0.0 copy-done
  20.6 3.3 %inner.2 = (f32[14,128,128]{2,1,0:T(8,128)S(1)}, f32[2,24,128]{2,1,0:T(8,128)S(1)}) custom-call(s32[4,32]{1,0:T(4,128)S(1)} %bitcast.4, f32[16,128,128]{2,1,0:T(8,128)S(1)} %get-tuple-element.55.refs_2__0_.refs_1__0_.refs_3__0_, f32[2,128,128]{2,1,0:T(8,128)S(1)} %get-tuple-element.56.refs_2__1_.refs_1__1_.refs_3__1_, ...), custom_call_target="tpu_custom_call" | custom-call | flops 400000000 | bytes 12000000 | tf_op jit(solution)/shard_map/inner/pallas_call | solution.py:520
  23.9 0.0 collective-permute-done.5.refs_1_
  23.9 0.0 collective-permute-done.6.refs_2_
  23.9 0.3 border.2
  24.2 0.1 collective-permute-start.9
  24.3 1.5 %collective-permute-start.8 = (f32[2,24,128]{2,1,0:T(8,128)S(1)}, f32[2,24,128]{2,1,0:T(8,128)S(1)}, u32[]{:S(2)}, u32[]{:S(2)}) collective-permute-start(f32[2,24,128]{2,1,0:T(8,128)S(1)} %get-tuple-element.72.refs_7__0_), channel_id=1, source_target_pairs={{0,16},{8,24},{16,0},{24,8},{1,17},{9,25},{17,1},{25,9},{2,18},{10... | collective-permute-start | bytes 73736 | tf_op jit(solution)/shard_map/ppermute | solution.py:550
  25.7 0.4 collective-permute-start.7
  26.1 1.6 %collective-permute-done.9.refs_7__3_ = f32[2,24,128]{2,1,0:T(8,128)S(1)} collective-permute-done((f32[2,24,128]{2,1,0:T(8,128)S(1)}, f32[2,24,128]{2,1,0:T(8,128)S(1)}, u32[]{:S(2)}, u32[]{:S(2)}) %collective-permute-start.9) | collective-permute-done | bytes 24608 | tf_op jit(solution)/shard_map/ppermute | solution.py:550
  27.8 0.4 collective-permute-done.8.refs_7__2_
  28.2 0.0 collective-permute-done.7.refs_7__1_
  28.2 2.1 %direction.2 = (f32[18,128,128]{2,1,0:T(8,128)S(1)}, f32[32,2,128]{2,1,0:T(2,128)S(1)}) custom-call(s32[4,32]{1,0:T(4,128)S(1)} %bitcast.5, f32[14,128,128]{2,1,0:T(8,128)S(1)} %get-tuple-element.66.refs_1_, f32[4,128,128]{2,1,0:T(8,128)S(1)} %get-tuple-element.71.refs_2_, f32[16,128,128]{2,1,0:T(8,128)S(1)} %get-tuple-element.55.refs_2__0_.refs_1__0_.refs_3__0_, ...), custom_call_target="tpu_custom_call" | custom-call | flops 400000000 | bytes 12000000 | tf_op jit(solution)/shard_map/direction/pallas_call | solution.py:520
  30.3 13.9 %all_to_all.10.refs_2_ = f32[32,2,128]{2,1,0:T(2,128)S(1)} all-to-all(f32[32,2,128]{2,1,0:T(2,128)S(1)} %get-tuple-element.74), channel_id=1, replica_groups=mesh['tm'=4,'tile'=8] {'tile','tm'}, dimensions={0} | all-to-all | bytes 65536 | tf_op jit(solution)/shard_map/all_to_all | solution.py:666
  44.2 0.7 update.1
  44.9 0.3 collective-permute-start.12
  45.2 1.5 %collective-permute-start.11 = (f32[1,24,128]{2,1,0:T(8,128)S(1)}, f32[1,24,128]{2,1,0:T(8,128)S(1)}, u32[]{:S(2)}, u32[]{:S(2)}) collective-permute-start(f32[1,24,128]{2,1,0:T(8,128)S(1)} %get-tuple-element.78.refs_5__0_), channel_id=1, source_target_pairs={{0,16},{8,24},{16,0},{24,8},{1,17},{9,25},{17,1},{25,9},{2,18},{10... | collective-permute-start | bytes 36872 | tf_op jit(solution)/shard_map/ppermute | solution.py:550
  46.7 0.1 collective-permute-start.10
  46.9 1.2 %collective-permute-done.12.refs_5__3_ = f32[1,24,128]{2,1,0:T(8,128)S(1)} collective-permute-done((f32[1,24,128]{2,1,0:T(8,128)S(1)}, f32[1,24,128]{2,1,0:T(8,128)S(1)}, u32[]{:S(2)}, u32[]{:S(2)}) %collective-permute-start.12) | collective-permute-done | bytes 12320 | tf_op jit(solution)/shard_map/ppermute | solution.py:550
  48.1 0.8 %collective-permute-done.11.refs_5__2_ = f32[1,24,128]{2,1,0:T(8,128)S(1)} collective-permute-done((f32[1,24,128]{2,1,0:T(8,128)S(1)}, f32[1,24,128]{2,1,0:T(8,128)S(1)}, u32[]{:S(2)}, u32[]{:S(2)}) %collective-permute-start.11) | collective-permute-done | bytes 12320 | tf_op jit(solution)/shard_map/ppermute | solution.py:550
  48.9 0.0 collective-permute-done.10.refs_5__1_
  48.9 1.7 %edge.3 = (bf16[2304,128]{1,0:T(8,128)(2,1)S(1)}, f32[4,128,128]{2,1,0:T(8,128)S(1)}, f32[4,128,128]{2,1,0:T(8,128)S(1)}, bf16[2,128,128]{2,1,0:T(8,128)(2,1)S(1...) custom-call(s32[4,32]{1,0:T(4,128)S(1)} %bitcast.6, f32[16,128,128]{2,1,0:T(8,128)S(1)} %get-tuple-element.76.refs_1__0_, ...), custom_call_target="tpu_custom_call" | custom-call | flops 250000000 | bytes 7500000 | tf_op jit(solution)/shard_map/edge/pallas_call | solution.py:520
  50.6 0.7 collective-permute-start.13
  51.3 0.7 collective-permute-start.14
  51.9 3.6 %inner.3 = (f32[14,128,128]{2,1,0:T(8,128)S(1)}, f32[2,24,128]{2,1,0:T(8,128)S(1)}, f32[2048,128]{1,0:T(8,128)}) custom-call(s32[4,32]{1,0:T(4,128)S(1)} %bitcast.7, f32[16,128,128]{2,1,0:T(8,128)S(1)} %get-tuple-element.55.refs_2__0_.refs_1__0_.refs_3__0_, f32[2,128,128]{2,1,0:T(8,128)S(1)} %get-tuple-element.56.refs_2__1_.refs_1__1_.refs_3__1_, ...), custom_call_target="tpu_custom_call" | custom-call | flops 400000000 | bytes 12000000 | tf_op jit(solution)/shard_map/inner/pallas_call | solution.py:520
  55.5 0.0 collective-permute-done.13.refs_1_
  55.5 0.0 collective-permute-done.14.refs_2_
  55.5 0.3 border.3
  55.8 0.1 collective-permute-start.17
  55.9 1.5 %collective-permute-start.16 = (f32[2,24,128]{2,1,0:T(8,128)S(1)}, f32[2,24,128]{2,1,0:T(8,128)S(1)}, u32[]{:S(2)}, u32[]{:S(2)}) collective-permute-start(f32[2,24,128]{2,1,0:T(8,128)S(1)} %get-tuple-element.88.refs_7__0_), channel_id=1, source_target_pairs={{0,16},{8,24},{16,0},{24,8},{1,17},{9,25},{17,1},{25,9},{2,18},{10... | collective-permute-start | bytes 73736 | tf_op jit(solution)/shard_map/ppermute | solution.py:550
  57.4 0.3 collective-permute-start.15
  57.7 1.6 %collective-permute-done.17.refs_7__3_ = f32[2,24,128]{2,1,0:T(8,128)S(1)} collective-permute-done((f32[2,24,128]{2,1,0:T(8,128)S(1)}, f32[2,24,128]{2,1,0:T(8,128)S(1)}, u32[]{:S(2)}, u32[]{:S(2)}) %collective-permute-start.17) | collective-permute-done | bytes 24608 | tf_op jit(solution)/shard_map/ppermute | solution.py:550
  59.4 0.4 collective-permute-done.16.refs_7__2_
  59.8 0.0 collective-permute-done.15.refs_7__1_
  59.8 2.1 %direction.3 = (f32[18,128,128]{2,1,0:T(8,128)S(1)}, f32[32,2,128]{2,1,0:T(2,128)S(1)}) custom-call(s32[4,32]{1,0:T(4,128)S(1)} %bitcast.8, f32[14,128,128]{2,1,0:T(8,128)S(1)} %get-tuple-element.82.refs_1_, f32[4,128,128]{2,1,0:T(8,128)S(1)} %get-tuple-element.87.refs_2_, f32[16,128,128]{2,1,0:T(8,128)S(1)} %get-tuple-element.55.refs_2__0_.refs_1__0_.refs_3__0_, ...), custom_call_target="tpu_custom_call" | custom-call | flops 400000000 | bytes 12000000 | tf_op jit(solution)/shard_map/direction/pallas_call | solution.py:520
  61.9 12.6 %all_to_all.11.refs_2_ = f32[32,2,128]{2,1,0:T(2,128)S(1)} all-to-all(f32[32,2,128]{2,1,0:T(2,128)S(1)} %get-tuple-element.90), channel_id=1, replica_groups=mesh['tm'=4,'tile'=8] {'tile','tm'}, dimensions={0} | all-to-all | bytes 65536 | tf_op jit(solution)/shard_map/all_to_all | solution.py:666
  74.5 1.3 %final.1 = f32[2048,128]{1,0:T(8,128)} custom-call(f32[16,128,128]{2,1,0:T(8,128)S(1)} %get-tuple-element.75.refs_8__0_.refs_9__0_.refs_7__0_.refs_0_, f32[18,128,128]{2,1,0:T(8,128)S(1)} %get-tuple-element.89.refs_1_, f32[32,2,128]{2,1,0:T(2,128)S(1)} %all_to_all.11.refs_2_), custom_call_target="tpu_custom_call" | custom-call | flops 140000000 | bytes 4200000 | tf_op jit(solution)/shard_map/final/pallas_call | solution.py:520
Async XLA Ops:
  0.6 0.7 copy-start.4
  2.2 7.0 %collective-permute-start = (f32[136,128]{1,0:T(8,128)S(1)}, f32[136,128]{1,0:T(8,128)S(1)}, u32[]{:S(2)}, u32[]{:S(2)}) collective-permute-start(f32[136,128]{1,0:T(8,128)S(1)} %get-tuple-element.49), channel_id=1, source_target_pairs={{0,1},{2,3},{4,5},{6,7},{1,0},{3,2},{5,4},{7,6},{8,9},{10,11},{12,... | collective-permute-start | bytes 208904 | tf_op jit(solution)/shard_map/ppermute | solution.py:544
  5.3 4.0 %collective-permute-start.1 = (f32[136,128]{1,0:T(8,128)S(1)}, f32[136,128]{1,0:T(8,128)S(1)}, u32[]{:S(2)}, u32[]{:S(2)}) collective-permute-start(f32[136,128]{1,0:T(8,128)S(1)} %get-tuple-element.50), channel_id=1, source_target_pairs={{1,2},{3,4},{5,6},{2,1},{4,3},{6,5},{9,10},{11,12},{13,14},{10,9},... | collective-permute-start | bytes 208904 | tf_op jit(solution)/shard_map/ppermute | solution.py:544
  5.9 1.2 %copy-start.2 = (f32[2048,128]{1,0:T(8,128)S(1)}, f32[2048,128]{1,0:T(8,128)}, u32[]{:S(2)}) copy-start(f32[2048,128]{1,0:T(8,128)} %refs_0_.3) | copy-start | bytes 3145732
  7.2 0.7 copy-start.5
  7.8 6.5 %copy-start.1 = (bf16[8192,128]{1,0:T(8,128)(2,1)S(1)}, bf16[8192,128]{1,0:T(8,128)(2,1)}, u32[]{:S(2)}) copy-start(bf16[8192,128]{1,0:T(8,128)(2,1)} %refs_7_.7) | copy-start | bytes 6291460
  7.8 6.6 %copy-start.3 = (s32[32,4]{0,1:T(4,128)S(1)}, s32[32,4]{0,1:T(4,128)}, u32[]{:S(2)}) copy-start(s32[32,4]{0,1:T(4,128)} %param.8) | copy-start | bytes 1540
  9.6 3.5 %collective-permute-start.4 = (f32[2,24,128]{2,1,0:T(8,128)S(1)}, f32[2,24,128]{2,1,0:T(8,128)S(1)}, u32[]{:S(2)}, u32[]{:S(2)}) collective-permute-start(f32[2,24,128]{2,1,0:T(8,128)S(1)} %get-tuple-element.62.refs_4__0_.refs_5__0_.refs_6__0_), channel_id=1, source_target_pairs={{0,24},{8,16},{16,8},{24,0},{1,25},{9,17},{17,9},{25,1},{2,26},{10... | collective-permute-start | bytes 73736 | tf_op jit(solution)/shard_map/ppermute | solution.py:550
  10.3 4.1 %collective-permute-start.3 = (f32[2,24,128]{2,1,0:T(8,128)S(1)}, f32[2,24,128]{2,1,0:T(8,128)S(1)}, u32[]{:S(2)}, u32[]{:S(2)}) collective-permute-start(f32[2,24,128]{2,1,0:T(8,128)S(1)} %get-tuple-element.62.refs_4__0_.refs_5__0_.refs_6__0_), channel_id=1, source_target_pairs={{0,16},{8,24},{16,0},{24,8},{1,17},{9,25},{17,1},{25,9},{2,18},{10... | collective-permute-start | bytes 73736 | tf_op jit(solution)/shard_map/ppermute | solution.py:550
  11.2 3.2 %collective-permute-start.2 = (f32[2,24,128]{2,1,0:T(8,128)S(1)}, f32[2,24,128]{2,1,0:T(8,128)S(1)}, u32[]{:S(2)}, u32[]{:S(2)}) collective-permute-start(f32[2,24,128]{2,1,0:T(8,128)S(1)} %get-tuple-element.62.refs_4__0_.refs_5__0_.refs_6__0_), channel_id=1, source_target_pairs={{0,8},{8,0},{16,24},{24,16},{1,9},{9,1},{17,25},{25,17},{2,10},{10... | collective-permute-start | bytes 73736 | tf_op jit(solution)/shard_map/ppermute | solution.py:550
  14.4 6.2 %copy-start = (bf16[8192,256]{1,0:T(8,128)(2,1)S(1)}, bf16[8192,256]{1,0:T(8,128)(2,1)}, u32[]{:S(2)}) copy-start(bf16[8192,256]{1,0:T(8,128)(2,1)} %refs_8_.3) | copy-start | bytes 12582916
  16.1 7.8 %collective-permute-start.5 = (bf16[2,128,128]{2,1,0:T(8,128)(2,1)S(1)}, bf16[2,128,128]{2,1,0:T(8,128)(2,1)S(1)}, u32[]{:S(2)}, u32[]{:S(2)}) collective-permute-start(bf16[2,128,128]{2,1,0:T(8,128)(2,1)S(1)} %get-tuple-element.68), channel_id=1, source_target_pairs={{0,1},{2,3},{4,5},{6,7},{1,0},{3,2},{5,4},{7,6},{8,9},{10,11},{12,... | collective-permute-start | bytes 196616 | tf_op jit(solution)/shard_map/ppermute | solution.py:544
  19.9 4.0 %collective-permute-start.6 = (bf16[2,128,128]{2,1,0:T(8,128)(2,1)S(1)}, bf16[2,128,128]{2,1,0:T(8,128)(2,1)S(1)}, u32[]{:S(2)}, u32[]{:S(2)}) collective-permute-start(bf16[2,128,128]{2,1,0:T(8,128)(2,1)S(1)} %get-tuple-element.69), channel_id=1, source_target_pairs={{1,2},{3,4},{5,6},{2,1},{4,3},{6,5},{9,10},{11,12},{13,14},{10,9},... | collective-permute-start | bytes 196616 | tf_op jit(solution)/shard_map/ppermute | solution.py:544
  24.2 3.6 %collective-permute-start.9 = (f32[2,24,128]{2,1,0:T(8,128)S(1)}, f32[2,24,128]{2,1,0:T(8,128)S(1)}, u32[]{:S(2)}, u32[]{:S(2)}) collective-permute-start(f32[2,24,128]{2,1,0:T(8,128)S(1)} %get-tuple-element.72.refs_7__0_), channel_id=1, source_target_pairs={{0,24},{8,16},{16,8},{24,0},{1,25},{9,17},{17,9},{25,1},{2,26},{10... | collective-permute-start | bytes 73736 | tf_op jit(solution)/shard_map/ppermute | solution.py:550
  24.3 3.9 %collective-permute-start.8 = (f32[2,24,128]{2,1,0:T(8,128)S(1)}, f32[2,24,128]{2,1,0:T(8,128)S(1)}, u32[]{:S(2)}, u32[]{:S(2)}) collective-permute-start(f32[2,24,128]{2,1,0:T(8,128)S(1)} %get-tuple-element.72.refs_7__0_), channel_id=1, source_target_pairs={{0,16},{8,24},{16,0},{24,8},{1,17},{9,25},{17,1},{25,9},{2,18},{10... | collective-permute-start | bytes 73736 | tf_op jit(solution)/shard_map/ppermute | solution.py:550
  25.7 2.4 %collective-permute-start.7 = (f32[2,24,128]{2,1,0:T(8,128)S(1)}, f32[2,24,128]{2,1,0:T(8,128)S(1)}, u32[]{:S(2)}, u32[]{:S(2)}) collective-permute-start(f32[2,24,128]{2,1,0:T(8,128)S(1)} %get-tuple-element.72.refs_7__0_), channel_id=1, source_target_pairs={{0,8},{8,0},{16,24},{24,16},{1,9},{9,1},{17,25},{25,17},{2,10},{10... | collective-permute-start | bytes 73736 | tf_op jit(solution)/shard_map/ppermute | solution.py:550
  44.9 3.2 %collective-permute-start.12 = (f32[1,24,128]{2,1,0:T(8,128)S(1)}, f32[1,24,128]{2,1,0:T(8,128)S(1)}, u32[]{:S(2)}, u32[]{:S(2)}) collective-permute-start(f32[1,24,128]{2,1,0:T(8,128)S(1)} %get-tuple-element.78.refs_5__0_), channel_id=1, source_target_pairs={{0,24},{8,16},{16,8},{24,0},{1,25},{9,17},{17,9},{25,1},{2,26},{10... | collective-permute-start | bytes 36872 | tf_op jit(solution)/shard_map/ppermute | solution.py:550
  45.2 3.7 %collective-permute-start.11 = (f32[1,24,128]{2,1,0:T(8,128)S(1)}, f32[1,24,128]{2,1,0:T(8,128)S(1)}, u32[]{:S(2)}, u32[]{:S(2)}) collective-permute-start(f32[1,24,128]{2,1,0:T(8,128)S(1)} %get-tuple-element.78.refs_5__0_), channel_id=1, source_target_pairs={{0,16},{8,24},{16,0},{24,8},{1,17},{9,25},{17,1},{25,9},{2,18},{10... | collective-permute-start | bytes 36872 | tf_op jit(solution)/shard_map/ppermute | solution.py:550
  46.7 2.2 %collective-permute-start.10 = (f32[1,24,128]{2,1,0:T(8,128)S(1)}, f32[1,24,128]{2,1,0:T(8,128)S(1)}, u32[]{:S(2)}, u32[]{:S(2)}) collective-permute-start(f32[1,24,128]{2,1,0:T(8,128)S(1)} %get-tuple-element.78.refs_5__0_), channel_id=1, source_target_pairs={{0,8},{8,0},{16,24},{24,16},{1,9},{9,1},{17,25},{25,17},{2,10},{10... | collective-permute-start | bytes 36872 | tf_op jit(solution)/shard_map/ppermute | solution.py:550
  50.6 4.9 %collective-permute-start.13 = (bf16[2,128,128]{2,1,0:T(8,128)(2,1)S(1)}, bf16[2,128,128]{2,1,0:T(8,128)(2,1)S(1)}, u32[]{:S(2)}, u32[]{:S(2)}) collective-permute-start(bf16[2,128,128]{2,1,0:T(8,128)(2,1)S(1)} %get-tuple-element.84), channel_id=1, source_target_pairs={{0,1},{2,3},{4,5},{6,7},{1,0},{3,2},{5,4},{7,6},{8,9},{10,11},{12,... | collective-permute-start | bytes 196616 | tf_op jit(solution)/shard_map/ppermute | solution.py:544
  51.3 4.2 %collective-permute-start.14 = (bf16[2,128,128]{2,1,0:T(8,128)(2,1)S(1)}, bf16[2,128,128]{2,1,0:T(8,128)(2,1)S(1)}, u32[]{:S(2)}, u32[]{:S(2)}) collective-permute-start(bf16[2,128,128]{2,1,0:T(8,128)(2,1)S(1)} %get-tuple-element.85), channel_id=1, source_target_pairs={{1,2},{3,4},{5,6},{2,1},{4,3},{6,5},{9,10},{11,12},{13,14},{10,9},... | collective-permute-start | bytes 196616 | tf_op jit(solution)/shard_map/ppermute | solution.py:544
  55.8 3.6 %collective-permute-start.17 = (f32[2,24,128]{2,1,0:T(8,128)S(1)}, f32[2,24,128]{2,1,0:T(8,128)S(1)}, u32[]{:S(2)}, u32[]{:S(2)}) collective-permute-start(f32[2,24,128]{2,1,0:T(8,128)S(1)} %get-tuple-element.88.refs_7__0_), channel_id=1, source_target_pairs={{0,24},{8,16},{16,8},{24,0},{1,25},{9,17},{17,9},{25,1},{2,26},{10... | collective-permute-start | bytes 73736 | tf_op jit(solution)/shard_map/ppermute | solution.py:550
  55.9 3.9 %collective-permute-start.16 = (f32[2,24,128]{2,1,0:T(8,128)S(1)}, f32[2,24,128]{2,1,0:T(8,128)S(1)}, u32[]{:S(2)}, u32[]{:S(2)}) collective-permute-start(f32[2,24,128]{2,1,0:T(8,128)S(1)} %get-tuple-element.88.refs_7__0_), channel_id=1, source_target_pairs={{0,16},{8,24},{16,0},{24,8},{1,17},{9,25},{17,1},{25,9},{2,18},{10... | collective-permute-start | bytes 73736 | tf_op jit(solution)/shard_map/ppermute | solution.py:550
  57.4 2.4 %collective-permute-start.15 = (f32[2,24,128]{2,1,0:T(8,128)S(1)}, f32[2,24,128]{2,1,0:T(8,128)S(1)}, u32[]{:S(2)}, u32[]{:S(2)}) collective-permute-start(f32[2,24,128]{2,1,0:T(8,128)S(1)} %get-tuple-element.88.refs_7__0_), channel_id=1, source_target_pairs={{0,8},{8,0},{16,24},{24,16},{1,9},{9,1},{17,25},{25,17},{2,10},{10... | collective-permute-start | bytes 73736 | tf_op jit(solution)/shard_map/ppermute | solution.py:550

commit v7 on v6

--- a/solution.py
+++ b/solution.py
@@ -61,7 +61,7 @@
     return field[0].shape[0] + field[1].shape[0]
 
 
-def prep_chunk(c, rate, field, gains, s3, p3, pinv3, z3, rows, pay):
+def prep_chunk(c, chunks, rate, field, gains, s3, p3, pinv3, z3, rows, pay):
     frames = field.shape[1]
     middle, prefix_col, inverse_col, sums_table = gains
     mid = frames // 2 - 1
@@ -83,9 +83,10 @@
     rows[0, c : c + 1, :] = gain
     rows[1, c : c + 1, :] = half * middle
     rows[2, c : c + 1, :] = half * half
-    pay[0, c : c + 1, :] = last * z[frames - 1 : frames, :]
+    pay[c : c + 1, :] = last * z[frames - 1 : frames, :]
     scale = last * gain
-    pay[1, c : c + 1, :] = scale * scale * jnp.sum(pinv * pinv, axis=0, keepdims=True)
+    squares = scale * scale * jnp.sum(pinv * pinv, axis=0, keepdims=True)
+    pay[chunks + c : chunks + c + 1, :] = squares
 
 
 def gain_columns(gains):
@@ -161,12 +162,13 @@
         rows[...] = jnp.ones_like(rows)
         rows[0, chunks : chunks + 1, :] = middle
         pay[...] = jnp.zeros_like(pay)
-        pay[0, chunks : chunks + 1, :] = whole
+        pay[2 * chunks : 2 * chunks + 1, :] = whole
         shared = middle, prefix_col, inverse_col, table(spikes.shape[1], False)
         for i in range(own):
             field = spikes[i * LANES : (i + 1) * LANES, :]
             at = [ref.at[i] for ref in (s3, p3, pinv3, z3)]
-            prep_chunk(i + RIM, decay[i : i + 1, :], field, shared, *at, rows, pay)
+            rate = decay[i : i + 1, :]
+            prep_chunk(i + RIM, chunks, rate, field, shared, *at, rows, pay)
 
     for fetch in fetches:
         fetch.wait()
@@ -193,7 +195,7 @@
         at = [ref.at[i] for ref in (s3, p3, pinv3, z3)]
         field = message[j * LANES : (j + 1) * LANES, :]
         rate = message[RIM * LANES + j : RIM * LANES + j + 1, :]
-        prep_chunk(c, rate, field, shared, *at, rows, pay)
+        prep_chunk(c, chunks, rate, field, shared, *at, rows, pay)
 
 
 def by_block(parts, me, index):
@@ -208,7 +210,8 @@
 
 
 def block_totals(pay, me, chunks, rows):
-    return [rows[2] * whole for whole in by_block(pay, me, (0, slice(chunks, chunks + 1)))]
+    wholes = by_block(pay, me, slice(2 * chunks, 2 * chunks + 1))
+    return [rows[2, 0:chunks] * whole for whole in wholes]
 
 
 def step_size(stats):
@@ -231,7 +234,7 @@
             new3[0][c - RIM] = field
         chunk(z3, c)[...] = z
         last = chunk(p3, c)[frames - 1 : frames, :]
-        pay[0, c : c + 1, :] = last * z[frames - 1 : frames, :]
+        pay[c : c + 1, :] = last * z[frames - 1 : frames, :]
 
 
 def final_kernel(s3, g3, stats, out, here, sems):
@@ -326,11 +329,11 @@
     def _():
         me = lax.axis_index("tm")
         totals = block_totals(pay, me, chunks, rows)
-        ends = by_block(pays, me, 0)
+        ends = by_block(pays, me, slice(0, chunks))
         carry = jnp.zeros_like(totals[0])
         for m, end in enumerate(ends):
             carry = jnp.where(m < me, end + totals[m] * carry, carry)
-        carry = carry * rows[1]
+        carry = carry * rows[1, 0:chunks]
         for c in range(chunks):
             field = chunk(p3, c)[...] * (chunk(z3, c)[...] + carry[c : c + 1, :])
             at = slice(c * LANES, (c + 1) * LANES)
@@ -358,14 +361,15 @@
         spill[i] = gathered(contrib, place, 2 * RIM + i, ranges)
         spill[2 * RIM + i] = gathered(contrib, place, chunks - 4 * RIM + i, ranges)
 
-def adjoint_chunk(sums_table, field, p, pinv, rows, c, r3, pay):
+def adjoint_chunk(sums_table, field, p, pinv, rows, c, chunks, r3, pay):
     frames = field.shape[0]
     r = summed(sums_table, field * p)
     r3[...] = r
     gain = rows[0, c : c + 1, :]
-    pay[0, c : c + 1, :] = rows[1, c : c + 1, :] * r[0:1, :]
+    pay[c : c + 1, :] = rows[1, c : c + 1, :] * r[0:1, :]
     ends = p[frames - 1 : frames, :] * gain * gain
-    pay[1, c : c + 1, :] = ends * jnp.sum(pinv * pinv * r, axis=0, keepdims=True)
+    ends = ends * jnp.sum(pinv * pinv * r, axis=0, keepdims=True)
+    pay[chunks + c : chunks + c + 1, :] = ends
 
 
 def inner_kernel(pattern_far, p3, pinv3, rows, ext, spill, feet, record, traces, r3, pay, *rest):
@@ -396,7 +400,7 @@
             if i >= inner - 2 * RIM:
                 field = field + spill[i - inner + 4 * RIM]
             p, pinv = chunk(p3, c)[...], chunk(pinv3, c)[...]
-            adjoint_chunk(sums_table, field, p, pinv, rows, c, r3.at[i], pay)
+            adjoint_chunk(sums_table, field, p, pinv, rows, c, chunks, r3.at[i], pay)
 
     if traces:
         after_start(compute)
@@ -417,7 +421,7 @@
             at = side * 2 * RIM + i
             field = zones[at] + both[side]
             p, pinv = chunk(p3, c)[...], chunk(pinv3, c)[...]
-            adjoint_chunk(sums_table, field, p, pinv, rows, c, r3.at[at], pay)
+            adjoint_chunk(sums_table, field, p, pinv, rows, c, chunks, r3.at[at], pay)
 
 
 def direction_kernel(
@@ -437,9 +441,9 @@
     def _():
         me = lax.axis_index("tm")
         totals = block_totals(pay, me, chunks, rows)
-        gains = by_block(pay, me, 1)
-        starts = by_block(pays, me, 0)
-        ends = by_block(pays, me, 1)
+        gains = by_block(pay, me, slice(chunks, 2 * chunks))
+        starts = by_block(pays, me, slice(0, chunks))
+        ends = by_block(pays, me, slice(chunks, 2 * chunks))
         blocks = len(pays)
         entering = [None] * blocks
         state = jnp.zeros_like(totals[0])
@@ -452,7 +456,7 @@
             end = ends[m] + gains[m] * entering[m]
             carry = jnp.where(m < me, end + totals[m] * carry, carry)
             adjoint = jnp.where(m == me, entering[m], adjoint)
-        carry = carry * rows[1]
+        carry = carry * rows[1, 0:chunks]
         sums_table = table(frames, False)
         grad_sq = jnp.zeros((8, LANES), F32)
         for c in range(chunks):
@@ -560,6 +564,7 @@
     own = neurons // LANES
     chunks = own + 2 * RIM
     lines = own + padded8(1)
+    pay_lines = padded8(2 * chunks + 1)
     devices = lax.axis_size("tile") * lax.axis_size("tm")
     split = (f32(own, frames, LANES), f32(2 * RIM, frames, LANES))
     message = f32(RIM * LANES + padded8(RIM), frames)
@@ -582,7 +587,7 @@
         "prep_own",
         1.6,
         (split[0],) * 4
-        + (f32(3, lines, LANES), f32(2, lines, LANES), f32(2, frames, LANES))
+        + (f32(3, lines, LANES), f32(pay_lines, LANES), f32(2, frames, LANES))
         + (bf16(ends_size, K * NEU_BLOCK),),
         (spikes, rates, gains, footprints),
         [pltpu.SemaphoreType.DMA((2,))],
@@ -593,7 +598,7 @@
         prep_rim_kernel,
         "prep_rim",
         0.3,
-        (split[1],) * 4 + (f32(3, lines, LANES), f32(2, lines, LANES)),
+        (split[1],) * 4 + (f32(3, lines, LANES), f32(pay_lines, LANES)),
         (first, second, columns, rows, pay),
     )
     s3, p3, pinv3, z3 = zip(owns, rims)
@@ -633,7 +638,7 @@
             inner_kernel,
             "inner",
             4.0,
-            (f32(chunks - 4 * RIM, frames, LANES), f32(2, lines, LANES))
+            (f32(chunks - 4 * RIM, frames, LANES), f32(pay_lines, LANES))
             + ((f32(neurons, frames),) if ends else ()),
             (pattern, p3, pinv3, rows, ext, spill, footprints, recording, traces),
             scratch + ([pltpu.SemaphoreType.DMA] if ends else []),
@@ -644,7 +649,7 @@
             border_kernel,
             "border",
             0.3,
-            (f32(*border), f32(2, lines, LANES)),
+            (f32(*border), f32(pay_lines, LANES)),
             (zones, got_a, got_b, p3, pinv3, rows, pay),
             keep=held,
         )
@@ -679,7 +684,7 @@
             update_kernel,
             "update",
             0.6,
-            (split if iteration < ITERS - 2 else split[:1], split, f32(1, lines, LANES)),
+            (split if iteration < ITERS - 2 else split[:1], split, f32(lines, LANES)),
             (s3, g3, stats, p3, pinv3, rows),
         )
         pays = shared_blocks(pay)

time: 76.3 us -> 76.2 us (level)
  no operation moved by 1% of the time
where the time goes in v7:
time: 76.2 us; the launch traced here: 75.9 us
  blocking collectives  26.5 us (35%)
  Pallas kernels  19.7 us (26%)
  starting transfers between devices  17.3 us (23%)
  waiting for transfers between devices  8.85 us (12%)
  local copies, waits for them, and re-layouts  2.58 us (3%)
  between operations  1.01 us (1%)
    all_to_all x2, blocking collectives, per_device(): stats = lax.all_to_all(stats, ('tile', 'tm'), 0, 0)  26.5 us
    pallas_call x13, Pallas kernels, call(): pl.pallas_call(body, name=name, out_shape=outs, in_specs=in_specs, out_sp...  19.7 us
    ppermute x12, waiting for transfers between devices, shared_blocks(): lax.ppermute(value, 'tm', [(i, i ^ j) for i in range(size)])  8.83 us
    ppermute x12, starting transfers between devices, shared_blocks(): lax.ppermute(value, 'tm', [(i, i ^ j) for i in range(size)])  7.7 us
    ppermute x3, starting transfers between devices, swapped(): lax.ppermute(first, 'tile', pairs(0))  7.59 us
    unnamed x12, local copies, waits for them, and re-layouts  2.58 us
    ppermute x3, starting transfers between devices, swapped(): lax.ppermute(second, 'tile', pairs(1))  1.96 us
  transfers between devices with their start and end apart: 18, of which 8 were waited for; matrix products, arithmetic and copies ran while one was open for 0% of the time, Pallas kernels for 11%

profile of v7, /device:TPU:0, one launch (start us, length us, event | category | flops | bytes accessed | tf_op | source)
XLA Modules:
  0.0 75.9 jit_solution(346162345862120630)
XLA Ops:
  0.6 0.0 copy-start.4
  0.6 0.7 copy-done.4
  1.3 0.9 %rims.1 = (f32[136,128]{1,0:T(8,128)S(1)}, f32[136,128]{1,0:T(8,128)S(1)}, f32[16,128]{1,0:T(8,128)S(1)}) custom-call(f32[2048,128]{1,0:T(8,128)} %refs_0_.3, f32[16,128]{1,0:T(8,128)S(1)} %bitcast.9), custom_call_target="tpu_custom_call" | custom-call | flops 100000000 | bytes 3000000 | tf_op jit(solution)/shard_map/rims/pallas_call | solution.py:524
  2.2 3.0 %collective-permute-start = (f32[136,128]{1,0:T(8,128)S(1)}, f32[136,128]{1,0:T(8,128)S(1)}, u32[]{:S(2)}, u32[]{:S(2)}) collective-permute-start(f32[136,128]{1,0:T(8,128)S(1)} %get-tuple-element.49), channel_id=1, source_target_pairs={{0,1},{2,3},{4,5},{6,7},{1,0},{3,2},{5,4},{7,6},{8,9},{10,11},{12,... | collective-permute-start | bytes 208904 | tf_op jit(solution)/shard_map/ppermute | solution.py:548
  5.3 0.7 collective-permute-start.1
  5.9 0.0 copy-start.2
  5.9 1.2 %copy-done.2 = f32[2048,128]{1,0:T(8,128)S(1)} copy-done((f32[2048,128]{1,0:T(8,128)S(1)}, f32[2048,128]{1,0:T(8,128)}, u32[]{:S(2)}) %copy-start.2) | copy-done | bytes 1048600
  7.2 0.0 copy-start.5
  7.2 0.7 copy-done.5
  7.8 0.0 copy-start.1
  7.8 0.0 copy-start.3
  7.8 1.4 %prep_own.1 = (f32[16,128,128]{2,1,0:T(8,128)S(1)}, f32[16,128,128]{2,1,0:T(8,128)S(1)}, f32[16,128,128]{2,1,0:T(8,128)S(1)}, f32[16,128,128]{2,1,0:T(8,128)S(1)...) custom-call(f32[2048,128]{1,0:T(8,128)S(1)} %copy-done.2, ...), custom_call_target="tpu_custom_call" | custom-call | flops 160000000 | bytes 4800000 | tf_op jit(solution)/shard_map/prep_own/pallas_call | solution.py:524
  9.2 0.0 collective-permute-done.refs_0_
  9.3 0.0 collective-permute-done.1.refs_1_
  9.3 0.3 prep_rim.1
  9.6 0.7 collective-permute-start.4
  10.3 0.9 %collective-permute-start.3 = (f32[40,128]{1,0:T(8,128)S(1)}, f32[40,128]{1,0:T(8,128)S(1)}, u32[]{:S(2)}, u32[]{:S(2)}) collective-permute-start(f32[40,128]{1,0:T(8,128)S(1)} %get-tuple-element.62.refs_4__0_.refs_5__0_.refs_6__0_), channel_id=1, source_target_pairs={{0,16},{8,24},{16,0},{24,8},{1,17},{9,25},{17,1},{25,9},{2,18},{10... | collective-permute-start | bytes 61448 | tf_op jit(solution)/shard_map/ppermute | solution.py:554
  11.2 0.3 collective-permute-start.2
  11.5 1.5 %collective-permute-done.4.refs_4__3_.refs_5__3_.refs_6__3_ = f32[40,128]{1,0:T(8,128)S(1)} collective-permute-done((f32[40,128]{1,0:T(8,128)S(1)}, f32[40,128]{1,0:T(8,128)S(1)}, u32[]{:S(2)}, u32[]{:S(2)}) %collective-permute-start.4) | collective-permute-done | bytes 20512 | tf_op jit(solution)/shard_map/ppermute | solution.py:554
  13.0 1.3 %collective-permute-done.3.refs_4__2_.refs_5__2_.refs_6__2_ = f32[40,128]{1,0:T(8,128)S(1)} collective-permute-done((f32[40,128]{1,0:T(8,128)S(1)}, f32[40,128]{1,0:T(8,128)S(1)}, u32[]{:S(2)}, u32[]{:S(2)}) %collective-permute-start.3) | collective-permute-done | bytes 20512 | tf_op jit(solution)/shard_map/ppermute | solution.py:554
  14.3 0.0 collective-permute-done.2.refs_4__1_.refs_5__1_.refs_6__1_
  14.3 0.0 copy-done.1
  14.3 0.0 copy-done.3
  14.3 0.0 copy-start
  14.3 1.7 %edge.2 = (bf16[2304,128]{1,0:T(8,128)(2,1)S(1)}, f32[4,128,128]{2,1,0:T(8,128)S(1)}, f32[4,128,128]{2,1,0:T(8,128)S(1)}, bf16[2,128,128]{2,1,0:T(8,128)(2,1)S(1)}, bf16[2,128,128]{2,1,0:T(8,128)(2,1)S(1)}) custom-call(s32[4,32]{1,0:T(4,128)S(1)} %bitcast.3, f32[16,128,128]{2,1,0:T(8,128)S(1)} %get-tuple-element.60.refs_1__0_, ...), custom_call_target="tpu_custom_call" | custom-call | flops 250000000 | bytes 7500000 | tf_op jit(solution)/shard_map/edge/pallas_call | solution.py:524
  16.0 3.9 %collective-permute-start.5 = (bf16[2,128,128]{2,1,0:T(8,128)(2,1)S(1)}, bf16[2,128,128]{2,1,0:T(8,128)(2,1)S(1)}, u32[]{:S(2)}, u32[]{:S(2)}) collective-permute-start(bf16[2,128,128]{2,1,0:T(8,128)(2,1)S(1)} %get-tuple-element.68), channel_id=1, source_target_pairs={{0,1},{2,3},{4,5},{6,7},{1,0},{3,2},{5,4},{7,6},{8,9},{10,11},{12,... | collective-permute-start | bytes 196616 | tf_op jit(solution)/shard_map/ppermute | solution.py:548
  19.8 0.7 collective-permute-start.6
  20.5 0.0 copy-done
  20.5 3.3 %inner.2 = (f32[14,128,128]{2,1,0:T(8,128)S(1)}, f32[40,128]{1,0:T(8,128)S(1)}) custom-call(s32[4,32]{1,0:T(4,128)S(1)} %bitcast.4, f32[16,128,128]{2,1,0:T(8,128)S(1)} %get-tuple-element.55.refs_2__0_.refs_1__0_.refs_3__0_, f32[2,128,128]{2,1,0:T(8,128)S(1)} %get-tuple-element.56.refs_2__1_.refs_1__1_.refs_3__1_, ...), custom_call_target="tpu_custom_call" | custom-call | flops 400000000 | bytes 12000000 | tf_op jit(solution)/shard_map/inner/pallas_call | solution.py:524
  23.8 0.0 collective-permute-done.5.refs_1_
  23.9 0.0 collective-permute-done.6.refs_2_
  23.9 0.3 border.2
  24.1 0.1 collective-permute-start.9
  24.2 1.4 %collective-permute-start.8 = (f32[40,128]{1,0:T(8,128)S(1)}, f32[40,128]{1,0:T(8,128)S(1)}, u32[]{:S(2)}, u32[]{:S(2)}) collective-permute-start(f32[40,128]{1,0:T(8,128)S(1)} %get-tuple-element.72.refs_7__0_), channel_id=1, source_target_pairs={{0,16},{8,24},{16,0},{24,8},{1,17},{9,25},{17,1},{25,9},{2,18},{10... | collective-permute-start | bytes 61448 | tf_op jit(solution)/shard_map/ppermute | solution.py:554
  25.7 0.4 collective-permute-start.7
  26.1 1.6 %collective-permute-done.9.refs_7__3_ = f32[40,128]{1,0:T(8,128)S(1)} collective-permute-done((f32[40,128]{1,0:T(8,128)S(1)}, f32[40,128]{1,0:T(8,128)S(1)}, u32[]{:S(2)}, u32[]{:S(2)}) %collective-permute-start.9) | collective-permute-done | bytes 20512 | tf_op jit(solution)/shard_map/ppermute | solution.py:554
  27.6 0.4 collective-permute-done.8.refs_7__2_
  28.1 0.0 collective-permute-done.7.refs_7__1_
  28.1 2.2 %direction.2 = (f32[18,128,128]{2,1,0:T(8,128)S(1)}, f32[32,2,128]{2,1,0:T(2,128)S(1)}) custom-call(s32[4,32]{1,0:T(4,128)S(1)} %bitcast.5, f32[14,128,128]{2,1,0:T(8,128)S(1)} %get-tuple-element.66.refs_1_, f32[4,128,128]{2,1,0:T(8,128)S(1)} %get-tuple-element.71.refs_2_, f32[16,128,128]{2,1,0:T(8,128)S(1)} %get-tuple-element.55.refs_2__0_.refs_1__0_.refs_3__0_, ...), custom_call_target="tpu_custom_call" | custom-call | flops 400000000 | bytes 12000000 | tf_op jit(solution)/shard_map/direction/pallas_call | solution.py:524
  30.2 13.9 %all_to_all.10.refs_2_ = f32[32,2,128]{2,1,0:T(2,128)S(1)} all-to-all(f32[32,2,128]{2,1,0:T(2,128)S(1)} %get-tuple-element.74), channel_id=1, replica_groups=mesh['tm'=4,'tile'=8] {'tile','tm'}, dimensions={0} | all-to-all | bytes 65536 | tf_op jit(solution)/shard_map/all_to_all | solution.py:671
  44.2 0.7 update.1
  44.9 0.3 collective-permute-start.12
  45.2 1.6 %collective-permute-start.11 = (f32[24,128]{1,0:T(8,128)S(1)}, f32[24,128]{1,0:T(8,128)S(1)}, u32[]{:S(2)}, u32[]{:S(2)}) collective-permute-start(f32[24,128]{1,0:T(8,128)S(1)} %get-tuple-element.78.refs_5__0_), channel_id=1, source_target_pairs={{0,16},{8,24},{16,0},{24,8},{1,17},{9,25},{17,1},{25,9},{2,18},{10... | collective-permute-start | bytes 36872 | tf_op jit(solution)/shard_map/ppermute | solution.py:554
  46.7 0.1 collective-permute-start.10
  46.8 1.3 %collective-permute-done.12.refs_5__3_ = f32[24,128]{1,0:T(8,128)S(1)} collective-permute-done((f32[24,128]{1,0:T(8,128)S(1)}, f32[24,128]{1,0:T(8,128)S(1)}, u32[]{:S(2)}, u32[]{:S(2)}) %collective-permute-start.12) | collective-permute-done | bytes 12320 | tf_op jit(solution)/shard_map/ppermute | solution.py:554
  48.1 0.8 %collective-permute-done.11.refs_5__2_ = f32[24,128]{1,0:T(8,128)S(1)} collective-permute-done((f32[24,128]{1,0:T(8,128)S(1)}, f32[24,128]{1,0:T(8,128)S(1)}, u32[]{:S(2)}, u32[]{:S(2)}) %collective-permute-start.11) | collective-permute-done | bytes 12320 | tf_op jit(solution)/shard_map/ppermute | solution.py:554
  48.9 0.0 collective-permute-done.10.refs_5__1_
  48.9 1.7 %edge.3 = (bf16[2304,128]{1,0:T(8,128)(2,1)S(1)}, f32[4,128,128]{2,1,0:T(8,128)S(1)}, f32[4,128,128]{2,1,0:T(8,128)S(1)}, bf16[2,128,128]{2,1,0:T(8,128)(2,1)S(1...) custom-call(s32[4,32]{1,0:T(4,128)S(1)} %bitcast.6, f32[16,128,128]{2,1,0:T(8,128)S(1)} %get-tuple-element.76.refs_1__0_, ...), custom_call_target="tpu_custom_call" | custom-call | flops 250000000 | bytes 7500000 | tf_op jit(solution)/shard_map/edge/pallas_call | solution.py:524
  50.5 0.7 collective-permute-start.13
  51.2 0.7 collective-permute-start.14
  51.9 3.5 %inner.3 = (f32[14,128,128]{2,1,0:T(8,128)S(1)}, f32[40,128]{1,0:T(8,128)S(1)}, f32[2048,128]{1,0:T(8,128)}) custom-call(s32[4,32]{1,0:T(4,128)S(1)} %bitcast.7, f32[16,128,128]{2,1,0:T(8,128)S(1)} %get-tuple-element.55.refs_2__0_.refs_1__0_.refs_3__0_, f32[2,128,128]{2,1,0:T(8,128)S(1)} %get-tuple-element.56.refs_2__1_.refs_1__1_.refs_3__1_, ...), custom_call_target="tpu_custom_call" | custom-call | flops 400000000 | bytes 12000000 | tf_op jit(solution)/shard_map/inner/pallas_call | solution.py:524
  55.4 0.0 collective-permute-done.13.refs_1_
  55.5 0.0 collective-permute-done.14.refs_2_
  55.5 0.3 border.3
  55.7 0.1 collective-permute-start.17
  55.8 1.5 %collective-permute-start.16 = (f32[40,128]{1,0:T(8,128)S(1)}, f32[40,128]{1,0:T(8,128)S(1)}, u32[]{:S(2)}, u32[]{:S(2)}) collective-permute-start(f32[40,128]{1,0:T(8,128)S(1)} %get-tuple-element.88.refs_7__0_), channel_id=1, source_target_pairs={{0,16},{8,24},{16,0},{24,8},{1,17},{9,25},{17,1},{25,9},{2,18},{10... | collective-permute-start | bytes 61448 | tf_op jit(solution)/shard_map/ppermute | solution.py:554
  57.3 0.3 collective-permute-start.15
  57.7 1.6 %collective-permute-done.17.refs_7__3_ = f32[40,128]{1,0:T(8,128)S(1)} collective-permute-done((f32[40,128]{1,0:T(8,128)S(1)}, f32[40,128]{1,0:T(8,128)S(1)}, u32[]{:S(2)}, u32[]{:S(2)}) %collective-permute-start.17) | collective-permute-done | bytes 20512 | tf_op jit(solution)/shard_map/ppermute | solution.py:554
  59.2 0.4 collective-permute-done.16.refs_7__2_
  59.7 0.0 collective-permute-done.15.refs_7__1_
  59.7 2.2 %direction.3 = (f32[18,128,128]{2,1,0:T(8,128)S(1)}, f32[32,2,128]{2,1,0:T(2,128)S(1)}) custom-call(s32[4,32]{1,0:T(4,128)S(1)} %bitcast.8, f32[14,128,128]{2,1,0:T(8,128)S(1)} %get-tuple-element.82.refs_1_, f32[4,128,128]{2,1,0:T(8,128)S(1)} %get-tuple-element.87.refs_2_, f32[16,128,128]{2,1,0:T(8,128)S(1)} %get-tuple-element.55.refs_2__0_.refs_1__0_.refs_3__0_, ...), custom_call_target="tpu_custom_call" | custom-call | flops 400000000 | bytes 12000000 | tf_op jit(solution)/shard_map/direction/pallas_call | solution.py:524
  61.8 12.6 %all_to_all.11.refs_2_ = f32[32,2,128]{2,1,0:T(2,128)S(1)} all-to-all(f32[32,2,128]{2,1,0:T(2,128)S(1)} %get-tuple-element.90), channel_id=1, replica_groups=mesh['tm'=4,'tile'=8] {'tile','tm'}, dimensions={0} | all-to-all | bytes 65536 | tf_op jit(solution)/shard_map/all_to_all | solution.py:671
  74.5 1.3 %final.1 = f32[2048,128]{1,0:T(8,128)} custom-call(f32[16,128,128]{2,1,0:T(8,128)S(1)} %get-tuple-element.75.refs_8__0_.refs_9__0_.refs_7__0_.refs_0_, f32[18,128,128]{2,1,0:T(8,128)S(1)} %get-tuple-element.89.refs_1_, f32[32,2,128]{2,1,0:T(2,128)S(1)} %all_to_all.11.refs_2_), custom_call_target="tpu_custom_call" | custom-call | flops 140000000 | bytes 4200000 | tf_op jit(solution)/shard_map/final/pallas_call | solution.py:524
Async XLA Ops:
  0.6 0.7 copy-start.4
  2.2 7.0 %collective-permute-start = (f32[136,128]{1,0:T(8,128)S(1)}, f32[136,128]{1,0:T(8,128)S(1)}, u32[]{:S(2)}, u32[]{:S(2)}) collective-permute-start(f32[136,128]{1,0:T(8,128)S(1)} %get-tuple-element.49), channel_id=1, source_target_pairs={{0,1},{2,3},{4,5},{6,7},{1,0},{3,2},{5,4},{7,6},{8,9},{10,11},{12,... | collective-permute-start | bytes 208904 | tf_op jit(solution)/shard_map/ppermute | solution.py:548
  5.3 4.0 %collective-permute-start.1 = (f32[136,128]{1,0:T(8,128)S(1)}, f32[136,128]{1,0:T(8,128)S(1)}, u32[]{:S(2)}, u32[]{:S(2)}) collective-permute-start(f32[136,128]{1,0:T(8,128)S(1)} %get-tuple-element.50), channel_id=1, source_target_pairs={{1,2},{3,4},{5,6},{2,1},{4,3},{6,5},{9,10},{11,12},{13,14},{10,9},... | collective-permute-start | bytes 208904 | tf_op jit(solution)/shard_map/ppermute | solution.py:548
  5.9 1.2 %copy-start.2 = (f32[2048,128]{1,0:T(8,128)S(1)}, f32[2048,128]{1,0:T(8,128)}, u32[]{:S(2)}) copy-start(f32[2048,128]{1,0:T(8,128)} %refs_0_.3) | copy-start | bytes 3145732
  7.2 0.7 copy-start.5
  7.8 6.4 %copy-start.1 = (bf16[8192,128]{1,0:T(8,128)(2,1)S(1)}, bf16[8192,128]{1,0:T(8,128)(2,1)}, u32[]{:S(2)}) copy-start(bf16[8192,128]{1,0:T(8,128)(2,1)} %refs_7_.7) | copy-start | bytes 6291460
  7.8 6.4 %copy-start.3 = (s32[32,4]{0,1:T(4,128)S(1)}, s32[32,4]{0,1:T(4,128)}, u32[]{:S(2)}) copy-start(s32[32,4]{0,1:T(4,128)} %param.8) | copy-start | bytes 1540
  9.6 3.4 %collective-permute-start.4 = (f32[40,128]{1,0:T(8,128)S(1)}, f32[40,128]{1,0:T(8,128)S(1)}, u32[]{:S(2)}, u32[]{:S(2)}) collective-permute-start(f32[40,128]{1,0:T(8,128)S(1)} %get-tuple-element.62.refs_4__0_.refs_5__0_.refs_6__0_), channel_id=1, source_target_pairs={{0,24},{8,16},{16,8},{24,0},{1,25},{9,17},{17,9},{25,1},{2,26},{10... | collective-permute-start | bytes 61448 | tf_op jit(solution)/shard_map/ppermute | solution.py:554
  10.3 4.0 %collective-permute-start.3 = (f32[40,128]{1,0:T(8,128)S(1)}, f32[40,128]{1,0:T(8,128)S(1)}, u32[]{:S(2)}, u32[]{:S(2)}) collective-permute-start(f32[40,128]{1,0:T(8,128)S(1)} %get-tuple-element.62.refs_4__0_.refs_5__0_.refs_6__0_), channel_id=1, source_target_pairs={{0,16},{8,24},{16,0},{24,8},{1,17},{9,25},{17,1},{25,9},{2,18},{10... | collective-permute-start | bytes 61448 | tf_op jit(solution)/shard_map/ppermute | solution.py:554
  11.2 3.1 %collective-permute-start.2 = (f32[40,128]{1,0:T(8,128)S(1)}, f32[40,128]{1,0:T(8,128)S(1)}, u32[]{:S(2)}, u32[]{:S(2)}) collective-permute-start(f32[40,128]{1,0:T(8,128)S(1)} %get-tuple-element.62.refs_4__0_.refs_5__0_.refs_6__0_), channel_id=1, source_target_pairs={{0,8},{8,0},{16,24},{24,16},{1,9},{9,1},{17,25},{25,17},{2,10},{10... | collective-permute-start | bytes 61448 | tf_op jit(solution)/shard_map/ppermute | solution.py:554
  14.3 6.2 %copy-start = (bf16[8192,256]{1,0:T(8,128)(2,1)S(1)}, bf16[8192,256]{1,0:T(8,128)(2,1)}, u32[]{:S(2)}) copy-start(bf16[8192,256]{1,0:T(8,128)(2,1)} %refs_8_.3) | copy-start | bytes 12582916
  16.0 7.9 %collective-permute-start.5 = (bf16[2,128,128]{2,1,0:T(8,128)(2,1)S(1)}, bf16[2,128,128]{2,1,0:T(8,128)(2,1)S(1)}, u32[]{:S(2)}, u32[]{:S(2)}) collective-permute-start(bf16[2,128,128]{2,1,0:T(8,128)(2,1)S(1)} %get-tuple-element.68), channel_id=1, source_target_pairs={{0,1},{2,3},{4,5},{6,7},{1,0},{3,2},{5,4},{7,6},{8,9},{10,11},{12,... | collective-permute-start | bytes 196616 | tf_op jit(solution)/shard_map/ppermute | solution.py:548
  19.8 4.0 %collective-permute-start.6 = (bf16[2,128,128]{2,1,0:T(8,128)(2,1)S(1)}, bf16[2,128,128]{2,1,0:T(8,128)(2,1)S(1)}, u32[]{:S(2)}, u32[]{:S(2)}) collective-permute-start(bf16[2,128,128]{2,1,0:T(8,128)(2,1)S(1)} %get-tuple-element.69), channel_id=1, source_target_pairs={{1,2},{3,4},{5,6},{2,1},{4,3},{6,5},{9,10},{11,12},{13,14},{10,9},... | collective-permute-start | bytes 196616 | tf_op jit(solution)/shard_map/ppermute | solution.py:548
  24.1 3.5 %collective-permute-start.9 = (f32[40,128]{1,0:T(8,128)S(1)}, f32[40,128]{1,0:T(8,128)S(1)}, u32[]{:S(2)}, u32[]{:S(2)}) collective-permute-start(f32[40,128]{1,0:T(8,128)S(1)} %get-tuple-element.72.refs_7__0_), channel_id=1, source_target_pairs={{0,24},{8,16},{16,8},{24,0},{1,25},{9,17},{17,9},{25,1},{2,26},{10... | collective-permute-start | bytes 61448 | tf_op jit(solution)/shard_map/ppermute | solution.py:554
  24.2 3.8 %collective-permute-start.8 = (f32[40,128]{1,0:T(8,128)S(1)}, f32[40,128]{1,0:T(8,128)S(1)}, u32[]{:S(2)}, u32[]{:S(2)}) collective-permute-start(f32[40,128]{1,0:T(8,128)S(1)} %get-tuple-element.72.refs_7__0_), channel_id=1, source_target_pairs={{0,16},{8,24},{16,0},{24,8},{1,17},{9,25},{17,1},{25,9},{2,18},{10... | collective-permute-start | bytes 61448 | tf_op jit(solution)/shard_map/ppermute | solution.py:554
  25.7 2.4 %collective-permute-start.7 = (f32[40,128]{1,0:T(8,128)S(1)}, f32[40,128]{1,0:T(8,128)S(1)}, u32[]{:S(2)}, u32[]{:S(2)}) collective-permute-start(f32[40,128]{1,0:T(8,128)S(1)} %get-tuple-element.72.refs_7__0_), channel_id=1, source_target_pairs={{0,8},{8,0},{16,24},{24,16},{1,9},{9,1},{17,25},{25,17},{2,10},{10... | collective-permute-start | bytes 61448 | tf_op jit(solution)/shard_map/ppermute | solution.py:554
  44.9 3.2 %collective-permute-start.12 = (f32[24,128]{1,0:T(8,128)S(1)}, f32[24,128]{1,0:T(8,128)S(1)}, u32[]{:S(2)}, u32[]{:S(2)}) collective-permute-start(f32[24,128]{1,0:T(8,128)S(1)} %get-tuple-element.78.refs_5__0_), channel_id=1, source_target_pairs={{0,24},{8,16},{16,8},{24,0},{1,25},{9,17},{17,9},{25,1},{2,26},{10... | collective-permute-start | bytes 36872 | tf_op jit(solution)/shard_map/ppermute | solution.py:554
  45.2 3.7 %collective-permute-start.11 = (f32[24,128]{1,0:T(8,128)S(1)}, f32[24,128]{1,0:T(8,128)S(1)}, u32[]{:S(2)}, u32[]{:S(2)}) collective-permute-start(f32[24,128]{1,0:T(8,128)S(1)} %get-tuple-element.78.refs_5__0_), channel_id=1, source_target_pairs={{0,16},{8,24},{16,0},{24,8},{1,17},{9,25},{17,1},{25,9},{2,18},{10... | collective-permute-start | bytes 36872 | tf_op jit(solution)/shard_map/ppermute | solution.py:554
  46.7 2.1 %collective-permute-start.10 = (f32[24,128]{1,0:T(8,128)S(1)}, f32[24,128]{1,0:T(8,128)S(1)}, u32[]{:S(2)}, u32[]{:S(2)}) collective-permute-start(f32[24,128]{1,0:T(8,128)S(1)} %get-tuple-element.78.refs_5__0_), channel_id=1, source_target_pairs={{0,8},{8,0},{16,24},{24,16},{1,9},{9,1},{17,25},{25,17},{2,10},{10... | collective-permute-start | bytes 36872 | tf_op jit(solution)/shard_map/ppermute | solution.py:554
  50.5 4.9 %collective-permute-start.13 = (bf16[2,128,128]{2,1,0:T(8,128)(2,1)S(1)}, bf16[2,128,128]{2,1,0:T(8,128)(2,1)S(1)}, u32[]{:S(2)}, u32[]{:S(2)}) collective-permute-start(bf16[2,128,128]{2,1,0:T(8,128)(2,1)S(1)} %get-tuple-element.84), channel_id=1, source_target_pairs={{0,1},{2,3},{4,5},{6,7},{1,0},{3,2},{5,4},{7,6},{8,9},{10,11},{12,... | collective-permute-start | bytes 196616 | tf_op jit(solution)/shard_map/ppermute | solution.py:548
  51.2 4.2 %collective-permute-start.14 = (bf16[2,128,128]{2,1,0:T(8,128)(2,1)S(1)}, bf16[2,128,128]{2,1,0:T(8,128)(2,1)S(1)}, u32[]{:S(2)}, u32[]{:S(2)}) collective-permute-start(bf16[2,128,128]{2,1,0:T(8,128)(2,1)S(1)} %get-tuple-element.85), channel_id=1, source_target_pairs={{1,2},{3,4},{5,6},{2,1},{4,3},{6,5},{9,10},{11,12},{13,14},{10,9},... | collective-permute-start | bytes 196616 | tf_op jit(solution)/shard_map/ppermute | solution.py:548
  55.7 3.5 %collective-permute-start.17 = (f32[40,128]{1,0:T(8,128)S(1)}, f32[40,128]{1,0:T(8,128)S(1)}, u32[]{:S(2)}, u32[]{:S(2)}) collective-permute-start(f32[40,128]{1,0:T(8,128)S(1)} %get-tuple-element.88.refs_7__0_), channel_id=1, source_target_pairs={{0,24},{8,16},{16,8},{24,0},{1,25},{9,17},{17,9},{25,1},{2,26},{10... | collective-permute-start | bytes 61448 | tf_op jit(solution)/shard_map/ppermute | solution.py:554
  55.8 3.8 %collective-permute-start.16 = (f32[40,128]{1,0:T(8,128)S(1)}, f32[40,128]{1,0:T(8,128)S(1)}, u32[]{:S(2)}, u32[]{:S(2)}) collective-permute-start(f32[40,128]{1,0:T(8,128)S(1)} %get-tuple-element.88.refs_7__0_), channel_id=1, source_target_pairs={{0,16},{8,24},{16,0},{24,8},{1,17},{9,25},{17,1},{25,9},{2,18},{10... | collective-permute-start | bytes 61448 | tf_op jit(solution)/shard_map/ppermute | solution.py:554
  57.3 2.3 %collective-permute-start.15 = (f32[40,128]{1,0:T(8,128)S(1)}, f32[40,128]{1,0:T(8,128)S(1)}, u32[]{:S(2)}, u32[]{:S(2)}) collective-permute-start(f32[40,128]{1,0:T(8,128)S(1)} %get-tuple-element.88.refs_7__0_), channel_id=1, source_target_pairs={{0,8},{8,0},{16,24},{24,16},{1,9},{9,1},{17,25},{25,17},{2,10},{10... | collective-permute-start | bytes 61448 | tf_op jit(solution)/shard_map/ppermute | solution.py:554

commit v8 on v6

--- a/solution.py
+++ b/solution.py
@@ -176,7 +176,7 @@
     return jnp.where(even, second, first), jnp.where(even, first, second)
 
 
-def prep_rim_kernel(first, second, columns, rows_own, pay_own, s3, p3, pinv3, z3, rows, pay):
+def prep_rim_kernel(second, first, columns, rows_own, pay_own, s3, p3, pinv3, z3, rows, pay):
     rims, frames = s3.shape[0], s3.shape[1]
     own = rows_own.shape[1] - padded8(1)
     chunks = own + 2 * RIM
@@ -405,7 +405,7 @@
         compute()
 
 
-def border_kernel(zones, got_a, got_b, p3, pinv3, rows, pay_inner, r3, pay):
+def border_kernel(zones, got_b, got_a, p3, pinv3, rows, pay_inner, r3, pay):
     chunks = chunk_count(p3)
     frames = zones.shape[1]
     sums_table = table(frames, True)
@@ -541,7 +541,8 @@
         both = [(i, i + 1) for i in range(start, size - 1, 2)]
         return both + [(j, i) for i, j in both]
 
-    return lax.ppermute(first, "tile", pairs(0)), lax.ppermute(second, "tile", pairs(1))
+    second = lax.ppermute(second, "tile", pairs(1))
+    return lax.ppermute(first, "tile", pairs(0)), second
 
 
 def shared_blocks(value):
@@ -594,7 +595,7 @@
         "prep_rim",
         0.3,
         (split[1],) * 4 + (f32(3, lines, LANES), f32(2, lines, LANES)),
-        (first, second, columns, rows, pay),
+        (second, first, columns, rows, pay),
     )
     s3, p3, pinv3, z3 = zip(owns, rims)
     constants = pays = shared_blocks(pay)
@@ -645,7 +646,7 @@
             "border",
             0.3,
             (f32(*border), f32(2, lines, LANES)),
-            (zones, got_a, got_b, p3, pinv3, rows, pay),
+            (zones, got_b, got_a, p3, pinv3, rows, pay),
             keep=held,
         )
         pays = shared_blocks(pay)

time: 76.3 us -> 77.1 us (1.010)
  starting transfers between devices: 17.2 us -> 23.6 us
  blocking collectives: 26.5 us -> 21.2 us
    ppermute x6, starting transfers between devices: 9.47 us -> 15.8 us  [the longest x3 13.8 us: swapped(): return (lax.ppermute(first, 'tile', pairs(0)), second)]
    all_to_all x2, blocking collectives: 26.5 us -> 21.2 us  [per_device(): stats = lax.all_to_all(stats, ('tile', 'tm'), 0, 0)]
where the time goes in v8:
time: 77.1 us; the launch traced here: 76.8 us
  starting transfers between devices  23.6 us (31%)
  blocking collectives  21.2 us (27%)
  Pallas kernels  19.6 us (25%)
  waiting for transfers between devices  8.87 us (12%)
  local copies, waits for them, and re-layouts  2.58 us (3%)
  between operations  0.99 us (1%)
    all_to_all x2, blocking collectives, per_device(): stats = lax.all_to_all(stats, ('tile', 'tm'), 0, 0)  21.2 us
    pallas_call x13, Pallas kernels, call(): pl.pallas_call(body, name=name, out_shape=outs, in_specs=in_specs, out_sp...  19.6 us
    ppermute x3, starting transfers between devices, swapped(): return (lax.ppermute(first, 'tile', pairs(0)), second)  13.8 us
    ppermute x12, waiting for transfers between devices, shared_blocks(): lax.ppermute(value, 'tm', [(i, i ^ j) for i in range(size)])  8.85 us
    ppermute x12, starting transfers between devices, shared_blocks(): lax.ppermute(value, 'tm', [(i, i ^ j) for i in range(size)])  7.73 us
    unnamed x12, local copies, waits for them, and re-layouts  2.58 us
    ppermute x3, starting transfers between devices, swapped(): second = lax.ppermute(second, 'tile', pairs(1))  1.99 us
  transfers between devices with their start and end apart: 18, of which 8 were waited for; matrix products, arithmetic and copies ran while one was open for 0% of the time, Pallas kernels for 11%

profile of v8, /device:TPU:0, one launch (start us, length us, event | category | flops | bytes accessed | tf_op | source)
XLA Modules:
  0.0 76.8 jit_solution(10622121902490075118)
XLA Ops:
  0.6 0.0 copy-start.4
  0.6 0.7 copy-done.4
  1.3 0.9 %rims.1 = (f32[136,128]{1,0:T(8,128)S(1)}, f32[136,128]{1,0:T(8,128)S(1)}, f32[16,128]{1,0:T(8,128)S(1)}) custom-call(f32[2048,128]{1,0:T(8,128)} %refs_0_.3, f32[16,128]{1,0:T(8,128)S(1)} %bitcast.9), custom_call_target="tpu_custom_call" | custom-call | flops 100000000 | bytes 3000000 | tf_op jit(solution)/shard_map/rims/pallas_call | solution.py:520
  2.2 0.7 collective-permute-start
  2.9 5.8 %collective-permute-start.1 = (f32[136,128]{1,0:T(8,128)S(1)}, f32[136,128]{1,0:T(8,128)S(1)}, u32[]{:S(2)}, u32[]{:S(2)}) collective-permute-start(f32[136,128]{1,0:T(8,128)S(1)} %get-tuple-element.50), channel_id=1, source_target_pairs={{0,1},{2,3},{4,5},{6,7},{1,0},{3,2},{5,4},{7,6},{8,9},{10,11},{12,... | collective-permute-start | bytes 208904 | tf_op jit(solution)/shard_map/ppermute | solution.py:545
  8.7 0.0 copy-start.2
  8.7 1.2 %copy-done.2 = f32[2048,128]{1,0:T(8,128)S(1)} copy-done((f32[2048,128]{1,0:T(8,128)S(1)}, f32[2048,128]{1,0:T(8,128)}, u32[]{:S(2)}) %copy-start.2) | copy-done | bytes 1048600
  9.9 0.0 copy-start.5
  9.9 0.7 copy-done.5
  10.6 0.0 copy-start.1
  10.6 0.0 copy-start.3
  10.6 1.4 %prep_own.1 = (f32[16,128,128]{2,1,0:T(8,128)S(1)}, f32[16,128,128]{2,1,0:T(8,128)S(1)}, f32[16,128,128]{2,1,0:T(8,128)S(1)}, f32[16,128,128]{2,1,0:T(8,128)S(1)...) custom-call(f32[2048,128]{1,0:T(8,128)S(1)} %copy-done.2, ...), custom_call_target="tpu_custom_call" | custom-call | flops 160000000 | bytes 4800000 | tf_op jit(solution)/shard_map/prep_own/pallas_call | solution.py:520
  12.0 0.0 collective-permute-done.refs_0_
  12.0 0.0 collective-permute-done.1.refs_1_
  12.1 0.3 prep_rim.1
  12.3 0.4 collective-permute-start.4
  12.8 1.2 %collective-permute-start.3 = (f32[2,24,128]{2,1,0:T(8,128)S(1)}, f32[2,24,128]{2,1,0:T(8,128)S(1)}, u32[]{:S(2)}, u32[]{:S(2)}) collective-permute-start(f32[2,24,128]{2,1,0:T(8,128)S(1)} %get-tuple-element.62.refs_4__0_.refs_5__0_.refs_6__0_), channel_id=1, source_target_pairs={{0,16},{8,24},{16,0},{24,8},{1,17},{9,25},{17,1},{25,9},{2,18},{10... | collective-permute-start | bytes 73736 | tf_op jit(solution)/shard_map/ppermute | solution.py:551
  14.0 0.3 collective-permute-start.2
  14.3 1.6 %collective-permute-done.4.refs_4__3_.refs_5__3_.refs_6__3_ = f32[2,24,128]{2,1,0:T(8,128)S(1)} collective-permute-done((f32[2,24,128]{2,1,0:T(8,128)S(1)}, f32[2,24,128]{2,1,0:T(8,128)S(1)}, u32[]{:S(2)}, u32[]{:S(2)}) %collective-permute-start.4) | collective-permute-done | bytes 24608 | tf_op jit(solution)/shard_map/ppermute | solution.py:551
  15.9 0.7 collective-permute-done.3.refs_4__2_.refs_5__2_.refs_6__2_
  16.6 0.0 collective-permute-done.2.refs_4__1_.refs_5__1_.refs_6__1_
  16.6 0.0 copy-done.1
  16.6 0.0 copy-done.3
  16.6 0.0 copy-start
  16.6 1.7 %edge.2 = (bf16[2304,128]{1,0:T(8,128)(2,1)S(1)}, f32[4,128,128]{2,1,0:T(8,128)S(1)}, f32[4,128,128]{2,1,0:T(8,128)S(1)}, bf16[2,128,128]{2,1,0:T(8,128)(2,1)S(1)}, bf16[2,128,128]{2,1,0:T(8,128)(2,1)S(1)}) custom-call(s32[4,32]{1,0:T(4,128)S(1)} %bitcast.3, f32[16,128,128]{2,1,0:T(8,128)S(1)} %get-tuple-element.60.refs_1__0_, ...), custom_call_target="tpu_custom_call" | custom-call | flops 250000000 | bytes 7500000 | tf_op jit(solution)/shard_map/edge/pallas_call | solution.py:520
  18.3 0.7 collective-permute-start.5
  19.0 4.7 %collective-permute-start.6 = (bf16[2,128,128]{2,1,0:T(8,128)(2,1)S(1)}, bf16[2,128,128]{2,1,0:T(8,128)(2,1)S(1)}, u32[]{:S(2)}, u32[]{:S(2)}) collective-permute-start(bf16[2,128,128]{2,1,0:T(8,128)(2,1)S(1)} %get-tuple-element.69), channel_id=1, source_target_pairs={{0,1},{2,3},{4,5},{6,7},{1,0},{3,2},{5,4},{7,6},{8,9},{10,11},{12,... | collective-permute-start | bytes 196616 | tf_op jit(solution)/shard_map/ppermute | solution.py:545
  23.7 0.0 copy-done
  23.7 3.3 %inner.2 = (f32[14,128,128]{2,1,0:T(8,128)S(1)}, f32[2,24,128]{2,1,0:T(8,128)S(1)}) custom-call(s32[4,32]{1,0:T(4,128)S(1)} %bitcast.4, f32[16,128,128]{2,1,0:T(8,128)S(1)} %get-tuple-element.55.refs_2__0_.refs_1__0_.refs_3__0_, f32[2,128,128]{2,1,0:T(8,128)S(1)} %get-tuple-element.56.refs_2__1_.refs_1__1_.refs_3__1_, ...), custom_call_target="tpu_custom_call" | custom-call | flops 400000000 | bytes 12000000 | tf_op jit(solution)/shard_map/inner/pallas_call | solution.py:520
  27.0 0.0 collective-permute-done.5.refs_1_
  27.0 0.0 collective-permute-done.6.refs_2_
  27.0 0.3 border.2
  27.3 0.1 collective-permute-start.9
  27.4 1.2 %collective-permute-start.8 = (f32[2,24,128]{2,1,0:T(8,128)S(1)}, f32[2,24,128]{2,1,0:T(8,128)S(1)}, u32[]{:S(2)}, u32[]{:S(2)}) collective-permute-start(f32[2,24,128]{2,1,0:T(8,128)S(1)} %get-tuple-element.72.refs_7__0_), channel_id=1, source_target_pairs={{0,16},{8,24},{16,0},{24,8},{1,17},{9,25},{17,1},{25,9},{2,18},{10... | collective-permute-start | bytes 73736 | tf_op jit(solution)/shard_map/ppermute | solution.py:551
  28.6 0.7 collective-permute-start.7
  29.2 1.4 %collective-permute-done.9.refs_7__3_ = f32[2,24,128]{2,1,0:T(8,128)S(1)} collective-permute-done((f32[2,24,128]{2,1,0:T(8,128)S(1)}, f32[2,24,128]{2,1,0:T(8,128)S(1)}, u32[]{:S(2)}, u32[]{:S(2)}) %collective-permute-start.9) | collective-permute-done | bytes 24608 | tf_op jit(solution)/shard_map/ppermute | solution.py:551
  30.6 0.8 %collective-permute-done.8.refs_7__2_ = f32[2,24,128]{2,1,0:T(8,128)S(1)} collective-permute-done((f32[2,24,128]{2,1,0:T(8,128)S(1)}, f32[2,24,128]{2,1,0:T(8,128)S(1)}, u32[]{:S(2)}, u32[]{:S(2)}) %collective-permute-start.8) | collective-permute-done | bytes 24608 | tf_op jit(solution)/shard_map/ppermute | solution.py:551
  31.5 0.0 collective-permute-done.7.refs_7__1_
  31.5 2.1 %direction.2 = (f32[18,128,128]{2,1,0:T(8,128)S(1)}, f32[32,2,128]{2,1,0:T(2,128)S(1)}) custom-call(s32[4,32]{1,0:T(4,128)S(1)} %bitcast.5, f32[14,128,128]{2,1,0:T(8,128)S(1)} %get-tuple-element.66.refs_1_, f32[4,128,128]{2,1,0:T(8,128)S(1)} %get-tuple-element.71.refs_2_, f32[16,128,128]{2,1,0:T(8,128)S(1)} %get-tuple-element.55.refs_2__0_.refs_1__0_.refs_3__0_, ...), custom_call_target="tpu_custom_call" | custom-call | flops 400000000 | bytes 12000000 | tf_op jit(solution)/shard_map/direction/pallas_call | solution.py:520
  33.6 11.5 %all_to_all.10.refs_2_ = f32[32,2,128]{2,1,0:T(2,128)S(1)} all-to-all(f32[32,2,128]{2,1,0:T(2,128)S(1)} %get-tuple-element.74), channel_id=1, replica_groups=mesh['tm'=4,'tile'=8] {'tile','tm'}, dimensions={0} | all-to-all | bytes 65536 | tf_op jit(solution)/shard_map/all_to_all | solution.py:667
  45.1 0.7 update.1
  45.8 0.3 collective-permute-start.12
  46.1 1.5 %collective-permute-start.11 = (f32[1,24,128]{2,1,0:T(8,128)S(1)}, f32[1,24,128]{2,1,0:T(8,128)S(1)}, u32[]{:S(2)}, u32[]{:S(2)}) collective-permute-start(f32[1,24,128]{2,1,0:T(8,128)S(1)} %get-tuple-element.78.refs_5__0_), channel_id=1, source_target_pairs={{0,16},{8,24},{16,0},{24,8},{1,17},{9,25},{17,1},{25,9},{2,18},{10... | collective-permute-start | bytes 36872 | tf_op jit(solution)/shard_map/ppermute | solution.py:551
  47.7 0.1 collective-permute-start.10
  47.8 1.2 %collective-permute-done.12.refs_5__3_ = f32[1,24,128]{2,1,0:T(8,128)S(1)} collective-permute-done((f32[1,24,128]{2,1,0:T(8,128)S(1)}, f32[1,24,128]{2,1,0:T(8,128)S(1)}, u32[]{:S(2)}, u32[]{:S(2)}) %collective-permute-start.12) | collective-permute-done | bytes 12320 | tf_op jit(solution)/shard_map/ppermute | solution.py:551
  49.0 0.8 %collective-permute-done.11.refs_5__2_ = f32[1,24,128]{2,1,0:T(8,128)S(1)} collective-permute-done((f32[1,24,128]{2,1,0:T(8,128)S(1)}, f32[1,24,128]{2,1,0:T(8,128)S(1)}, u32[]{:S(2)}, u32[]{:S(2)}) %collective-permute-start.11) | collective-permute-done | bytes 12320 | tf_op jit(solution)/shard_map/ppermute | solution.py:551
  49.8 0.0 collective-permute-done.10.refs_5__1_
  49.8 1.7 %edge.3 = (bf16[2304,128]{1,0:T(8,128)(2,1)S(1)}, f32[4,128,128]{2,1,0:T(8,128)S(1)}, f32[4,128,128]{2,1,0:T(8,128)S(1)}, bf16[2,128,128]{2,1,0:T(8,128)(2,1)S(1...) custom-call(s32[4,32]{1,0:T(4,128)S(1)} %bitcast.6, f32[16,128,128]{2,1,0:T(8,128)S(1)} %get-tuple-element.76.refs_1__0_, ...), custom_call_target="tpu_custom_call" | custom-call | flops 250000000 | bytes 7500000 | tf_op jit(solution)/shard_map/edge/pallas_call | solution.py:520
  51.5 0.7 collective-permute-start.13
  52.2 3.4 %collective-permute-start.14 = (bf16[2,128,128]{2,1,0:T(8,128)(2,1)S(1)}, bf16[2,128,128]{2,1,0:T(8,128)(2,1)S(1)}, u32[]{:S(2)}, u32[]{:S(2)}) collective-permute-start(bf16[2,128,128]{2,1,0:T(8,128)(2,1)S(1)} %get-tuple-element.85), channel_id=1, source_target_pairs={{0,1},{2,3},{4,5},{6,7},{1,0},{3,2},{5,4},{7,6},{8,9},{10,11},{12,... | collective-permute-start | bytes 196616 | tf_op jit(solution)/shard_map/ppermute | solution.py:545
  55.5 3.5 %inner.3 = (f32[14,128,128]{2,1,0:T(8,128)S(1)}, f32[2,24,128]{2,1,0:T(8,128)S(1)}, f32[2048,128]{1,0:T(8,128)}) custom-call(s32[4,32]{1,0:T(4,128)S(1)} %bitcast.7, f32[16,128,128]{2,1,0:T(8,128)S(1)} %get-tuple-element.55.refs_2__0_.refs_1__0_.refs_3__0_, f32[2,128,128]{2,1,0:T(8,128)S(1)} %get-tuple-element.56.refs_2__1_.refs_1__1_.refs_3__1_, ...), custom_call_target="tpu_custom_call" | custom-call | flops 400000000 | bytes 12000000 | tf_op jit(solution)/shard_map/inner/pallas_call | solution.py:520
  59.1 0.0 collective-permute-done.13.refs_1_
  59.1 0.0 collective-permute-done.14.refs_2_
  59.1 0.3 border.3
  59.4 0.2 collective-permute-start.17
  59.6 1.0 %collective-permute-start.16 = (f32[2,24,128]{2,1,0:T(8,128)S(1)}, f32[2,24,128]{2,1,0:T(8,128)S(1)}, u32[]{:S(2)}, u32[]{:S(2)}) collective-permute-start(f32[2,24,128]{2,1,0:T(8,128)S(1)} %get-tuple-element.88.refs_7__0_), channel_id=1, source_target_pairs={{0,16},{8,24},{16,0},{24,8},{1,17},{9,25},{17,1},{25,9},{2,18},{10... | collective-permute-start | bytes 73736 | tf_op jit(solution)/shard_map/ppermute | solution.py:551
  60.6 0.7 collective-permute-start.15
  61.3 1.4 %collective-permute-done.17.refs_7__3_ = f32[2,24,128]{2,1,0:T(8,128)S(1)} collective-permute-done((f32[2,24,128]{2,1,0:T(8,128)S(1)}, f32[2,24,128]{2,1,0:T(8,128)S(1)}, u32[]{:S(2)}, u32[]{:S(2)}) %collective-permute-start.17) | collective-permute-done | bytes 24608 | tf_op jit(solution)/shard_map/ppermute | solution.py:551
  62.7 0.9 %collective-permute-done.16.refs_7__2_ = f32[2,24,128]{2,1,0:T(8,128)S(1)} collective-permute-done((f32[2,24,128]{2,1,0:T(8,128)S(1)}, f32[2,24,128]{2,1,0:T(8,128)S(1)}, u32[]{:S(2)}, u32[]{:S(2)}) %collective-permute-start.16) | collective-permute-done | bytes 24608 | tf_op jit(solution)/shard_map/ppermute | solution.py:551
  63.6 0.0 collective-permute-done.15.refs_7__1_
  63.6 2.1 %direction.3 = (f32[18,128,128]{2,1,0:T(8,128)S(1)}, f32[32,2,128]{2,1,0:T(2,128)S(1)}) custom-call(s32[4,32]{1,0:T(4,128)S(1)} %bitcast.8, f32[14,128,128]{2,1,0:T(8,128)S(1)} %get-tuple-element.82.refs_1_, f32[4,128,128]{2,1,0:T(8,128)S(1)} %get-tuple-element.87.refs_2_, f32[16,128,128]{2,1,0:T(8,128)S(1)} %get-tuple-element.55.refs_2__0_.refs_1__0_.refs_3__0_, ...), custom_call_target="tpu_custom_call" | custom-call | flops 400000000 | bytes 12000000 | tf_op jit(solution)/shard_map/direction/pallas_call | solution.py:520
  65.7 9.6 %all_to_all.11.refs_2_ = f32[32,2,128]{2,1,0:T(2,128)S(1)} all-to-all(f32[32,2,128]{2,1,0:T(2,128)S(1)} %get-tuple-element.90), channel_id=1, replica_groups=mesh['tm'=4,'tile'=8] {'tile','tm'}, dimensions={0} | all-to-all | bytes 65536 | tf_op jit(solution)/shard_map/all_to_all | solution.py:667
  75.3 1.3 %final.1 = f32[2048,128]{1,0:T(8,128)} custom-call(f32[16,128,128]{2,1,0:T(8,128)S(1)} %get-tuple-element.75.refs_8__0_.refs_9__0_.refs_7__0_.refs_0_, f32[18,128,128]{2,1,0:T(8,128)S(1)} %get-tuple-element.89.refs_1_, f32[32,2,128]{2,1,0:T(2,128)S(1)} %all_to_all.11.refs_2_), custom_call_target="tpu_custom_call" | custom-call | flops 140000000 | bytes 4200000 | tf_op jit(solution)/shard_map/final/pallas_call | solution.py:520
Async XLA Ops:
  0.6 0.7 copy-start.4
  2.2 9.8 %collective-permute-start = (f32[136,128]{1,0:T(8,128)S(1)}, f32[136,128]{1,0:T(8,128)S(1)}, u32[]{:S(2)}, u32[]{:S(2)}) collective-permute-start(f32[136,128]{1,0:T(8,128)S(1)} %get-tuple-element.49), channel_id=1, source_target_pairs={{1,2},{3,4},{5,6},{2,1},{4,3},{6,5},{9,10},{11,12},{13,14},{10,9},... | collective-permute-start | bytes 208904 | tf_op jit(solution)/shard_map/ppermute | solution.py:544
  2.9 9.1 %collective-permute-start.1 = (f32[136,128]{1,0:T(8,128)S(1)}, f32[136,128]{1,0:T(8,128)S(1)}, u32[]{:S(2)}, u32[]{:S(2)}) collective-permute-start(f32[136,128]{1,0:T(8,128)S(1)} %get-tuple-element.50), channel_id=1, source_target_pairs={{0,1},{2,3},{4,5},{6,7},{1,0},{3,2},{5,4},{7,6},{8,9},{10,11},{12,... | collective-permute-start | bytes 208904 | tf_op jit(solution)/shard_map/ppermute | solution.py:545
  8.7 1.2 %copy-start.2 = (f32[2048,128]{1,0:T(8,128)S(1)}, f32[2048,128]{1,0:T(8,128)}, u32[]{:S(2)}) copy-start(f32[2048,128]{1,0:T(8,128)} %refs_0_.3) | copy-start | bytes 3145732
  9.9 0.7 copy-start.5
  10.6 6.0 %copy-start.1 = (bf16[8192,128]{1,0:T(8,128)(2,1)S(1)}, bf16[8192,128]{1,0:T(8,128)(2,1)}, u32[]{:S(2)}) copy-start(bf16[8192,128]{1,0:T(8,128)(2,1)} %refs_7_.7) | copy-start | bytes 6291460
  10.6 6.0 %copy-start.3 = (s32[32,4]{0,1:T(4,128)S(1)}, s32[32,4]{0,1:T(4,128)}, u32[]{:S(2)}) copy-start(s32[32,4]{0,1:T(4,128)} %param.8) | copy-start | bytes 1540
  12.3 3.5 %collective-permute-start.4 = (f32[2,24,128]{2,1,0:T(8,128)S(1)}, f32[2,24,128]{2,1,0:T(8,128)S(1)}, u32[]{:S(2)}, u32[]{:S(2)}) collective-permute-start(f32[2,24,128]{2,1,0:T(8,128)S(1)} %get-tuple-element.62.refs_4__0_.refs_5__0_.refs_6__0_), channel_id=1, source_target_pairs={{0,24},{8,16},{16,8},{24,0},{1,25},{9,17},{17,9},{25,1},{2,26},{10... | collective-permute-start | bytes 73736 | tf_op jit(solution)/shard_map/ppermute | solution.py:551
  12.8 3.8 %collective-permute-start.3 = (f32[2,24,128]{2,1,0:T(8,128)S(1)}, f32[2,24,128]{2,1,0:T(8,128)S(1)}, u32[]{:S(2)}, u32[]{:S(2)}) collective-permute-start(f32[2,24,128]{2,1,0:T(8,128)S(1)} %get-tuple-element.62.refs_4__0_.refs_5__0_.refs_6__0_), channel_id=1, source_target_pairs={{0,16},{8,24},{16,0},{24,8},{1,17},{9,25},{17,1},{25,9},{2,18},{10... | collective-permute-start | bytes 73736 | tf_op jit(solution)/shard_map/ppermute | solution.py:551
  14.0 2.6 %collective-permute-start.2 = (f32[2,24,128]{2,1,0:T(8,128)S(1)}, f32[2,24,128]{2,1,0:T(8,128)S(1)}, u32[]{:S(2)}, u32[]{:S(2)}) collective-permute-start(f32[2,24,128]{2,1,0:T(8,128)S(1)} %get-tuple-element.62.refs_4__0_.refs_5__0_.refs_6__0_), channel_id=1, source_target_pairs={{0,8},{8,0},{16,24},{24,16},{1,9},{9,1},{17,25},{25,17},{2,10},{10... | collective-permute-start | bytes 73736 | tf_op jit(solution)/shard_map/ppermute | solution.py:551
  16.6 7.1 %copy-start = (bf16[8192,256]{1,0:T(8,128)(2,1)S(1)}, bf16[8192,256]{1,0:T(8,128)(2,1)}, u32[]{:S(2)}) copy-start(bf16[8192,256]{1,0:T(8,128)(2,1)} %refs_8_.3) | copy-start | bytes 12582916
  18.3 8.7 %collective-permute-start.5 = (bf16[2,128,128]{2,1,0:T(8,128)(2,1)S(1)}, bf16[2,128,128]{2,1,0:T(8,128)(2,1)S(1)}, u32[]{:S(2)}, u32[]{:S(2)}) collective-permute-start(bf16[2,128,128]{2,1,0:T(8,128)(2,1)S(1)} %get-tuple-element.68), channel_id=1, source_target_pairs={{1,2},{3,4},{5,6},{2,1},{4,3},{6,5},{9,10},{11,12},{13,14},{10,9},... | collective-permute-start | bytes 196616 | tf_op jit(solution)/shard_map/ppermute | solution.py:544
  19.0 8.0 %collective-permute-start.6 = (bf16[2,128,128]{2,1,0:T(8,128)(2,1)S(1)}, bf16[2,128,128]{2,1,0:T(8,128)(2,1)S(1)}, u32[]{:S(2)}, u32[]{:S(2)}) collective-permute-start(bf16[2,128,128]{2,1,0:T(8,128)(2,1)S(1)} %get-tuple-element.69), channel_id=1, source_target_pairs={{0,1},{2,3},{4,5},{6,7},{1,0},{3,2},{5,4},{7,6},{8,9},{10,11},{12,... | collective-permute-start | bytes 196616 | tf_op jit(solution)/shard_map/ppermute | solution.py:545
  27.3 3.3 %collective-permute-start.9 = (f32[2,24,128]{2,1,0:T(8,128)S(1)}, f32[2,24,128]{2,1,0:T(8,128)S(1)}, u32[]{:S(2)}, u32[]{:S(2)}) collective-permute-start(f32[2,24,128]{2,1,0:T(8,128)S(1)} %get-tuple-element.72.refs_7__0_), channel_id=1, source_target_pairs={{0,24},{8,16},{16,8},{24,0},{1,25},{9,17},{17,9},{25,1},{2,26},{10... | collective-permute-start | bytes 73736 | tf_op jit(solution)/shard_map/ppermute | solution.py:551
  27.4 4.1 %collective-permute-start.8 = (f32[2,24,128]{2,1,0:T(8,128)S(1)}, f32[2,24,128]{2,1,0:T(8,128)S(1)}, u32[]{:S(2)}, u32[]{:S(2)}) collective-permute-start(f32[2,24,128]{2,1,0:T(8,128)S(1)} %get-tuple-element.72.refs_7__0_), channel_id=1, source_target_pairs={{0,16},{8,24},{16,0},{24,8},{1,17},{9,25},{17,1},{25,9},{2,18},{10... | collective-permute-start | bytes 73736 | tf_op jit(solution)/shard_map/ppermute | solution.py:551
  28.6 2.9 %collective-permute-start.7 = (f32[2,24,128]{2,1,0:T(8,128)S(1)}, f32[2,24,128]{2,1,0:T(8,128)S(1)}, u32[]{:S(2)}, u32[]{:S(2)}) collective-permute-start(f32[2,24,128]{2,1,0:T(8,128)S(1)} %get-tuple-element.72.refs_7__0_), channel_id=1, source_target_pairs={{0,8},{8,0},{16,24},{24,16},{1,9},{9,1},{17,25},{25,17},{2,10},{10... | collective-permute-start | bytes 73736 | tf_op jit(solution)/shard_map/ppermute | solution.py:551
  45.8 3.2 %collective-permute-start.12 = (f32[1,24,128]{2,1,0:T(8,128)S(1)}, f32[1,24,128]{2,1,0:T(8,128)S(1)}, u32[]{:S(2)}, u32[]{:S(2)}) collective-permute-start(f32[1,24,128]{2,1,0:T(8,128)S(1)} %get-tuple-element.78.refs_5__0_), channel_id=1, source_target_pairs={{0,24},{8,16},{16,8},{24,0},{1,25},{9,17},{17,9},{25,1},{2,26},{10... | collective-permute-start | bytes 36872 | tf_op jit(solution)/shard_map/ppermute | solution.py:551
  46.1 3.7 %collective-permute-start.11 = (f32[1,24,128]{2,1,0:T(8,128)S(1)}, f32[1,24,128]{2,1,0:T(8,128)S(1)}, u32[]{:S(2)}, u32[]{:S(2)}) collective-permute-start(f32[1,24,128]{2,1,0:T(8,128)S(1)} %get-tuple-element.78.refs_5__0_), channel_id=1, source_target_pairs={{0,16},{8,24},{16,0},{24,8},{1,17},{9,25},{17,1},{25,9},{2,18},{10... | collective-permute-start | bytes 36872 | tf_op jit(solution)/shard_map/ppermute | solution.py:551
  47.7 2.2 %collective-permute-start.10 = (f32[1,24,128]{2,1,0:T(8,128)S(1)}, f32[1,24,128]{2,1,0:T(8,128)S(1)}, u32[]{:S(2)}, u32[]{:S(2)}) collective-permute-start(f32[1,24,128]{2,1,0:T(8,128)S(1)} %get-tuple-element.78.refs_5__0_), channel_id=1, source_target_pairs={{0,8},{8,0},{16,24},{24,16},{1,9},{9,1},{17,25},{25,17},{2,10},{10... | collective-permute-start | bytes 36872 | tf_op jit(solution)/shard_map/ppermute | solution.py:551
  51.5 7.6 %collective-permute-start.13 = (bf16[2,128,128]{2,1,0:T(8,128)(2,1)S(1)}, bf16[2,128,128]{2,1,0:T(8,128)(2,1)S(1)}, u32[]{:S(2)}, u32[]{:S(2)}) collective-permute-start(bf16[2,128,128]{2,1,0:T(8,128)(2,1)S(1)} %get-tuple-element.84), channel_id=1, source_target_pairs={{1,2},{3,4},{5,6},{2,1},{4,3},{6,5},{9,10},{11,12},{13,14},{10,9},... | collective-permute-start | bytes 196616 | tf_op jit(solution)/shard_map/ppermute | solution.py:544
  52.2 6.9 %collective-permute-start.14 = (bf16[2,128,128]{2,1,0:T(8,128)(2,1)S(1)}, bf16[2,128,128]{2,1,0:T(8,128)(2,1)S(1)}, u32[]{:S(2)}, u32[]{:S(2)}) collective-permute-start(bf16[2,128,128]{2,1,0:T(8,128)(2,1)S(1)} %get-tuple-element.85), channel_id=1, source_target_pairs={{0,1},{2,3},{4,5},{6,7},{1,0},{3,2},{5,4},{7,6},{8,9},{10,11},{12,... | collective-permute-start | bytes 196616 | tf_op jit(solution)/shard_map/ppermute | solution.py:545
  59.4 3.3 %collective-permute-start.17 = (f32[2,24,128]{2,1,0:T(8,128)S(1)}, f32[2,24,128]{2,1,0:T(8,128)S(1)}, u32[]{:S(2)}, u32[]{:S(2)}) collective-permute-start(f32[2,24,128]{2,1,0:T(8,128)S(1)} %get-tuple-element.88.refs_7__0_), channel_id=1, source_target_pairs={{0,24},{8,16},{16,8},{24,0},{1,25},{9,17},{17,9},{25,1},{2,26},{10... | collective-permute-start | bytes 73736 | tf_op jit(solution)/shard_map/ppermute | solution.py:551
  59.6 4.0 %collective-permute-start.16 = (f32[2,24,128]{2,1,0:T(8,128)S(1)}, f32[2,24,128]{2,1,0:T(8,128)S(1)}, u32[]{:S(2)}, u32[]{:S(2)}) collective-permute-start(f32[2,24,128]{2,1,0:T(8,128)S(1)} %get-tuple-element.88.refs_7__0_), channel_id=1, source_target_pairs={{0,16},{8,24},{16,0},{24,8},{1,17},{9,25},{17,1},{25,9},{2,18},{10... | collective-permute-start | bytes 73736 | tf_op jit(solution)/shard_map/ppermute | solution.py:551
  60.6 3.0 %collective-permute-start.15 = (f32[2,24,128]{2,1,0:T(8,128)S(1)}, f32[2,24,128]{2,1,0:T(8,128)S(1)}, u32[]{:S(2)}, u32[]{:S(2)}) collective-permute-start(f32[2,24,128]{2,1,0:T(8,128)S(1)} %get-tuple-element.88.refs_7__0_), channel_id=1, source_target_pairs={{0,8},{8,0},{16,24},{24,16},{1,9},{9,1},{17,25},{25,17},{2,10},{10... | collective-permute-start | bytes 73736 | tf_op jit(solution)/shard_map/ppermute | solution.py:551

commit v9 on v6

--- a/solution.py
+++ b/solution.py
@@ -353,8 +353,23 @@
         above = gathered(contrib, place, chunks - 2 * RIM + i, ranges)
         zones[i] = below
         zones[2 * RIM + i] = above
-        send_a[i] = jnp.where(even, above, below).astype(BF16)
-        send_b[i] = jnp.where(even, below, above).astype(BF16)
+        for to, other, held in ((send_a, above, below), (send_b, below, above)):
+            to[i] = jnp.where(even, other, held).astype(BF16)
+        lows = [value - value.astype(BF16).astype(F32) for value in (below, above)]
+        at = 2 * RIM + i % RIM
+        for to, takes in ((send_a, jnp.logical_not(even)), (send_b, even)):
+            if i < RIM:
+
+                @pl.when(takes)
+                def _():
+                    to[at] = lows[0].astype(BF16)
+
+            else:
+
+                @pl.when(jnp.logical_not(takes))
+                def _():
+                    to[at] = lows[1].astype(BF16)
+
         spill[i] = gathered(contrib, place, 2 * RIM + i, ranges)
         spill[2 * RIM + i] = gathered(contrib, place, chunks - 4 * RIM + i, ranges)
 
@@ -413,9 +428,13 @@
     even = lax.axis_index("tile") % 2 == 0
     for i in range(2 * RIM):
         both = sides(even, got_a[i].astype(F32), got_b[i].astype(F32))
+        at = 2 * RIM + i % RIM
+        lows = sides(even, got_a[at].astype(F32), got_b[at].astype(F32))
         for side, c in ((0, i), (1, chunks - 2 * RIM + i)):
             at = side * 2 * RIM + i
             field = zones[at] + both[side]
+            if (i >= RIM) == (side == 0):
+                field = field + lows[side]
             p, pinv = chunk(p3, c)[...], chunk(pinv3, c)[...]
             adjoint_chunk(sums_table, field, p, pinv, rows, c, r3.at[at], pay)
 
@@ -607,7 +626,6 @@
     staged = [pltpu.VMEM((neurons, frames), F32), pltpu.SemaphoreType.DMA((PARTS,))]
     middle = stripe * NEU_BLOCK // LANES // 2
     halves = (middle + 2 * RIM, chunks - middle)
-    zone = (2 * RIM, frames, LANES)
     border = (4 * RIM, frames, LANES)
     for iteration in range(ITERS):
         ends = iteration == ITERS - 1
@@ -619,8 +637,8 @@
                 bf16(chunks * LANES, frames),
                 f32(*border),
                 f32(*border),
-                bf16(*zone),
-                bf16(*zone),
+                bf16(3 * RIM, frames, LANES),
+                bf16(3 * RIM, frames, LANES),
             )
             + ((f32(neurons, frames),) if ends else ()),
             (pattern, z3, p3, rows, constants, pays, feet_ends, recording),

time: 76.3 us -> 77.3 us (1.013)
  blocking collectives: 26.5 us -> 27.3 us
    all_to_all x2, blocking collectives: 26.5 us -> 27.3 us  [per_device(): stats = lax.all_to_all(stats, ('tile', 'tm'), 0, 0)]
where the time goes in v9:
time: 77.3 us; the launch traced here: 77 us
  blocking collectives  27.3 us (35%)
  Pallas kernels  19.9 us (26%)
  starting transfers between devices  17.2 us (22%)
  waiting for transfers between devices  8.99 us (12%)
  local copies, waits for them, and re-layouts  2.58 us (3%)
  between operations  1.02 us (1%)
    all_to_all x2, blocking collectives, per_device(): stats = lax.all_to_all(stats, ('tile', 'tm'), 0, 0)  27.3 us
    pallas_call x13, Pallas kernels, call(): pl.pallas_call(body, name=name, out_shape=outs, in_specs=in_specs, out_sp...  19.9 us
    ppermute x12, waiting for transfers between devices, shared_blocks(): lax.ppermute(value, 'tm', [(i, i ^ j) for i in range(size)])  8.98 us
    ppermute x12, starting transfers between devices, shared_blocks(): lax.ppermute(value, 'tm', [(i, i ^ j) for i in range(size)])  7.73 us
    ppermute x3, starting transfers between devices, swapped(): lax.ppermute(first, 'tile', pairs(0))  7.55 us
    unnamed x12, local copies, waits for them, and re-layouts  2.58 us
    ppermute x3, starting transfers between devices, swapped(): lax.ppermute(second, 'tile', pairs(1))  1.96 us
  transfers between devices with their start and end apart: 18, of which 8 were waited for; matrix products, arithmetic and copies ran while one was open for 0% of the time, Pallas kernels for 11%

profile of v9, /device:TPU:0, one launch (start us, length us, event | category | flops | bytes accessed | tf_op | source)
XLA Modules:
  0.0 77.0 jit_solution(10239003109519867751)
XLA Ops:
  0.6 0.0 copy-start.4
  0.6 0.7 copy-done.4
  1.3 0.9 %rims.1 = (f32[136,128]{1,0:T(8,128)S(1)}, f32[136,128]{1,0:T(8,128)S(1)}, f32[16,128]{1,0:T(8,128)S(1)}) custom-call(f32[2048,128]{1,0:T(8,128)} %refs_0_.3, f32[16,128]{1,0:T(8,128)S(1)} %bitcast.9), custom_call_target="tpu_custom_call" | custom-call | flops 100000000 | bytes 3000000 | tf_op jit(solution)/shard_map/rims/pallas_call | solution.py:539
  2.2 3.0 %collective-permute-start = (f32[136,128]{1,0:T(8,128)S(1)}, f32[136,128]{1,0:T(8,128)S(1)}, u32[]{:S(2)}, u32[]{:S(2)}) collective-permute-start(f32[136,128]{1,0:T(8,128)S(1)} %get-tuple-element.49), channel_id=1, source_target_pairs={{0,1},{2,3},{4,5},{6,7},{1,0},{3,2},{5,4},{7,6},{8,9},{10,11},{12,... | collective-permute-start | bytes 208904 | tf_op jit(solution)/shard_map/ppermute | solution.py:563
  5.3 0.7 collective-permute-start.1
  5.9 0.0 copy-start.2
  5.9 1.2 %copy-done.2 = f32[2048,128]{1,0:T(8,128)S(1)} copy-done((f32[2048,128]{1,0:T(8,128)S(1)}, f32[2048,128]{1,0:T(8,128)}, u32[]{:S(2)}) %copy-start.2) | copy-done | bytes 1048600
  7.2 0.0 copy-start.5
  7.2 0.7 copy-done.5
  7.8 0.0 copy-start.1
  7.8 0.0 copy-start.3
  7.8 1.4 %prep_own.1 = (f32[16,128,128]{2,1,0:T(8,128)S(1)}, f32[16,128,128]{2,1,0:T(8,128)S(1)}, f32[16,128,128]{2,1,0:T(8,128)S(1)}, f32[16,128,128]{2,1,0:T(8,128)S(1)...) custom-call(f32[2048,128]{1,0:T(8,128)S(1)} %copy-done.2, ...), custom_call_target="tpu_custom_call" | custom-call | flops 160000000 | bytes 4800000 | tf_op jit(solution)/shard_map/prep_own/pallas_call | solution.py:539
  9.3 0.0 collective-permute-done.refs_0_
  9.3 0.0 collective-permute-done.1.refs_1_
  9.3 0.3 prep_rim.1
  9.6 0.7 collective-permute-start.4
  10.3 0.9 %collective-permute-start.3 = (f32[2,24,128]{2,1,0:T(8,128)S(1)}, f32[2,24,128]{2,1,0:T(8,128)S(1)}, u32[]{:S(2)}, u32[]{:S(2)}) collective-permute-start(f32[2,24,128]{2,1,0:T(8,128)S(1)} %get-tuple-element.62.refs_4__0_.refs_5__0_.refs_6__0_), channel_id=1, source_target_pairs={{0,16},{8,24},{16,0},{24,8},{1,17},{9,25},{17,1},{25,9},{2,18},{10... | collective-permute-start | bytes 73736 | tf_op jit(solution)/shard_map/ppermute | solution.py:569
  11.2 0.3 collective-permute-start.2
  11.5 1.6 %collective-permute-done.4.refs_4__3_.refs_5__3_.refs_6__3_ = f32[2,24,128]{2,1,0:T(8,128)S(1)} collective-permute-done((f32[2,24,128]{2,1,0:T(8,128)S(1)}, f32[2,24,128]{2,1,0:T(8,128)S(1)}, u32[]{:S(2)}, u32[]{:S(2)}) %collective-permute-start.4) | collective-permute-done | bytes 24608 | tf_op jit(solution)/shard_map/ppermute | solution.py:569
  13.1 1.3 %collective-permute-done.3.refs_4__2_.refs_5__2_.refs_6__2_ = f32[2,24,128]{2,1,0:T(8,128)S(1)} collective-permute-done((f32[2,24,128]{2,1,0:T(8,128)S(1)}, f32[2,24,128]{2,1,0:T(8,128)S(1)}, u32[]{:S(2)}, u32[]{:S(2)}) %collective-permute-start.3) | collective-permute-done | bytes 24608 | tf_op jit(solution)/shard_map/ppermute | solution.py:569
  14.4 0.0 collective-permute-done.2.refs_4__1_.refs_5__1_.refs_6__1_
  14.4 0.0 copy-done.1
  14.4 0.0 copy-done.3
  14.4 0.0 copy-start
  14.4 1.8 %edge.2 = (bf16[2304,128]{1,0:T(8,128)(2,1)S(1)}, f32[4,128,128]{2,1,0:T(8,128)S(1)}, f32[4,128,128]{2,1,0:T(8,128)S(1)}, bf16[3,128,128]{2,1,0:T(8,128)(2,1)S(1)}, bf16[3,128,128]{2,1,0:T(8,128)(2,1)S(1)}) custom-call(s32[4,32]{1,0:T(4,128)S(1)} %bitcast.3, f32[16,128,128]{2,1,0:T(8,128)S(1)} %get-tuple-element.60.refs_1__0_, ...), custom_call_target="tpu_custom_call" | custom-call | flops 250000000 | bytes 7500000 | tf_op jit(solution)/shard_map/edge/pallas_call | solution.py:539
  16.2 3.8 %collective-permute-start.5 = (bf16[3,128,128]{2,1,0:T(8,128)(2,1)S(1)}, bf16[3,128,128]{2,1,0:T(8,128)(2,1)S(1)}, u32[]{:S(2)}, u32[]{:S(2)}) collective-permute-start(bf16[3,128,128]{2,1,0:T(8,128)(2,1)S(1)} %get-tuple-element.68), channel_id=1, source_target_pairs={{0,1},{2,3},{4,5},{6,7},{1,0},{3,2},{5,4},{7,6},{8,9},{10,11},{12,... | collective-permute-start | bytes 294920 | tf_op jit(solution)/shard_map/ppermute | solution.py:563
  20.0 0.7 collective-permute-start.6
  20.7 0.0 copy-done
  20.7 3.3 %inner.2 = (f32[14,128,128]{2,1,0:T(8,128)S(1)}, f32[2,24,128]{2,1,0:T(8,128)S(1)}) custom-call(s32[4,32]{1,0:T(4,128)S(1)} %bitcast.4, f32[16,128,128]{2,1,0:T(8,128)S(1)} %get-tuple-element.55.refs_2__0_.refs_1__0_.refs_3__0_, f32[2,128,128]{2,1,0:T(8,128)S(1)} %get-tuple-element.56.refs_2__1_.refs_1__1_.refs_3__1_, ...), custom_call_target="tpu_custom_call" | custom-call | flops 400000000 | bytes 12000000 | tf_op jit(solution)/shard_map/inner/pallas_call | solution.py:539
  24.0 0.0 collective-permute-done.5.refs_1_
  24.0 0.0 collective-permute-done.6.refs_2_
  24.0 0.3 border.2
  24.3 0.1 collective-permute-start.9
  24.4 1.5 %collective-permute-start.8 = (f32[2,24,128]{2,1,0:T(8,128)S(1)}, f32[2,24,128]{2,1,0:T(8,128)S(1)}, u32[]{:S(2)}, u32[]{:S(2)}) collective-permute-start(f32[2,24,128]{2,1,0:T(8,128)S(1)} %get-tuple-element.72.refs_7__0_), channel_id=1, source_target_pairs={{0,16},{8,24},{16,0},{24,8},{1,17},{9,25},{17,1},{25,9},{2,18},{10... | collective-permute-start | bytes 73736 | tf_op jit(solution)/shard_map/ppermute | solution.py:569
  25.9 0.4 collective-permute-start.7
  26.3 1.6 %collective-permute-done.9.refs_7__3_ = f32[2,24,128]{2,1,0:T(8,128)S(1)} collective-permute-done((f32[2,24,128]{2,1,0:T(8,128)S(1)}, f32[2,24,128]{2,1,0:T(8,128)S(1)}, u32[]{:S(2)}, u32[]{:S(2)}) %collective-permute-start.9) | collective-permute-done | bytes 24608 | tf_op jit(solution)/shard_map/ppermute | solution.py:569
  27.9 0.4 collective-permute-done.8.refs_7__2_
  28.3 0.0 collective-permute-done.7.refs_7__1_
  28.3 2.1 %direction.2 = (f32[18,128,128]{2,1,0:T(8,128)S(1)}, f32[32,2,128]{2,1,0:T(2,128)S(1)}) custom-call(s32[4,32]{1,0:T(4,128)S(1)} %bitcast.5, f32[14,128,128]{2,1,0:T(8,128)S(1)} %get-tuple-element.66.refs_1_, f32[4,128,128]{2,1,0:T(8,128)S(1)} %get-tuple-element.71.refs_2_, f32[16,128,128]{2,1,0:T(8,128)S(1)} %get-tuple-element.55.refs_2__0_.refs_1__0_.refs_3__0_, ...), custom_call_target="tpu_custom_call" | custom-call | flops 400000000 | bytes 12000000 | tf_op jit(solution)/shard_map/direction/pallas_call | solution.py:539
  30.4 14.3 %all_to_all.10.refs_2_ = f32[32,2,128]{2,1,0:T(2,128)S(1)} all-to-all(f32[32,2,128]{2,1,0:T(2,128)S(1)} %get-tuple-element.74), channel_id=1, replica_groups=mesh['tm'=4,'tile'=8] {'tile','tm'}, dimensions={0} | all-to-all | bytes 65536 | tf_op jit(solution)/shard_map/all_to_all | solution.py:684
  44.8 0.7 update.1
  45.5 0.3 collective-permute-start.12
  45.8 1.5 %collective-permute-start.11 = (f32[1,24,128]{2,1,0:T(8,128)S(1)}, f32[1,24,128]{2,1,0:T(8,128)S(1)}, u32[]{:S(2)}, u32[]{:S(2)}) collective-permute-start(f32[1,24,128]{2,1,0:T(8,128)S(1)} %get-tuple-element.78.refs_5__0_), channel_id=1, source_target_pairs={{0,16},{8,24},{16,0},{24,8},{1,17},{9,25},{17,1},{25,9},{2,18},{10... | collective-permute-start | bytes 36872 | tf_op jit(solution)/shard_map/ppermute | solution.py:569
  47.3 0.1 collective-permute-start.10
  47.5 1.2 %collective-permute-done.12.refs_5__3_ = f32[1,24,128]{2,1,0:T(8,128)S(1)} collective-permute-done((f32[1,24,128]{2,1,0:T(8,128)S(1)}, f32[1,24,128]{2,1,0:T(8,128)S(1)}, u32[]{:S(2)}, u32[]{:S(2)}) %collective-permute-start.12) | collective-permute-done | bytes 12320 | tf_op jit(solution)/shard_map/ppermute | solution.py:569
  48.7 0.8 %collective-permute-done.11.refs_5__2_ = f32[1,24,128]{2,1,0:T(8,128)S(1)} collective-permute-done((f32[1,24,128]{2,1,0:T(8,128)S(1)}, f32[1,24,128]{2,1,0:T(8,128)S(1)}, u32[]{:S(2)}, u32[]{:S(2)}) %collective-permute-start.11) | collective-permute-done | bytes 12320 | tf_op jit(solution)/shard_map/ppermute | solution.py:569
  49.5 0.0 collective-permute-done.10.refs_5__1_
  49.5 1.8 %edge.3 = (bf16[2304,128]{1,0:T(8,128)(2,1)S(1)}, f32[4,128,128]{2,1,0:T(8,128)S(1)}, f32[4,128,128]{2,1,0:T(8,128)S(1)}, bf16[3,128,128]{2,1,0:T(8,128)(2,1)S(1...) custom-call(s32[4,32]{1,0:T(4,128)S(1)} %bitcast.6, f32[16,128,128]{2,1,0:T(8,128)S(1)} %get-tuple-element.76.refs_1__0_, ...), custom_call_target="tpu_custom_call" | custom-call | flops 250000000 | bytes 7500000 | tf_op jit(solution)/shard_map/edge/pallas_call | solution.py:539
  51.3 0.7 collective-permute-start.13
  52.0 0.7 collective-permute-start.14
  52.7 3.5 %inner.3 = (f32[14,128,128]{2,1,0:T(8,128)S(1)}, f32[2,24,128]{2,1,0:T(8,128)S(1)}, f32[2048,128]{1,0:T(8,128)}) custom-call(s32[4,32]{1,0:T(4,128)S(1)} %bitcast.7, f32[16,128,128]{2,1,0:T(8,128)S(1)} %get-tuple-element.55.refs_2__0_.refs_1__0_.refs_3__0_, f32[2,128,128]{2,1,0:T(8,128)S(1)} %get-tuple-element.56.refs_2__1_.refs_1__1_.refs_3__1_, ...), custom_call_target="tpu_custom_call" | custom-call | flops 400000000 | bytes 12000000 | tf_op jit(solution)/shard_map/inner/pallas_call | solution.py:539
  56.2 0.0 collective-permute-done.13.refs_1_
  56.2 0.0 collective-permute-done.14.refs_2_
  56.2 0.3 border.3
  56.5 0.1 collective-permute-start.17
  56.6 1.5 %collective-permute-start.16 = (f32[2,24,128]{2,1,0:T(8,128)S(1)}, f32[2,24,128]{2,1,0:T(8,128)S(1)}, u32[]{:S(2)}, u32[]{:S(2)}) collective-permute-start(f32[2,24,128]{2,1,0:T(8,128)S(1)} %get-tuple-element.88.refs_7__0_), channel_id=1, source_target_pairs={{0,16},{8,24},{16,0},{24,8},{1,17},{9,25},{17,1},{25,9},{2,18},{10... | collective-permute-start | bytes 73736 | tf_op jit(solution)/shard_map/ppermute | solution.py:569
  58.1 0.4 collective-permute-start.15
  58.4 1.6 %collective-permute-done.17.refs_7__3_ = f32[2,24,128]{2,1,0:T(8,128)S(1)} collective-permute-done((f32[2,24,128]{2,1,0:T(8,128)S(1)}, f32[2,24,128]{2,1,0:T(8,128)S(1)}, u32[]{:S(2)}, u32[]{:S(2)}) %collective-permute-start.17) | collective-permute-done | bytes 24608 | tf_op jit(solution)/shard_map/ppermute | solution.py:569
  60.1 0.4 collective-permute-done.16.refs_7__2_
  60.5 0.0 collective-permute-done.15.refs_7__1_
  60.5 2.1 %direction.3 = (f32[18,128,128]{2,1,0:T(8,128)S(1)}, f32[32,2,128]{2,1,0:T(2,128)S(1)}) custom-call(s32[4,32]{1,0:T(4,128)S(1)} %bitcast.8, f32[14,128,128]{2,1,0:T(8,128)S(1)} %get-tuple-element.82.refs_1_, f32[4,128,128]{2,1,0:T(8,128)S(1)} %get-tuple-element.87.refs_2_, f32[16,128,128]{2,1,0:T(8,128)S(1)} %get-tuple-element.55.refs_2__0_.refs_1__0_.refs_3__0_, ...), custom_call_target="tpu_custom_call" | custom-call | flops 400000000 | bytes 12000000 | tf_op jit(solution)/shard_map/direction/pallas_call | solution.py:539
  62.6 12.9 %all_to_all.11.refs_2_ = f32[32,2,128]{2,1,0:T(2,128)S(1)} all-to-all(f32[32,2,128]{2,1,0:T(2,128)S(1)} %get-tuple-element.90), channel_id=1, replica_groups=mesh['tm'=4,'tile'=8] {'tile','tm'}, dimensions={0} | all-to-all | bytes 65536 | tf_op jit(solution)/shard_map/all_to_all | solution.py:684
  75.6 1.3 %final.1 = f32[2048,128]{1,0:T(8,128)} custom-call(f32[16,128,128]{2,1,0:T(8,128)S(1)} %get-tuple-element.75.refs_8__0_.refs_9__0_.refs_7__0_.refs_0_, f32[18,128,128]{2,1,0:T(8,128)S(1)} %get-tuple-element.89.refs_1_, f32[32,2,128]{2,1,0:T(2,128)S(1)} %all_to_all.11.refs_2_), custom_call_target="tpu_custom_call" | custom-call | flops 140000000 | bytes 4200000 | tf_op jit(solution)/shard_map/final/pallas_call | solution.py:539
Async XLA Ops:
  0.6 0.7 copy-start.4
  2.2 7.0 %collective-permute-start = (f32[136,128]{1,0:T(8,128)S(1)}, f32[136,128]{1,0:T(8,128)S(1)}, u32[]{:S(2)}, u32[]{:S(2)}) collective-permute-start(f32[136,128]{1,0:T(8,128)S(1)} %get-tuple-element.49), channel_id=1, source_target_pairs={{0,1},{2,3},{4,5},{6,7},{1,0},{3,2},{5,4},{7,6},{8,9},{10,11},{12,... | collective-permute-start | bytes 208904 | tf_op jit(solution)/shard_map/ppermute | solution.py:563
  5.3 4.0 %collective-permute-start.1 = (f32[136,128]{1,0:T(8,128)S(1)}, f32[136,128]{1,0:T(8,128)S(1)}, u32[]{:S(2)}, u32[]{:S(2)}) collective-permute-start(f32[136,128]{1,0:T(8,128)S(1)} %get-tuple-element.50), channel_id=1, source_target_pairs={{1,2},{3,4},{5,6},{2,1},{4,3},{6,5},{9,10},{11,12},{13,14},{10,9},... | collective-permute-start | bytes 208904 | tf_op jit(solution)/shard_map/ppermute | solution.py:563
  5.9 1.2 %copy-start.2 = (f32[2048,128]{1,0:T(8,128)S(1)}, f32[2048,128]{1,0:T(8,128)}, u32[]{:S(2)}) copy-start(f32[2048,128]{1,0:T(8,128)} %refs_0_.3) | copy-start | bytes 3145732
  7.2 0.7 copy-start.5
  7.8 6.6 %copy-start.1 = (bf16[8192,128]{1,0:T(8,128)(2,1)S(1)}, bf16[8192,128]{1,0:T(8,128)(2,1)}, u32[]{:S(2)}) copy-start(bf16[8192,128]{1,0:T(8,128)(2,1)} %refs_7_.7) | copy-start | bytes 6291460
  7.8 6.6 %copy-start.3 = (s32[32,4]{0,1:T(4,128)S(1)}, s32[32,4]{0,1:T(4,128)}, u32[]{:S(2)}) copy-start(s32[32,4]{0,1:T(4,128)} %param.8) | copy-start | bytes 1540
  9.6 3.5 %collective-permute-start.4 = (f32[2,24,128]{2,1,0:T(8,128)S(1)}, f32[2,24,128]{2,1,0:T(8,128)S(1)}, u32[]{:S(2)}, u32[]{:S(2)}) collective-permute-start(f32[2,24,128]{2,1,0:T(8,128)S(1)} %get-tuple-element.62.refs_4__0_.refs_5__0_.refs_6__0_), channel_id=1, source_target_pairs={{0,24},{8,16},{16,8},{24,0},{1,25},{9,17},{17,9},{25,1},{2,26},{10... | collective-permute-start | bytes 73736 | tf_op jit(solution)/shard_map/ppermute | solution.py:569
  10.3 4.1 %collective-permute-start.3 = (f32[2,24,128]{2,1,0:T(8,128)S(1)}, f32[2,24,128]{2,1,0:T(8,128)S(1)}, u32[]{:S(2)}, u32[]{:S(2)}) collective-permute-start(f32[2,24,128]{2,1,0:T(8,128)S(1)} %get-tuple-element.62.refs_4__0_.refs_5__0_.refs_6__0_), channel_id=1, source_target_pairs={{0,16},{8,24},{16,0},{24,8},{1,17},{9,25},{17,1},{25,9},{2,18},{10... | collective-permute-start | bytes 73736 | tf_op jit(solution)/shard_map/ppermute | solution.py:569
  11.2 3.2 %collective-permute-start.2 = (f32[2,24,128]{2,1,0:T(8,128)S(1)}, f32[2,24,128]{2,1,0:T(8,128)S(1)}, u32[]{:S(2)}, u32[]{:S(2)}) collective-permute-start(f32[2,24,128]{2,1,0:T(8,128)S(1)} %get-tuple-element.62.refs_4__0_.refs_5__0_.refs_6__0_), channel_id=1, source_target_pairs={{0,8},{8,0},{16,24},{24,16},{1,9},{9,1},{17,25},{25,17},{2,10},{10... | collective-permute-start | bytes 73736 | tf_op jit(solution)/shard_map/ppermute | solution.py:569
  14.4 6.3 %copy-start = (bf16[8192,256]{1,0:T(8,128)(2,1)S(1)}, bf16[8192,256]{1,0:T(8,128)(2,1)}, u32[]{:S(2)}) copy-start(bf16[8192,256]{1,0:T(8,128)(2,1)} %refs_8_.3) | copy-start | bytes 12582916
  16.2 7.8 %collective-permute-start.5 = (bf16[3,128,128]{2,1,0:T(8,128)(2,1)S(1)}, bf16[3,128,128]{2,1,0:T(8,128)(2,1)S(1)}, u32[]{:S(2)}, u32[]{:S(2)}) collective-permute-start(bf16[3,128,128]{2,1,0:T(8,128)(2,1)S(1)} %get-tuple-element.68), channel_id=1, source_target_pairs={{0,1},{2,3},{4,5},{6,7},{1,0},{3,2},{5,4},{7,6},{8,9},{10,11},{12,... | collective-permute-start | bytes 294920 | tf_op jit(solution)/shard_map/ppermute | solution.py:563
  20.0 4.0 %collective-permute-start.6 = (bf16[3,128,128]{2,1,0:T(8,128)(2,1)S(1)}, bf16[3,128,128]{2,1,0:T(8,128)(2,1)S(1)}, u32[]{:S(2)}, u32[]{:S(2)}) collective-permute-start(bf16[3,128,128]{2,1,0:T(8,128)(2,1)S(1)} %get-tuple-element.69), channel_id=1, source_target_pairs={{1,2},{3,4},{5,6},{2,1},{4,3},{6,5},{9,10},{11,12},{13,14},{10,9},... | collective-permute-start | bytes 294920 | tf_op jit(solution)/shard_map/ppermute | solution.py:563
  24.3 3.6 %collective-permute-start.9 = (f32[2,24,128]{2,1,0:T(8,128)S(1)}, f32[2,24,128]{2,1,0:T(8,128)S(1)}, u32[]{:S(2)}, u32[]{:S(2)}) collective-permute-start(f32[2,24,128]{2,1,0:T(8,128)S(1)} %get-tuple-element.72.refs_7__0_), channel_id=1, source_target_pairs={{0,24},{8,16},{16,8},{24,0},{1,25},{9,17},{17,9},{25,1},{2,26},{10... | collective-permute-start | bytes 73736 | tf_op jit(solution)/shard_map/ppermute | solution.py:569
  24.4 3.9 %collective-permute-start.8 = (f32[2,24,128]{2,1,0:T(8,128)S(1)}, f32[2,24,128]{2,1,0:T(8,128)S(1)}, u32[]{:S(2)}, u32[]{:S(2)}) collective-permute-start(f32[2,24,128]{2,1,0:T(8,128)S(1)} %get-tuple-element.72.refs_7__0_), channel_id=1, source_target_pairs={{0,16},{8,24},{16,0},{24,8},{1,17},{9,25},{17,1},{25,9},{2,18},{10... | collective-permute-start | bytes 73736 | tf_op jit(solution)/shard_map/ppermute | solution.py:569
  25.9 2.4 %collective-permute-start.7 = (f32[2,24,128]{2,1,0:T(8,128)S(1)}, f32[2,24,128]{2,1,0:T(8,128)S(1)}, u32[]{:S(2)}, u32[]{:S(2)}) collective-permute-start(f32[2,24,128]{2,1,0:T(8,128)S(1)} %get-tuple-element.72.refs_7__0_), channel_id=1, source_target_pairs={{0,8},{8,0},{16,24},{24,16},{1,9},{9,1},{17,25},{25,17},{2,10},{10... | collective-permute-start | bytes 73736 | tf_op jit(solution)/shard_map/ppermute | solution.py:569
  45.5 3.2 %collective-permute-start.12 = (f32[1,24,128]{2,1,0:T(8,128)S(1)}, f32[1,24,128]{2,1,0:T(8,128)S(1)}, u32[]{:S(2)}, u32[]{:S(2)}) collective-permute-start(f32[1,24,128]{2,1,0:T(8,128)S(1)} %get-tuple-element.78.refs_5__0_), channel_id=1, source_target_pairs={{0,24},{8,16},{16,8},{24,0},{1,25},{9,17},{17,9},{25,1},{2,26},{10... | collective-permute-start | bytes 36872 | tf_op jit(solution)/shard_map/ppermute | solution.py:569
  45.8 3.7 %collective-permute-start.11 = (f32[1,24,128]{2,1,0:T(8,128)S(1)}, f32[1,24,128]{2,1,0:T(8,128)S(1)}, u32[]{:S(2)}, u32[]{:S(2)}) collective-permute-start(f32[1,24,128]{2,1,0:T(8,128)S(1)} %get-tuple-element.78.refs_5__0_), channel_id=1, source_target_pairs={{0,16},{8,24},{16,0},{24,8},{1,17},{9,25},{17,1},{25,9},{2,18},{10... | collective-permute-start | bytes 36872 | tf_op jit(solution)/shard_map/ppermute | solution.py:569
  47.3 2.2 %collective-permute-start.10 = (f32[1,24,128]{2,1,0:T(8,128)S(1)}, f32[1,24,128]{2,1,0:T(8,128)S(1)}, u32[]{:S(2)}, u32[]{:S(2)}) collective-permute-start(f32[1,24,128]{2,1,0:T(8,128)S(1)} %get-tuple-element.78.refs_5__0_), channel_id=1, source_target_pairs={{0,8},{8,0},{16,24},{24,16},{1,9},{9,1},{17,25},{25,17},{2,10},{10... | collective-permute-start | bytes 36872 | tf_op jit(solution)/shard_map/ppermute | solution.py:569
  51.3 4.9 %collective-permute-start.13 = (bf16[3,128,128]{2,1,0:T(8,128)(2,1)S(1)}, bf16[3,128,128]{2,1,0:T(8,128)(2,1)S(1)}, u32[]{:S(2)}, u32[]{:S(2)}) collective-permute-start(bf16[3,128,128]{2,1,0:T(8,128)(2,1)S(1)} %get-tuple-element.84), channel_id=1, source_target_pairs={{0,1},{2,3},{4,5},{6,7},{1,0},{3,2},{5,4},{7,6},{8,9},{10,11},{12,... | collective-permute-start | bytes 294920 | tf_op jit(solution)/shard_map/ppermute | solution.py:563
  52.0 4.2 %collective-permute-start.14 = (bf16[3,128,128]{2,1,0:T(8,128)(2,1)S(1)}, bf16[3,128,128]{2,1,0:T(8,128)(2,1)S(1)}, u32[]{:S(2)}, u32[]{:S(2)}) collective-permute-start(bf16[3,128,128]{2,1,0:T(8,128)(2,1)S(1)} %get-tuple-element.85), channel_id=1, source_target_pairs={{1,2},{3,4},{5,6},{2,1},{4,3},{6,5},{9,10},{11,12},{13,14},{10,9},... | collective-permute-start | bytes 294920 | tf_op jit(solution)/shard_map/ppermute | solution.py:563
  56.5 3.6 %collective-permute-start.17 = (f32[2,24,128]{2,1,0:T(8,128)S(1)}, f32[2,24,128]{2,1,0:T(8,128)S(1)}, u32[]{:S(2)}, u32[]{:S(2)}) collective-permute-start(f32[2,24,128]{2,1,0:T(8,128)S(1)} %get-tuple-element.88.refs_7__0_), channel_id=1, source_target_pairs={{0,24},{8,16},{16,8},{24,0},{1,25},{9,17},{17,9},{25,1},{2,26},{10... | collective-permute-start | bytes 73736 | tf_op jit(solution)/shard_map/ppermute | solution.py:569
  56.6 3.9 %collective-permute-start.16 = (f32[2,24,128]{2,1,0:T(8,128)S(1)}, f32[2,24,128]{2,1,0:T(8,128)S(1)}, u32[]{:S(2)}, u32[]{:S(2)}) collective-permute-start(f32[2,24,128]{2,1,0:T(8,128)S(1)} %get-tuple-element.88.refs_7__0_), channel_id=1, source_target_pairs={{0,16},{8,24},{16,0},{24,8},{1,17},{9,25},{17,1},{25,9},{2,18},{10... | collective-permute-start | bytes 73736 | tf_op jit(solution)/shard_map/ppermute | solution.py:569
  58.1 2.4 %collective-permute-start.15 = (f32[2,24,128]{2,1,0:T(8,128)S(1)}, f32[2,24,128]{2,1,0:T(8,128)S(1)}, u32[]{:S(2)}, u32[]{:S(2)}) collective-permute-start(f32[2,24,128]{2,1,0:T(8,128)S(1)} %get-tuple-element.88.refs_7__0_), channel_id=1, source_target_pairs={{0,8},{8,0},{16,24},{24,16},{1,9},{9,1},{17,25},{25,17},{2,10},{10... | collective-permute-start | bytes 73736 | tf_op jit(solution)/shard_map/ppermute | solution.py:569

commit v10 on v9

--- a/solution.py
+++ b/solution.py
@@ -355,23 +355,15 @@
         zones[2 * RIM + i] = above
         for to, other, held in ((send_a, above, below), (send_b, below, above)):
             to[i] = jnp.where(even, other, held).astype(BF16)
-        lows = [value - value.astype(BF16).astype(F32) for value in (below, above)]
-        at = 2 * RIM + i % RIM
-        for to, takes in ((send_a, jnp.logical_not(even)), (send_b, even)):
-            if i < RIM:
-
-                @pl.when(takes)
-                def _():
-                    to[at] = lows[0].astype(BF16)
-
-            else:
-
-                @pl.when(jnp.logical_not(takes))
-                def _():
-                    to[at] = lows[1].astype(BF16)
-
         spill[i] = gathered(contrib, place, 2 * RIM + i, ranges)
         spill[2 * RIM + i] = gathered(contrib, place, chunks - 4 * RIM + i, ranges)
+    for i in range(RIM):
+        lows = [
+            zones[at] - zones[at].astype(BF16).astype(F32)
+            for at in (i, 3 * RIM + i)
+        ]
+        send_a[2 * RIM + i] = jnp.where(even, lows[1], lows[0]).astype(BF16)
+        send_b[2 * RIM + i] = jnp.where(even, lows[0], lows[1]).astype(BF16)
 
 def adjoint_chunk(sums_table, field, p, pinv, rows, c, r3, pay):
     frames = field.shape[0]

time: 77.3 us -> 77.1 us (level)
  no operation moved by 1% of the time
where the time goes in v10:
time: 77.1 us; the launch traced here: 76.8 us
  blocking collectives  27.3 us (35%)
  Pallas kernels  19.7 us (26%)
  starting transfers between devices  17.2 us (22%)
  waiting for transfers between devices  8.99 us (12%)
  local copies, waits for them, and re-layouts  2.58 us (3%)
  between operations  1.02 us (1%)
    all_to_all x2, blocking collectives, per_device(): stats = lax.all_to_all(stats, ('tile', 'tm'), 0, 0)  27.3 us
    pallas_call x13, Pallas kernels, call(): pl.pallas_call(body, name=name, out_shape=outs, in_specs=in_specs, out_sp...  19.7 us
    ppermute x12, waiting for transfers between devices, shared_blocks(): lax.ppermute(value, 'tm', [(i, i ^ j) for i in range(size)])  8.98 us
    ppermute x12, starting transfers between devices, shared_blocks(): lax.ppermute(value, 'tm', [(i, i ^ j) for i in range(size)])  7.73 us
    ppermute x3, starting transfers between devices, swapped(): lax.ppermute(first, 'tile', pairs(0))  7.55 us
    unnamed x12, local copies, waits for them, and re-layouts  2.58 us
    ppermute x3, starting transfers between devices, swapped(): lax.ppermute(second, 'tile', pairs(1))  1.96 us
  transfers between devices with their start and end apart: 18, of which 8 were waited for; matrix products, arithmetic and copies ran while one was open for 0% of the time, Pallas kernels for 11%

profile of v10, /device:TPU:0, one launch (start us, length us, event | category | flops | bytes accessed | tf_op | source)
XLA Modules:
  0.0 76.8 jit_solution(16906119346805578495)
XLA Ops:
  0.6 0.0 copy-start.4
  0.6 0.7 copy-done.4
  1.3 0.9 %rims.1 = (f32[136,128]{1,0:T(8,128)S(1)}, f32[136,128]{1,0:T(8,128)S(1)}, f32[16,128]{1,0:T(8,128)S(1)}) custom-call(f32[2048,128]{1,0:T(8,128)} %refs_0_.3, f32[16,128]{1,0:T(8,128)S(1)} %bitcast.9), custom_call_target="tpu_custom_call" | custom-call | flops 100000000 | bytes 3000000 | tf_op jit(solution)/shard_map/rims/pallas_call | solution.py:531
  2.2 3.0 %collective-permute-start = (f32[136,128]{1,0:T(8,128)S(1)}, f32[136,128]{1,0:T(8,128)S(1)}, u32[]{:S(2)}, u32[]{:S(2)}) collective-permute-start(f32[136,128]{1,0:T(8,128)S(1)} %get-tuple-element.49), channel_id=1, source_target_pairs={{0,1},{2,3},{4,5},{6,7},{1,0},{3,2},{5,4},{7,6},{8,9},{10,11},{12,... | collective-permute-start | bytes 208904 | tf_op jit(solution)/shard_map/ppermute | solution.py:555
  5.3 0.7 collective-permute-start.1
  5.9 0.0 copy-start.2
  5.9 1.2 %copy-done.2 = f32[2048,128]{1,0:T(8,128)S(1)} copy-done((f32[2048,128]{1,0:T(8,128)S(1)}, f32[2048,128]{1,0:T(8,128)}, u32[]{:S(2)}) %copy-start.2) | copy-done | bytes 1048600
  7.2 0.0 copy-start.5
  7.2 0.7 copy-done.5
  7.8 0.0 copy-start.1
  7.8 0.0 copy-start.3
  7.8 1.4 %prep_own.1 = (f32[16,128,128]{2,1,0:T(8,128)S(1)}, f32[16,128,128]{2,1,0:T(8,128)S(1)}, f32[16,128,128]{2,1,0:T(8,128)S(1)}, f32[16,128,128]{2,1,0:T(8,128)S(1)...) custom-call(f32[2048,128]{1,0:T(8,128)S(1)} %copy-done.2, ...), custom_call_target="tpu_custom_call" | custom-call | flops 160000000 | bytes 4800000 | tf_op jit(solution)/shard_map/prep_own/pallas_call | solution.py:531
  9.3 0.0 collective-permute-done.refs_0_
  9.3 0.0 collective-permute-done.1.refs_1_
  9.3 0.3 prep_rim.1
  9.6 0.7 collective-permute-start.4
  10.3 0.9 %collective-permute-start.3 = (f32[2,24,128]{2,1,0:T(8,128)S(1)}, f32[2,24,128]{2,1,0:T(8,128)S(1)}, u32[]{:S(2)}, u32[]{:S(2)}) collective-permute-start(f32[2,24,128]{2,1,0:T(8,128)S(1)} %get-tuple-element.62.refs_4__0_.refs_5__0_.refs_6__0_), channel_id=1, source_target_pairs={{0,16},{8,24},{16,0},{24,8},{1,17},{9,25},{17,1},{25,9},{2,18},{10... | collective-permute-start | bytes 73736 | tf_op jit(solution)/shard_map/ppermute | solution.py:561
  11.2 0.3 collective-permute-start.2
  11.5 1.6 %collective-permute-done.4.refs_4__3_.refs_5__3_.refs_6__3_ = f32[2,24,128]{2,1,0:T(8,128)S(1)} collective-permute-done((f32[2,24,128]{2,1,0:T(8,128)S(1)}, f32[2,24,128]{2,1,0:T(8,128)S(1)}, u32[]{:S(2)}, u32[]{:S(2)}) %collective-permute-start.4) | collective-permute-done | bytes 24608 | tf_op jit(solution)/shard_map/ppermute | solution.py:561
  13.1 1.3 %collective-permute-done.3.refs_4__2_.refs_5__2_.refs_6__2_ = f32[2,24,128]{2,1,0:T(8,128)S(1)} collective-permute-done((f32[2,24,128]{2,1,0:T(8,128)S(1)}, f32[2,24,128]{2,1,0:T(8,128)S(1)}, u32[]{:S(2)}, u32[]{:S(2)}) %collective-permute-start.3) | collective-permute-done | bytes 24608 | tf_op jit(solution)/shard_map/ppermute | solution.py:561
  14.4 0.0 collective-permute-done.2.refs_4__1_.refs_5__1_.refs_6__1_
  14.4 0.0 copy-done.1
  14.4 0.0 copy-done.3
  14.4 0.0 copy-start
  14.4 1.7 %edge.2 = (bf16[2304,128]{1,0:T(8,128)(2,1)S(1)}, f32[4,128,128]{2,1,0:T(8,128)S(1)}, f32[4,128,128]{2,1,0:T(8,128)S(1)}, bf16[3,128,128]{2,1,0:T(8,128)(2,1)S(1)}, bf16[3,128,128]{2,1,0:T(8,128)(2,1)S(1)}) custom-call(s32[4,32]{1,0:T(4,128)S(1)} %bitcast.3, f32[16,128,128]{2,1,0:T(8,128)S(1)} %get-tuple-element.60.refs_1__0_, ...), custom_call_target="tpu_custom_call" | custom-call | flops 250000000 | bytes 7500000 | tf_op jit(solution)/shard_map/edge/pallas_call | solution.py:531
  16.1 3.8 %collective-permute-start.5 = (bf16[3,128,128]{2,1,0:T(8,128)(2,1)S(1)}, bf16[3,128,128]{2,1,0:T(8,128)(2,1)S(1)}, u32[]{:S(2)}, u32[]{:S(2)}) collective-permute-start(bf16[3,128,128]{2,1,0:T(8,128)(2,1)S(1)} %get-tuple-element.68), channel_id=1, source_target_pairs={{0,1},{2,3},{4,5},{6,7},{1,0},{3,2},{5,4},{7,6},{8,9},{10,11},{12,... | collective-permute-start | bytes 294920 | tf_op jit(solution)/shard_map/ppermute | solution.py:555
  19.9 0.7 collective-permute-start.6
  20.6 0.0 copy-done
  20.6 3.3 %inner.2 = (f32[14,128,128]{2,1,0:T(8,128)S(1)}, f32[2,24,128]{2,1,0:T(8,128)S(1)}) custom-call(s32[4,32]{1,0:T(4,128)S(1)} %bitcast.4, f32[16,128,128]{2,1,0:T(8,128)S(1)} %get-tuple-element.55.refs_2__0_.refs_1__0_.refs_3__0_, f32[2,128,128]{2,1,0:T(8,128)S(1)} %get-tuple-element.56.refs_2__1_.refs_1__1_.refs_3__1_, ...), custom_call_target="tpu_custom_call" | custom-call | flops 400000000 | bytes 12000000 | tf_op jit(solution)/shard_map/inner/pallas_call | solution.py:531
  23.9 0.0 collective-permute-done.5.refs_1_
  23.9 0.0 collective-permute-done.6.refs_2_
  23.9 0.3 border.2
  24.2 0.1 collective-permute-start.9
  24.3 1.5 %collective-permute-start.8 = (f32[2,24,128]{2,1,0:T(8,128)S(1)}, f32[2,24,128]{2,1,0:T(8,128)S(1)}, u32[]{:S(2)}, u32[]{:S(2)}) collective-permute-start(f32[2,24,128]{2,1,0:T(8,128)S(1)} %get-tuple-element.72.refs_7__0_), channel_id=1, source_target_pairs={{0,16},{8,24},{16,0},{24,8},{1,17},{9,25},{17,1},{25,9},{2,18},{10... | collective-permute-start | bytes 73736 | tf_op jit(solution)/shard_map/ppermute | solution.py:561
  25.7 0.4 collective-permute-start.7
  26.1 1.6 %collective-permute-done.9.refs_7__3_ = f32[2,24,128]{2,1,0:T(8,128)S(1)} collective-permute-done((f32[2,24,128]{2,1,0:T(8,128)S(1)}, f32[2,24,128]{2,1,0:T(8,128)S(1)}, u32[]{:S(2)}, u32[]{:S(2)}) %collective-permute-start.9) | collective-permute-done | bytes 24608 | tf_op jit(solution)/shard_map/ppermute | solution.py:561
  27.8 0.4 collective-permute-done.8.refs_7__2_
  28.2 0.0 collective-permute-done.7.refs_7__1_
  28.2 2.1 %direction.2 = (f32[18,128,128]{2,1,0:T(8,128)S(1)}, f32[32,2,128]{2,1,0:T(2,128)S(1)}) custom-call(s32[4,32]{1,0:T(4,128)S(1)} %bitcast.5, f32[14,128,128]{2,1,0:T(8,128)S(1)} %get-tuple-element.66.refs_1_, f32[4,128,128]{2,1,0:T(8,128)S(1)} %get-tuple-element.71.refs_2_, f32[16,128,128]{2,1,0:T(8,128)S(1)} %get-tuple-element.55.refs_2__0_.refs_1__0_.refs_3__0_, ...), custom_call_target="tpu_custom_call" | custom-call | flops 400000000 | bytes 12000000 | tf_op jit(solution)/shard_map/direction/pallas_call | solution.py:531
  30.3 14.3 %all_to_all.10.refs_2_ = f32[32,2,128]{2,1,0:T(2,128)S(1)} all-to-all(f32[32,2,128]{2,1,0:T(2,128)S(1)} %get-tuple-element.74), channel_id=1, replica_groups=mesh['tm'=4,'tile'=8] {'tile','tm'}, dimensions={0} | all-to-all | bytes 65536 | tf_op jit(solution)/shard_map/all_to_all | solution.py:676
  44.6 0.7 update.1
  45.4 0.3 collective-permute-start.12
  45.6 1.5 %collective-permute-start.11 = (f32[1,24,128]{2,1,0:T(8,128)S(1)}, f32[1,24,128]{2,1,0:T(8,128)S(1)}, u32[]{:S(2)}, u32[]{:S(2)}) collective-permute-start(f32[1,24,128]{2,1,0:T(8,128)S(1)} %get-tuple-element.78.refs_5__0_), channel_id=1, source_target_pairs={{0,16},{8,24},{16,0},{24,8},{1,17},{9,25},{17,1},{25,9},{2,18},{10... | collective-permute-start | bytes 36872 | tf_op jit(solution)/shard_map/ppermute | solution.py:561
  47.2 0.1 collective-permute-start.10
  47.3 1.2 %collective-permute-done.12.refs_5__3_ = f32[1,24,128]{2,1,0:T(8,128)S(1)} collective-permute-done((f32[1,24,128]{2,1,0:T(8,128)S(1)}, f32[1,24,128]{2,1,0:T(8,128)S(1)}, u32[]{:S(2)}, u32[]{:S(2)}) %collective-permute-start.12) | collective-permute-done | bytes 12320 | tf_op jit(solution)/shard_map/ppermute | solution.py:561
  48.5 0.8 %collective-permute-done.11.refs_5__2_ = f32[1,24,128]{2,1,0:T(8,128)S(1)} collective-permute-done((f32[1,24,128]{2,1,0:T(8,128)S(1)}, f32[1,24,128]{2,1,0:T(8,128)S(1)}, u32[]{:S(2)}, u32[]{:S(2)}) %collective-permute-start.11) | collective-permute-done | bytes 12320 | tf_op jit(solution)/shard_map/ppermute | solution.py:561
  49.3 0.0 collective-permute-done.10.refs_5__1_
  49.3 1.7 %edge.3 = (bf16[2304,128]{1,0:T(8,128)(2,1)S(1)}, f32[4,128,128]{2,1,0:T(8,128)S(1)}, f32[4,128,128]{2,1,0:T(8,128)S(1)}, bf16[3,128,128]{2,1,0:T(8,128)(2,1)S(1...) custom-call(s32[4,32]{1,0:T(4,128)S(1)} %bitcast.6, f32[16,128,128]{2,1,0:T(8,128)S(1)} %get-tuple-element.76.refs_1__0_, ...), custom_call_target="tpu_custom_call" | custom-call | flops 250000000 | bytes 7500000 | tf_op jit(solution)/shard_map/edge/pallas_call | solution.py:531
  51.0 0.7 collective-permute-start.13
  51.7 0.7 collective-permute-start.14
  52.4 3.5 %inner.3 = (f32[14,128,128]{2,1,0:T(8,128)S(1)}, f32[2,24,128]{2,1,0:T(8,128)S(1)}, f32[2048,128]{1,0:T(8,128)}) custom-call(s32[4,32]{1,0:T(4,128)S(1)} %bitcast.7, f32[16,128,128]{2,1,0:T(8,128)S(1)} %get-tuple-element.55.refs_2__0_.refs_1__0_.refs_3__0_, f32[2,128,128]{2,1,0:T(8,128)S(1)} %get-tuple-element.56.refs_2__1_.refs_1__1_.refs_3__1_, ...), custom_call_target="tpu_custom_call" | custom-call | flops 400000000 | bytes 12000000 | tf_op jit(solution)/shard_map/inner/pallas_call | solution.py:531
  56.0 0.0 collective-permute-done.13.refs_1_
  56.0 0.0 collective-permute-done.14.refs_2_
  56.0 0.3 border.3
  56.3 0.1 collective-permute-start.17
  56.4 1.5 %collective-permute-start.16 = (f32[2,24,128]{2,1,0:T(8,128)S(1)}, f32[2,24,128]{2,1,0:T(8,128)S(1)}, u32[]{:S(2)}, u32[]{:S(2)}) collective-permute-start(f32[2,24,128]{2,1,0:T(8,128)S(1)} %get-tuple-element.88.refs_7__0_), channel_id=1, source_target_pairs={{0,16},{8,24},{16,0},{24,8},{1,17},{9,25},{17,1},{25,9},{2,18},{10... | collective-permute-start | bytes 73736 | tf_op jit(solution)/shard_map/ppermute | solution.py:561
  57.9 0.3 collective-permute-start.15
  58.2 1.6 %collective-permute-done.17.refs_7__3_ = f32[2,24,128]{2,1,0:T(8,128)S(1)} collective-permute-done((f32[2,24,128]{2,1,0:T(8,128)S(1)}, f32[2,24,128]{2,1,0:T(8,128)S(1)}, u32[]{:S(2)}, u32[]{:S(2)}) %collective-permute-start.17) | collective-permute-done | bytes 24608 | tf_op jit(solution)/shard_map/ppermute | solution.py:561
  59.8 0.4 collective-permute-done.16.refs_7__2_
  60.2 0.0 collective-permute-done.15.refs_7__1_
  60.2 2.1 %direction.3 = (f32[18,128,128]{2,1,0:T(8,128)S(1)}, f32[32,2,128]{2,1,0:T(2,128)S(1)}) custom-call(s32[4,32]{1,0:T(4,128)S(1)} %bitcast.8, f32[14,128,128]{2,1,0:T(8,128)S(1)} %get-tuple-element.82.refs_1_, f32[4,128,128]{2,1,0:T(8,128)S(1)} %get-tuple-element.87.refs_2_, f32[16,128,128]{2,1,0:T(8,128)S(1)} %get-tuple-element.55.refs_2__0_.refs_1__0_.refs_3__0_, ...), custom_call_target="tpu_custom_call" | custom-call | flops 400000000 | bytes 12000000 | tf_op jit(solution)/shard_map/direction/pallas_call | solution.py:531
  62.4 12.9 %all_to_all.11.refs_2_ = f32[32,2,128]{2,1,0:T(2,128)S(1)} all-to-all(f32[32,2,128]{2,1,0:T(2,128)S(1)} %get-tuple-element.90), channel_id=1, replica_groups=mesh['tm'=4,'tile'=8] {'tile','tm'}, dimensions={0} | all-to-all | bytes 65536 | tf_op jit(solution)/shard_map/all_to_all | solution.py:676
  75.3 1.3 %final.1 = f32[2048,128]{1,0:T(8,128)} custom-call(f32[16,128,128]{2,1,0:T(8,128)S(1)} %get-tuple-element.75.refs_8__0_.refs_9__0_.refs_7__0_.refs_0_, f32[18,128,128]{2,1,0:T(8,128)S(1)} %get-tuple-element.89.refs_1_, f32[32,2,128]{2,1,0:T(2,128)S(1)} %all_to_all.11.refs_2_), custom_call_target="tpu_custom_call" | custom-call | flops 140000000 | bytes 4200000 | tf_op jit(solution)/shard_map/final/pallas_call | solution.py:531
Async XLA Ops:
  0.6 0.7 copy-start.4
  2.2 7.0 %collective-permute-start = (f32[136,128]{1,0:T(8,128)S(1)}, f32[136,128]{1,0:T(8,128)S(1)}, u32[]{:S(2)}, u32[]{:S(2)}) collective-permute-start(f32[136,128]{1,0:T(8,128)S(1)} %get-tuple-element.49), channel_id=1, source_target_pairs={{0,1},{2,3},{4,5},{6,7},{1,0},{3,2},{5,4},{7,6},{8,9},{10,11},{12,... | collective-permute-start | bytes 208904 | tf_op jit(solution)/shard_map/ppermute | solution.py:555
  5.3 4.0 %collective-permute-start.1 = (f32[136,128]{1,0:T(8,128)S(1)}, f32[136,128]{1,0:T(8,128)S(1)}, u32[]{:S(2)}, u32[]{:S(2)}) collective-permute-start(f32[136,128]{1,0:T(8,128)S(1)} %get-tuple-element.50), channel_id=1, source_target_pairs={{1,2},{3,4},{5,6},{2,1},{4,3},{6,5},{9,10},{11,12},{13,14},{10,9},... | collective-permute-start | bytes 208904 | tf_op jit(solution)/shard_map/ppermute | solution.py:555
  5.9 1.2 %copy-start.2 = (f32[2048,128]{1,0:T(8,128)S(1)}, f32[2048,128]{1,0:T(8,128)}, u32[]{:S(2)}) copy-start(f32[2048,128]{1,0:T(8,128)} %refs_0_.3) | copy-start | bytes 3145732
  7.2 0.7 copy-start.5
  7.8 6.6 %copy-start.1 = (bf16[8192,128]{1,0:T(8,128)(2,1)S(1)}, bf16[8192,128]{1,0:T(8,128)(2,1)}, u32[]{:S(2)}) copy-start(bf16[8192,128]{1,0:T(8,128)(2,1)} %refs_7_.7) | copy-start | bytes 6291460
  7.8 6.6 %copy-start.3 = (s32[32,4]{0,1:T(4,128)S(1)}, s32[32,4]{0,1:T(4,128)}, u32[]{:S(2)}) copy-start(s32[32,4]{0,1:T(4,128)} %param.8) | copy-start | bytes 1540
  9.6 3.5 %collective-permute-start.4 = (f32[2,24,128]{2,1,0:T(8,128)S(1)}, f32[2,24,128]{2,1,0:T(8,128)S(1)}, u32[]{:S(2)}, u32[]{:S(2)}) collective-permute-start(f32[2,24,128]{2,1,0:T(8,128)S(1)} %get-tuple-element.62.refs_4__0_.refs_5__0_.refs_6__0_), channel_id=1, source_target_pairs={{0,24},{8,16},{16,8},{24,0},{1,25},{9,17},{17,9},{25,1},{2,26},{10... | collective-permute-start | bytes 73736 | tf_op jit(solution)/shard_map/ppermute | solution.py:561
  10.3 4.1 %collective-permute-start.3 = (f32[2,24,128]{2,1,0:T(8,128)S(1)}, f32[2,24,128]{2,1,0:T(8,128)S(1)}, u32[]{:S(2)}, u32[]{:S(2)}) collective-permute-start(f32[2,24,128]{2,1,0:T(8,128)S(1)} %get-tuple-element.62.refs_4__0_.refs_5__0_.refs_6__0_), channel_id=1, source_target_pairs={{0,16},{8,24},{16,0},{24,8},{1,17},{9,25},{17,1},{25,9},{2,18},{10... | collective-permute-start | bytes 73736 | tf_op jit(solution)/shard_map/ppermute | solution.py:561
  11.2 3.2 %collective-permute-start.2 = (f32[2,24,128]{2,1,0:T(8,128)S(1)}, f32[2,24,128]{2,1,0:T(8,128)S(1)}, u32[]{:S(2)}, u32[]{:S(2)}) collective-permute-start(f32[2,24,128]{2,1,0:T(8,128)S(1)} %get-tuple-element.62.refs_4__0_.refs_5__0_.refs_6__0_), channel_id=1, source_target_pairs={{0,8},{8,0},{16,24},{24,16},{1,9},{9,1},{17,25},{25,17},{2,10},{10... | collective-permute-start | bytes 73736 | tf_op jit(solution)/shard_map/ppermute | solution.py:561
  14.4 6.2 %copy-start = (bf16[8192,256]{1,0:T(8,128)(2,1)S(1)}, bf16[8192,256]{1,0:T(8,128)(2,1)}, u32[]{:S(2)}) copy-start(bf16[8192,256]{1,0:T(8,128)(2,1)} %refs_8_.3) | copy-start | bytes 12582916
  16.1 7.8 %collective-permute-start.5 = (bf16[3,128,128]{2,1,0:T(8,128)(2,1)S(1)}, bf16[3,128,128]{2,1,0:T(8,128)(2,1)S(1)}, u32[]{:S(2)}, u32[]{:S(2)}) collective-permute-start(bf16[3,128,128]{2,1,0:T(8,128)(2,1)S(1)} %get-tuple-element.68), channel_id=1, source_target_pairs={{0,1},{2,3},{4,5},{6,7},{1,0},{3,2},{5,4},{7,6},{8,9},{10,11},{12,... | collective-permute-start | bytes 294920 | tf_op jit(solution)/shard_map/ppermute | solution.py:555
  19.9 4.0 %collective-permute-start.6 = (bf16[3,128,128]{2,1,0:T(8,128)(2,1)S(1)}, bf16[3,128,128]{2,1,0:T(8,128)(2,1)S(1)}, u32[]{:S(2)}, u32[]{:S(2)}) collective-permute-start(bf16[3,128,128]{2,1,0:T(8,128)(2,1)S(1)} %get-tuple-element.69), channel_id=1, source_target_pairs={{1,2},{3,4},{5,6},{2,1},{4,3},{6,5},{9,10},{11,12},{13,14},{10,9},... | collective-permute-start | bytes 294920 | tf_op jit(solution)/shard_map/ppermute | solution.py:555
  24.2 3.6 %collective-permute-start.9 = (f32[2,24,128]{2,1,0:T(8,128)S(1)}, f32[2,24,128]{2,1,0:T(8,128)S(1)}, u32[]{:S(2)}, u32[]{:S(2)}) collective-permute-start(f32[2,24,128]{2,1,0:T(8,128)S(1)} %get-tuple-element.72.refs_7__0_), channel_id=1, source_target_pairs={{0,24},{8,16},{16,8},{24,0},{1,25},{9,17},{17,9},{25,1},{2,26},{10... | collective-permute-start | bytes 73736 | tf_op jit(solution)/shard_map/ppermute | solution.py:561
  24.3 3.9 %collective-permute-start.8 = (f32[2,24,128]{2,1,0:T(8,128)S(1)}, f32[2,24,128]{2,1,0:T(8,128)S(1)}, u32[]{:S(2)}, u32[]{:S(2)}) collective-permute-start(f32[2,24,128]{2,1,0:T(8,128)S(1)} %get-tuple-element.72.refs_7__0_), channel_id=1, source_target_pairs={{0,16},{8,24},{16,0},{24,8},{1,17},{9,25},{17,1},{25,9},{2,18},{10... | collective-permute-start | bytes 73736 | tf_op jit(solution)/shard_map/ppermute | solution.py:561
  25.7 2.4 %collective-permute-start.7 = (f32[2,24,128]{2,1,0:T(8,128)S(1)}, f32[2,24,128]{2,1,0:T(8,128)S(1)}, u32[]{:S(2)}, u32[]{:S(2)}) collective-permute-start(f32[2,24,128]{2,1,0:T(8,128)S(1)} %get-tuple-element.72.refs_7__0_), channel_id=1, source_target_pairs={{0,8},{8,0},{16,24},{24,16},{1,9},{9,1},{17,25},{25,17},{2,10},{10... | collective-permute-start | bytes 73736 | tf_op jit(solution)/shard_map/ppermute | solution.py:561
  45.4 3.2 %collective-permute-start.12 = (f32[1,24,128]{2,1,0:T(8,128)S(1)}, f32[1,24,128]{2,1,0:T(8,128)S(1)}, u32[]{:S(2)}, u32[]{:S(2)}) collective-permute-start(f32[1,24,128]{2,1,0:T(8,128)S(1)} %get-tuple-element.78.refs_5__0_), channel_id=1, source_target_pairs={{0,24},{8,16},{16,8},{24,0},{1,25},{9,17},{17,9},{25,1},{2,26},{10... | collective-permute-start | bytes 36872 | tf_op jit(solution)/shard_map/ppermute | solution.py:561
  45.6 3.7 %collective-permute-start.11 = (f32[1,24,128]{2,1,0:T(8,128)S(1)}, f32[1,24,128]{2,1,0:T(8,128)S(1)}, u32[]{:S(2)}, u32[]{:S(2)}) collective-permute-start(f32[1,24,128]{2,1,0:T(8,128)S(1)} %get-tuple-element.78.refs_5__0_), channel_id=1, source_target_pairs={{0,16},{8,24},{16,0},{24,8},{1,17},{9,25},{17,1},{25,9},{2,18},{10... | collective-permute-start | bytes 36872 | tf_op jit(solution)/shard_map/ppermute | solution.py:561
  47.2 2.2 %collective-permute-start.10 = (f32[1,24,128]{2,1,0:T(8,128)S(1)}, f32[1,24,128]{2,1,0:T(8,128)S(1)}, u32[]{:S(2)}, u32[]{:S(2)}) collective-permute-start(f32[1,24,128]{2,1,0:T(8,128)S(1)} %get-tuple-element.78.refs_5__0_), channel_id=1, source_target_pairs={{0,8},{8,0},{16,24},{24,16},{1,9},{9,1},{17,25},{25,17},{2,10},{10... | collective-permute-start | bytes 36872 | tf_op jit(solution)/shard_map/ppermute | solution.py:561
  51.0 4.9 %collective-permute-start.13 = (bf16[3,128,128]{2,1,0:T(8,128)(2,1)S(1)}, bf16[3,128,128]{2,1,0:T(8,128)(2,1)S(1)}, u32[]{:S(2)}, u32[]{:S(2)}) collective-permute-start(bf16[3,128,128]{2,1,0:T(8,128)(2,1)S(1)} %get-tuple-element.84), channel_id=1, source_target_pairs={{0,1},{2,3},{4,5},{6,7},{1,0},{3,2},{5,4},{7,6},{8,9},{10,11},{12,... | collective-permute-start | bytes 294920 | tf_op jit(solution)/shard_map/ppermute | solution.py:555
  51.7 4.2 %collective-permute-start.14 = (bf16[3,128,128]{2,1,0:T(8,128)(2,1)S(1)}, bf16[3,128,128]{2,1,0:T(8,128)(2,1)S(1)}, u32[]{:S(2)}, u32[]{:S(2)}) collective-permute-start(bf16[3,128,128]{2,1,0:T(8,128)(2,1)S(1)} %get-tuple-element.85), channel_id=1, source_target_pairs={{1,2},{3,4},{5,6},{2,1},{4,3},{6,5},{9,10},{11,12},{13,14},{10,9},... | collective-permute-start | bytes 294920 | tf_op jit(solution)/shard_map/ppermute | solution.py:555
  56.3 3.6 %collective-permute-start.17 = (f32[2,24,128]{2,1,0:T(8,128)S(1)}, f32[2,24,128]{2,1,0:T(8,128)S(1)}, u32[]{:S(2)}, u32[]{:S(2)}) collective-permute-start(f32[2,24,128]{2,1,0:T(8,128)S(1)} %get-tuple-element.88.refs_7__0_), channel_id=1, source_target_pairs={{0,24},{8,16},{16,8},{24,0},{1,25},{9,17},{17,9},{25,1},{2,26},{10... | collective-permute-start | bytes 73736 | tf_op jit(solution)/shard_map/ppermute | solution.py:561
  56.4 3.9 %collective-permute-start.16 = (f32[2,24,128]{2,1,0:T(8,128)S(1)}, f32[2,24,128]{2,1,0:T(8,128)S(1)}, u32[]{:S(2)}, u32[]{:S(2)}) collective-permute-start(f32[2,24,128]{2,1,0:T(8,128)S(1)} %get-tuple-element.88.refs_7__0_), channel_id=1, source_target_pairs={{0,16},{8,24},{16,0},{24,8},{1,17},{9,25},{17,1},{25,9},{2,18},{10... | collective-permute-start | bytes 73736 | tf_op jit(solution)/shard_map/ppermute | solution.py:561
  57.9 2.4 %collective-permute-start.15 = (f32[2,24,128]{2,1,0:T(8,128)S(1)}, f32[2,24,128]{2,1,0:T(8,128)S(1)}, u32[]{:S(2)}, u32[]{:S(2)}) collective-permute-start(f32[2,24,128]{2,1,0:T(8,128)S(1)} %get-tuple-element.88.refs_7__0_), channel_id=1, source_target_pairs={{0,8},{8,0},{16,24},{24,16},{1,9},{9,1},{17,25},{25,17},{2,10},{10... | collective-permute-start | bytes 73736 | tf_op jit(solution)/shard_map/ppermute | solution.py:561
